TPU v7x, 32 devices: a whole 2x2x4 slice. The times are simulated.
32 devices in a mesh: rep: 4 (over x, core), shard: 8 (over z, y).
Axes of the slice: x: 2, y: 2, z: 4, core: 2. Of those that a mesh axis runs over, the one named last changes fastest.
Arguments:
- tokens: bfloat16 [4096, 2304], P(('rep', 'shard')), may hold values from -6 to 6
- cotangent: bfloat16 [4096, 2304], P(('rep', 'shard')), may hold values from -6 to 6
- piece_starts: int32 [4, 2], replicated, may hold values from 0 to 768, as said below
- inproj: float32 [2304, 4096], P(('rep', 'shard'))
- outproj: float32 [2048, 2304], P(('rep', 'shard'))
- ffn_gate: float32 [2304, 9216], P(('rep', 'shard'))
- ffn_up: float32 [2304, 9216], P(('rep', 'shard'))
- ffn_down: float32 [9216, 2304], P(('rep', 'shard'))
- norm_gains: float32 [2304, 4], P(('rep', 'shard'))
- mean_inproj: float32 [2304, 4096], P(('rep', 'shard'))
- mean_outproj: float32 [2048, 2304], P(('rep', 'shard'))
- mean_gate: float32 [2304, 9216], P(('rep', 'shard'))
- mean_up: float32 [2304, 9216], P(('rep', 'shard'))
- mean_down: float32 [9216, 2304], P(('rep', 'shard'))
- mean_gains: float32 [2304, 4], P(('rep', 'shard'))
- square_inproj: float32 [2304, 4096], P(('rep', 'shard')), may hold values from 409.6 to 1638.4
- square_outproj: float32 [2048, 2304], P(('rep', 'shard')), may hold values from 409.6 to 1638.4
- square_gate: float32 [2304, 9216], P(('rep', 'shard')), may hold values from 409.6 to 1638.4
- square_up: float32 [2304, 9216], P(('rep', 'shard')), may hold values from 409.6 to 1638.4
- square_down: float32 [9216, 2304], P(('rep', 'shard')), may hold values from 409.6 to 1638.4
- square_gains: float32 [2304, 4], P(('rep', 'shard')), may hold values from 409.6 to 1638.4
Outputs:
- layer_out: bfloat16 [4096, 2304], P(('rep', 'shard'))
- input_grad: float32 [4096, 2304], P(('rep', 'shard'))
- grad_inproj: float32 [2304, 4096], P(('rep', 'shard'))
- grad_outproj: float32 [2048, 2304], P(('rep', 'shard'))
- grad_gate: float32 [2304, 9216], P(('rep', 'shard'))
- grad_up: float32 [2304, 9216], P(('rep', 'shard'))
- grad_down: float32 [9216, 2304], P(('rep', 'shard'))
- grad_gains: float32 [2304, 4], P(('rep', 'shard'))
- newmean_inproj: float32 [2304, 4096], P(('rep', 'shard'))
- newmean_outproj: float32 [2048, 2304], P(('rep', 'shard'))
- newmean_gate: float32 [2304, 9216], P(('rep', 'shard'))
- newmean_up: float32 [2304, 9216], P(('rep', 'shard'))
- newmean_down: float32 [9216, 2304], P(('rep', 'shard'))
- newmean_gains: float32 [2304, 4], P(('rep', 'shard'))
- newsquare_inproj: float32 [2304, 4096], P(('rep', 'shard'))
- newsquare_outproj: float32 [2048, 2304], P(('rep', 'shard'))
- newsquare_gate: float32 [2304, 9216], P(('rep', 'shard'))
- newsquare_up: float32 [2304, 9216], P(('rep', 'shard'))
- newsquare_down: float32 [9216, 2304], P(('rep', 'shard'))
- newsquare_gains: float32 [2304, 4], P(('rep', 'shard'))
- new_inproj: float32 [2304, 4096], P(('rep', 'shard'))
- new_outproj: float32 [2048, 2304], P(('rep', 'shard'))
- new_gate: float32 [2304, 9216], P(('rep', 'shard'))
- new_up: float32 [2304, 9216], P(('rep', 'shard'))
- new_down: float32 [9216, 2304], P(('rep', 'shard'))
- new_gains: float32 [2304, 4], P(('rep', 'shard'))
- norm_table: float32 [2, 6], replicated
Inputs may be any that keep to these rules, and one draw needn't show every extreme that they name: `piece_starts`: each sequence's 2 picture pieces of 256 positions start in increasing order, lie inside the sequence and do not intersect.
All inputs are finite; a program needn't handle non-finite values.
Results may differ from a plain program's by a relative error of at most 0.019.
Values may be sent and summed in bfloat16 or wider, within the bound.
A program may use at most 512 MiB of HBM per device.

v0:
```python
import jax
import jax.numpy as jnp
from jax import lax
from jax.sharding import PartitionSpec as P

HEADS = 8
KV_HEADS = 4
HEAD_DIM = 256
PIC = 256


def rms_norm(values_in, gain_col):
    return (
        values_in
        * lax.rsqrt(jnp.mean(values_in * values_in, axis=-1, keepdims=True) + 1e-06)
        * (1.0 + gain_col)
    )


def geglu(gate_lin, up_lin):
    return jax.nn.gelu(gate_lin, approximate=True) * up_lin


def rotate(flat, position, head_count, sign):
    row_count = flat.shape[0]
    width = flat.shape[1] // head_count
    half = width // 2
    vectors = flat.reshape(row_count, head_count, width)
    freq = 10000.0 ** (-(jnp.arange(half, dtype=jnp.float32) * 2.0 / width))
    angle = position.astype(jnp.float32)[:, None] * freq[None, :]
    cosine = jnp.cos(angle)[:, None, :]
    sine = sign * jnp.sin(angle)[:, None, :]
    first = vectors[..., :half]
    second = vectors[..., half:]
    turned = jnp.concatenate(
        [first * cosine - second * sine, second * cosine + first * sine], axis=-1
    )
    return turned.reshape(row_count, head_count * width)


def owned_rows(activation, gradient, rep_index, width):
    piece = lax.dynamic_slice_in_dim(activation, rep_index * width, width, 1)
    return lax.dot_general(
        piece, gradient, (((0,), (0,)), ((), ())), preferred_element_type=jnp.float32
    )


def back_dot(gradient, weight):
    return lax.dot_general(
        gradient, weight, (((1,), (1,)), ((), ())), preferred_element_type=jnp.float32
    )


def describe(rows, piece_starts, seq_offset, seq_len):
    local_seq = rows // seq_len
    position = rows % seq_len
    global_seq = local_seq + seq_offset
    seq_total = piece_starts.shape[0]
    piece_count = piece_starts.shape[1]
    select = (global_seq[:, None] == jnp.arange(seq_total, dtype=jnp.int32)[None, :]).astype(
        jnp.int32
    )
    starts = jnp.sum(select[:, :, None] * piece_starts[None, :, :], axis=1)
    inside = ((position[:, None] >= starts) & (position[:, None] < starts + PIC)).astype(jnp.int32)
    labels = (
        global_seq[:, None] * piece_count + jnp.arange(piece_count, dtype=jnp.int32)[None, :] + 1
    )
    return (local_seq, position, jnp.sum(inside * labels, axis=1))


def visibility(piece_starts, query_rows, key_rows, seq_offset, seq_len):
    seq_q, pos_q, tag_q = describe(query_rows, piece_starts, seq_offset, seq_len)
    seq_k, pos_k, tag_k = describe(key_rows, piece_starts, seq_offset, seq_len)
    causal = pos_k[None, :] <= pos_q[:, None]
    same_piece = (tag_q[:, None] == tag_k[None, :]) & (tag_q[:, None] > 0)
    return (seq_q[:, None] == seq_k[None, :]) & (causal | same_piece)


def lamb_local(master, gradient, first, second):
    newmean = 0.5 * first + 0.5 * gradient
    newsquare = 0.5 * second + 0.5 * gradient * gradient
    step_dir = newmean / (jnp.sqrt(newsquare) + 1e-06) + 0.01 * master
    return (newmean, newsquare, step_dir)


def per_device(
    tokens,
    cotangent,
    piece_starts,
    inproj,
    outproj,
    ffn_gate,
    ffn_up,
    ffn_down,
    norm_gains,
    mean_inproj,
    mean_outproj,
    mean_gate,
    mean_up,
    mean_down,
    mean_gains,
    square_inproj,
    square_outproj,
    square_gate,
    square_up,
    square_down,
    square_gains,
):
    bf16 = jnp.bfloat16
    f32 = jnp.float32
    rep_count = lax.axis_size("rep")
    shard_count = lax.axis_size("shard")
    rep_index = lax.axis_index("rep")
    w_in, w_out, w_gate, w_up, w_down, gain_copy = (
        lax.all_gather(inproj.astype(bf16), ("rep", "shard"), axis=0, tiled=True),
        lax.all_gather(outproj.astype(bf16), ("rep", "shard"), axis=0, tiled=True),
        lax.all_gather(ffn_gate.astype(bf16), ("rep", "shard"), axis=0, tiled=True),
        lax.all_gather(ffn_up.astype(bf16), ("rep", "shard"), axis=0, tiled=True),
        lax.all_gather(ffn_down.astype(bf16), ("rep", "shard"), axis=0, tiled=True),
        lax.all_gather(norm_gains.astype(bf16), ("rep", "shard"), axis=0, tiled=True),
    )
    gains_used = gain_copy.astype(f32)
    residual = tokens.astype(f32)
    row_count = residual.shape[0]
    seq_len = row_count * shard_count
    q_width = HEADS * HEAD_DIM
    k_width = KV_HEADS * HEAD_DIM
    group_size = HEADS // KV_HEADS
    query_scale = HEAD_DIM ** (-0.5)
    local_rows = lax.axis_index("shard") * row_count + jnp.arange(row_count, dtype=jnp.int32)
    position = local_rows % seq_len
    normed_in = rms_norm(residual, gains_used[:, 0]).astype(bf16)
    projected = jnp.dot(normed_in, w_in, preferred_element_type=f32)
    queries = (rotate(projected[:, :q_width], position, HEADS, 1.0) * query_scale).astype(bf16)
    keys = rotate(projected[:, q_width : q_width + k_width], position, KV_HEADS, 1.0).astype(bf16)
    values = projected[:, q_width + k_width :].astype(bf16)
    all_keys, all_values = (
        lax.all_gather(keys, "shard", axis=0, tiled=True),
        lax.all_gather(values, "shard", axis=0, tiled=True),
    )
    key_rows = all_keys.shape[0]
    visible = visibility(
        piece_starts,
        local_rows,
        jnp.arange(key_rows, dtype=jnp.int32),
        rep_index * (key_rows // seq_len),
        seq_len,
    )
    query_heads = queries.reshape(row_count, KV_HEADS, group_size, HEAD_DIM)
    key_heads = all_keys.reshape(key_rows, KV_HEADS, HEAD_DIM)
    value_heads = all_values.reshape(key_rows, KV_HEADS, HEAD_DIM)

    def capped_scores():
        raw_scores = jnp.einsum(
            "tgrd,kgd->grtk", query_heads, key_heads, preferred_element_type=f32
        )
        bent_scores = jnp.tanh(raw_scores / 50.0)
        return (bent_scores, jnp.where(visible, 50.0 * bent_scores, -1e30))

    bent_scores, masked = capped_scores()
    top_score = jnp.max(masked, axis=-1, keepdims=True)
    log_total = top_score + jnp.log(jnp.sum(jnp.exp(masked - top_score), axis=-1, keepdims=True))
    probs_low = jnp.exp(masked - log_total).astype(bf16)
    attended = (
        jnp.einsum("grtk,kgd->tgrd", probs_low, value_heads, preferred_element_type=f32)
        .reshape(row_count, q_width)
        .astype(bf16)
    )
    attn_proj = jnp.dot(attended, w_out, preferred_element_type=f32)
    middle = residual + rms_norm(attn_proj, gains_used[:, 1])
    normed_mid = rms_norm(middle, gains_used[:, 2]).astype(bf16)
    gate_lin = jnp.dot(normed_mid, w_gate, preferred_element_type=f32)
    up_lin = jnp.dot(normed_mid, w_up, preferred_element_type=f32)
    hidden = geglu(gate_lin, up_lin).astype(bf16)
    ffn_proj = jnp.dot(hidden, w_down, preferred_element_type=f32)
    layer_out = (middle + rms_norm(ffn_proj, gains_used[:, 3])).astype(bf16)
    d_out = cotangent.astype(f32)
    _, post_back = jax.vjp(rms_norm, ffn_proj, gains_used[:, 3])
    d_ffn, d_gain3 = post_back(d_out)
    d_ffn_low = d_ffn.astype(bf16)
    hidden_all, d_ffn_all = (
        lax.all_gather(hidden, "rep", axis=0, tiled=True),
        lax.all_gather(d_ffn_low, "rep", axis=0, tiled=True),
    )
    part_down = owned_rows(hidden_all, d_ffn_all, rep_index, hidden.shape[1] // rep_count)
    d_hidden = back_dot(d_ffn_low, w_down)
    _, glu_back = jax.vjp(geglu, gate_lin, up_lin)
    d_gate, d_up = glu_back(d_hidden)
    d_gate_low = d_gate.astype(bf16)
    d_up_low = d_up.astype(bf16)
    gate_up_grad = jnp.concatenate([d_gate_low, d_up_low], axis=1)
    mid_all, gate_up_all = (
        lax.all_gather(normed_mid, "rep", axis=0, tiled=True),
        lax.all_gather(gate_up_grad, "rep", axis=0, tiled=True),
    )
    part_gate_up = owned_rows(mid_all, gate_up_all, rep_index, normed_mid.shape[1] // rep_count)
    d_mid_in = back_dot(d_gate_low, w_gate) + back_dot(d_up_low, w_up)
    _, pre_back = jax.vjp(rms_norm, middle, gains_used[:, 2])
    d_mid_part, d_gain2 = pre_back(d_mid_in)
    d_middle = d_out + d_mid_part
    _, attn_back = jax.vjp(rms_norm, attn_proj, gains_used[:, 1])
    d_attn, d_gain1 = attn_back(d_middle)
    d_attn_low = d_attn.astype(bf16)
    d_attended = back_dot(d_attn_low, w_out).astype(bf16)
    d_heads = d_attended.reshape(row_count, KV_HEADS, group_size, HEAD_DIM)
    bent_again, masked_again = capped_scores()
    attn_probs = jnp.exp(masked_again - log_total)
    probs_again = attn_probs.astype(bf16)
    d_probs = jnp.einsum("tgrd,kgd->grtk", d_heads, value_heads, preferred_element_type=f32)
    d_scores = (
        attn_probs
        * (d_probs - jnp.sum(attn_probs * d_probs, axis=-1, keepdims=True))
        * (1.0 - bent_again * bent_again)
    ).astype(bf16)
    d_queries = jnp.einsum(
        "grtk,kgd->tgrd", d_scores, key_heads, preferred_element_type=f32
    ).reshape(row_count, q_width)
    d_key = jnp.einsum("grtk,tgrd->kgd", d_scores, query_heads, preferred_element_type=f32).reshape(
        row_count * lax.axis_size("shard"), k_width
    )
    d_value = jnp.einsum(
        "grtk,tgrd->kgd", probs_again, d_heads, preferred_element_type=f32
    ).reshape(row_count * lax.axis_size("shard"), k_width)
    d_key_value = lax.psum_scatter(
        jnp.concatenate([d_key, d_value], axis=1), "shard", scatter_dimension=0, tiled=True
    )
    d_projected = jnp.concatenate(
        [
            rotate(d_queries, position, HEADS, -1.0) * query_scale,
            rotate(d_key_value[:, :k_width], position, KV_HEADS, -1.0),
            d_key_value[:, k_width:],
        ],
        axis=1,
    ).astype(bf16)
    d_normed_in = back_dot(d_projected, w_in)
    _, first_back = jax.vjp(rms_norm, residual, gains_used[:, 0])
    d_input_part, d_gain0 = first_back(d_normed_in)
    input_grad = d_middle + d_input_part
    gain_grad = jnp.stack([d_gain0, d_gain1, d_gain2, d_gain3], axis=1)
    attended_all, d_attn_all, normed_all, d_proj_all = (
        lax.all_gather(attended, "rep", axis=0, tiled=True),
        lax.all_gather(d_attn_low, "rep", axis=0, tiled=True),
        lax.all_gather(normed_in, "rep", axis=0, tiled=True),
        lax.all_gather(d_projected, "rep", axis=0, tiled=True),
    )
    part_out = owned_rows(attended_all, d_attn_all, rep_index, attended.shape[1] // rep_count)
    part_in = owned_rows(normed_all, d_proj_all, rep_index, normed_in.shape[1] // rep_count)
    part_gain = lax.psum_scatter(gain_grad, "rep", scatter_dimension=0, tiled=True)
    owned = (
        lax.psum_scatter(part_in, "shard", scatter_dimension=0, tiled=True),
        lax.psum_scatter(part_gain, "shard", scatter_dimension=0, tiled=True),
        lax.psum_scatter(part_out, "shard", scatter_dimension=0, tiled=True),
        lax.psum_scatter(part_gate_up, "shard", scatter_dimension=0, tiled=True),
        lax.psum_scatter(part_down, "shard", scatter_dimension=0, tiled=True),
    )
    grad_inproj, grad_gains, grad_outproj, grad_gate_up, grad_down = owned
    split_at = grad_gate_up.shape[1] // 2
    grad_gate = grad_gate_up[:, :split_at]
    grad_up = grad_gate_up[:, split_at:]
    masters = (inproj, outproj, ffn_gate, ffn_up, ffn_down, norm_gains)
    gradients = (grad_inproj, grad_outproj, grad_gate, grad_up, grad_down, grad_gains)
    firsts = (mean_inproj, mean_outproj, mean_gate, mean_up, mean_down, mean_gains)
    seconds = (square_inproj, square_outproj, square_gate, square_up, square_down, square_gains)
    results = [
        lamb_local(masters[index], gradients[index], firsts[index], seconds[index])
        for index in range(6)
    ]
    weight_sums = jnp.stack([jnp.sum(master * master) for master in masters])
    step_sums = jnp.stack([jnp.sum(item[2] * item[2]) for item in results])
    totals = lax.psum(jnp.stack([weight_sums, step_sums]), ("rep", "shard"))
    counts = jnp.array([float(master.size * rep_count * shard_count) for master in masters], f32)
    norm_table = jnp.sqrt(totals / counts[None, :] + 1e-06)
    fresh = [
        masters[index] - 0.3 * norm_table[0, index] / norm_table[1, index] * results[index][2]
        for index in range(6)
    ]
    return (
        layer_out,
        input_grad,
        grad_inproj,
        grad_outproj,
        grad_gate,
        grad_up,
        grad_down,
        grad_gains,
        results[0][0],
        results[1][0],
        results[2][0],
        results[3][0],
        results[4][0],
        results[5][0],
        results[0][1],
        results[1][1],
        results[2][1],
        results[3][1],
        results[4][1],
        results[5][1],
        fresh[0],
        fresh[1],
        fresh[2],
        fresh[3],
        fresh[4],
        fresh[5],
        norm_table,
    )


def solution(mesh):
    return jax.shard_map(
        per_device,
        mesh=mesh,
        in_specs=(
            P(("rep", "shard"), None),
            P(("rep", "shard"), None),
            P(),
            P(("rep", "shard"), None),
            P(("rep", "shard"), None),
            P(("rep", "shard"), None),
            P(("rep", "shard"), None),
            P(("rep", "shard"), None),
            P(("rep", "shard"), None),
            P(("rep", "shard"), None),
            P(("rep", "shard"), None),
            P(("rep", "shard"), None),
            P(("rep", "shard"), None),
            P(("rep", "shard"), None),
            P(("rep", "shard"), None),
            P(("rep", "shard"), None),
            P(("rep", "shard"), None),
            P(("rep", "shard"), None),
            P(("rep", "shard"), None),
            P(("rep", "shard"), None),
            P(("rep", "shard"), None),
        ),
        out_specs=(
            P(("rep", "shard"), None),
            P(("rep", "shard"), None),
            P(("rep", "shard"), None),
            P(("rep", "shard"), None),
            P(("rep", "shard"), None),
            P(("rep", "shard"), None),
            P(("rep", "shard"), None),
            P(("rep", "shard"), None),
            P(("rep", "shard"), None),
            P(("rep", "shard"), None),
            P(("rep", "shard"), None),
            P(("rep", "shard"), None),
            P(("rep", "shard"), None),
            P(("rep", "shard"), None),
            P(("rep", "shard"), None),
            P(("rep", "shard"), None),
            P(("rep", "shard"), None),
            P(("rep", "shard"), None),
            P(("rep", "shard"), None),
            P(("rep", "shard"), None),
            P(("rep", "shard"), None),
            P(("rep", "shard"), None),
            P(("rep", "shard"), None),
            P(("rep", "shard"), None),
            P(("rep", "shard"), None),
            P(("rep", "shard"), None),
            P(),
        ),
        check_vma=False,
    )
```

profile of v0, /device:TPU:0, one launch (start us, length us, event | category | flops | bytes accessed | tf_op | source)
XLA Modules:
  0.0 3678.9 jit_solution(5824742477921021234)
XLA Ops:
  7.3 2.2 convert_element_type.113
  10.9 70.1 %all-gather = bf16[32,72,4]{1,2,0:T(4,128)(2,1)S(1)} all-gather(bf16[1,72,4]{1,2,0:T(4,128)(2,1)S(1)} %get-tuple-element.93), channel_id=1, replica_groups=mesh['rep'=4,'shard'=8] {'rep','shard'}, dimensions={0}, use_global_device_ids=true | all-gather | bytes 19008 | tf_op jit(solution)/shard_map/all_gather | solution.py:120
  82.3 56.7 %all-gather.17.cloned.1.call-done = bf16[2304,4096]{1,0:T(8,128)(2,1)} async-done(((bf16[72,4096]{1,0:T(8,128)(2,1)}), bf16[2304,4096]{1,0:T(8,128)(2,1)}) %all-gather.17.cloned.1.call-update) | async-done | bytes 18874384 | tf_op jit(solution)/shard_map/all_gather | solution.py:115
  139.0 7.8 fusion.121
  150.0 2.0 slice.132
  152.0 2.1 reshape.451
  161.2 3.1 convert_element_type.127
  167.7 28.9 all-gather.19.cloned.1.call-done
  196.5 3.3 reshape.450
  199.9 48.9 %all-gather.21.cloned.1.call-done = bf16[1024,1024]{0,1:T(8,128)(2,1)} async-done(((bf16[128,1024]{0,1:T(8,128)(2,1)}), bf16[1024,1024]{0,1:T(8,128)(2,1)}) %all-gather.21.cloned.1.call-update) | async-done | bytes 2097168 | tf_op jit(solution)/shard_map/all_gather | solution.py:138
  248.8 2.9 fusion.16
  255.5 76.9 %all-gather.23.cloned.1.call-done = bf16[2048,2304]{1,0:T(8,128)(2,1)} async-done(((bf16[64,2304]{1,0:T(8,128)(2,1)}), bf16[2048,2304]{1,0:T(8,128)(2,1)}) %all-gather.23.cloned.1.call-update) | async-done | bytes 9437200 | tf_op jit(solution)/shard_map/all_gather | solution.py:116
  332.3 5.2 multiply_reduce_fusion.14
  339.2 232.9 %all-gather.25.cloned.1.call-done = bf16[2304,9216]{1,0:T(8,128)(2,1)} async-done(((bf16[72,9216]{1,0:T(8,128)(2,1)}), bf16[2304,9216]{1,0:T(8,128)(2,1)}) %all-gather.25.cloned.1.call-update) | async-done | bytes 42467344 | tf_op jit(solution)/shard_map/all_gather | solution.py:117
  572.0 19.4 fusion.122
  591.5 219.8 %all-gather.27.cloned.1.call-done = bf16[2304,9216]{1,0:T(8,128)(2,1)} async-done(((bf16[72,9216]{1,0:T(8,128)(2,1)}), bf16[2304,9216]{1,0:T(8,128)(2,1)}) %all-gather.27.cloned.1.call-update) | async-done | bytes 42467344 | tf_op jit(solution)/shard_map/all_gather | solution.py:118
  811.3 21.7 multiply_convert_fusion.1
  833.1 217.7 %all-gather.29.cloned.1.call-done = bf16[9216,2304]{1,0:T(8,128)(2,1)} async-done(((bf16[288,2304]{1,0:T(8,128)(2,1)}), bf16[9216,2304]{1,0:T(8,128)(2,1)}) %all-gather.29.cloned.1.call-update) | async-done | bytes 42467344 | tf_op jit(solution)/shard_map/all_gather | solution.py:119
  1050.8 15.5 multiply_reduce_fusion.12
  1066.3 2.1 fusion.51
  1068.4 2.9 fusion.52
  1071.4 22.4 multiply_convert_fusion
  1093.7 21.5 fusion.123
  1115.3 21.7 multiply_reduce_fusion.8
  1137.1 2.5 multiply_reduce_fusion.9
  1140.9 7.0 convolution_convert_fusion
  1148.3 5.9 fusion.108
  1154.3 2.7 fusion.38
  1156.9 11.8 fusion.18
  1168.7 8.4 pad_maximum_fusion
  1179.5 10.7 fusion.19
  1191.4 133.4 %reduce-scatter.9.cloned.1.call-done = f32[128,2048]{0,1:T(8,128)} async-done(((f32[1024,2048]{0,1:T(8,128)}), f32[128,2048]{0,1:T(8,128)}) %reduce-scatter.9.cloned.1.call-update) | async-done | bytes 1048592 | tf_op jit(solution)/shard_map/reduce_scatter | solution.py:224
  1330.9 4.4 pad_maximum_fusion.1
  1335.4 13.6 all-gather.35.cloned.1.call-done
  1348.9 26.2 all-gather.37.cloned.1.call-done
  1375.1 5.3 fusion.64
  1381.7 14.6 fusion.48
  1398.3 3.2 all-gather.31.cloned.1.call-done
  1401.4 36.6 all-gather.33.cloned.1.call-done
  1438.0 8.8 fusion.61
  1446.9 17.5 all-gather.45.cloned.1.call-done
  1464.3 66.3 %all-gather.43.cloned.1.call-done = bf16[512,9216]{1,0:T(8,128)(2,1)} async-done(((bf16[128,9216]{1,0:T(8,128)(2,1)}), bf16[512,9216]{1,0:T(8,128)(2,1)}) %all-gather.43.cloned.1.call-update) | async-done | bytes 9437200 | tf_op jit(solution)/shard_map/all_gather | solution.py:182
  1530.7 12.5 fusion.14
  1543.3 13.6 all-gather.39.cloned.1.call-done
  1556.9 121.6 %all-gather.41.cloned.1.call-done = bf16[512,18432]{1,0:T(8,128)(2,1)} async-done(((bf16[128,18432]{1,0:T(8,128)(2,1)}), bf16[512,18432]{1,0:T(8,128)(2,1)}) %all-gather.41.cloned.1.call-update) | async-done | bytes 18874384 | tf_op jit(solution)/shard_map/all_gather | solution.py:194
  1678.4 23.4 fusion.59
  1703.7 74.5 %reduce-scatter.13.cloned.1.call-done = f32[64,2304]{1,0:T(8,128)} async-done(((f32[512,2304]{1,0:T(8,128)}), f32[64,2304]{1,0:T(8,128)}) %reduce-scatter.13.cloned.1.call-update) | async-done | bytes 589840 | tf_op jit(solution)/shard_map/reduce_scatter | solution.py:252
  1778.2 3.1 multiply_reduce_fusion.16
  1781.3 25.6 reduce-scatter.17.cloned.1.call-done
  1808.0 39.2 %all-reduce.1 = f32[576,4]{0,1:T(4,128)S(1)} all-reduce(f32[576,4]{0,1:T(4,128)S(1)} %copy.159), channel_id=8, replica_groups=mesh['rep'=4,'shard'=8] {'shard'}, use_global_device_ids=true, to_apply=%region_25.26.clone | all-reduce | flops 2304 | bytes 18432
  1848.5 126.1 %reduce-scatter.11.cloned.1.call-done = f32[72,4096]{1,0:T(8,128)} async-done(((f32[576,4096]{1,0:T(8,128)}), f32[72,4096]{1,0:T(8,128)}) %reduce-scatter.11.cloned.1.call-update) | async-done | bytes 1179664 | tf_op jit(solution)/shard_map/reduce_scatter | solution.py:250
  1974.6 5.2 multiply_reduce_fusion.7
  1979.8 345.5 %reduce-scatter.15.cloned.1.call-done = f32[288,2304]{1,0:T(8,128)} async-done(((f32[2304,2304]{1,0:T(8,128)}), f32[288,2304]{1,0:T(8,128)}) %reduce-scatter.15.cloned.1.call-update) | async-done | bytes 2654224 | tf_op jit(solution)/shard_map/reduce_scatter | solution.py:254
  2325.3 8.2 multiply_reduce_fusion.3
  2333.5 1249.5 %all-reduce.4.cloned.1.call-done = f32[576,18432]{1,0:T(8,128)} async-done(((f32[576,18432]{1,0:T(8,128)}), f32[576,18432]{1,0:T(8,128)}) %all-reduce.4.cloned.1.call-update) | async-done | bytes 42467344
  3583.0 14.1 multiply_reduce_fusion.4
  3597.1 3.8 stack.85
  3600.8 3.9 stack.77
  3604.8 3.0 fusion.54
  3607.7 39.3 %psum.7 = f32[2,6]{1,0:T(2,128)S(1)} all-reduce(f32[2,6]{1,0:T(2,128)S(1)} %pad_maximum_fusion.6), channel_id=1, replica_groups=mesh['rep'=4,'shard'=8] {'rep','shard'}, use_global_device_ids=true, to_apply=%region_38.39 | all-reduce | flops 12 | bytes 96 | tf_op jit(solution)/shard_map/psum | solution.py:270
  3656.2 3.7 multiply_subtract_fusion.3
  3661.0 4.7 multiply_subtract_fusion.2
  3665.8 2.7 multiply_subtract_fusion.1
  3669.1 2.7 multiply_subtract_fusion
  (256 shorter events, 42.3 us)
Async XLA Ops:
  7.2 74.6 %copy-start.18 = (bf16[128,2304]{1,0:T(8,128)(2,1)S(1)}, bf16[128,2304]{1,0:T(8,128)(2,1)}, u32[]{:S(2)}) copy-start(bf16[128,2304]{1,0:T(8,128)(2,1)} %param.22) | copy-start | bytes 1769476
  7.2 131.8 %all-gather.17.cloned.1.call-start = ((), (), s32[]{:S(2)}) async-start(), calls=%async_computation.5 | async-start | bytes 19464192 | tf_op jit(solution)/shard_map/all_gather | solution.py:115
  9.5 187.1 %all-gather.19.cloned.1.call-start = ((), (), s32[]{:S(2)}) async-start(), calls=%async_computation.6 | async-start | bytes 2359296 | tf_op jit(solution)/shard_map/all_gather | solution.py:139
  81.8 65.0 %copy-start.44 = (f32[2304]{0:T(1024)}, f32[2304]{0:T(1024)S(1)}, u32[]{:S(2)}) copy-start(f32[2304]{0:T(1024)S(1)} %get-tuple-element.48) | copy-start | bytes 27652
  81.8 257.2 %copy-start.42 = (f32[2304]{0:T(1024)}, f32[2304]{0:T(1024)S(1)}, u32[]{:S(2)}) copy-start(f32[2304]{0:T(1024)S(1)} %get-tuple-element.46) | copy-start | bytes 27652
  82.0 64.8 %copy-start.63 = (f32[128]{0:T(128)}, f32[128]{0:T(128)S(1)}, u32[]{:S(2)}) copy-start(f32[128]{0:T(128)S(1)} %fusion.55) | copy-start | bytes 1540
  82.0 64.8 %copy-start.58 = (f32[128]{0:T(128)}, f32[128]{0:T(128)S(1)}, u32[]{:S(2)}) copy-start(f32[128]{0:T(128)S(1)} %fusion.89) | copy-start | bytes 1540
  82.3 64.6 %copy-start.23 = (bf16[128,2304]{1,0:T(8,128)(2,1)}, bf16[128,2304]{1,0:T(8,128)(2,1)S(1)}, u32[]{:S(2)}) copy-start(bf16[128,2304]{1,0:T(8,128)(2,1)S(1)} %fusion.47) | copy-start | bytes 1769476
  148.9 99.8 %all-gather.21.cloned.1.call-start = ((), (), s32[]{:S(2)}) async-start(), calls=%async_computation.7 | async-start | bytes 2359296 | tf_op jit(solution)/shard_map/all_gather | solution.py:138
  150.0 17.4 copy-start.35
  150.0 9.9 copy-start.3
  157.9 174.4 %all-gather.23.cloned.1.call-start = ((), (), s32[]{:S(2)}) async-start(), calls=%async_computation.8 | async-start | bytes 9732096 | tf_op jit(solution)/shard_map/all_gather | solution.py:116
  159.8 412.2 %all-gather.25.cloned.1.call-start = ((), (), s32[]{:S(2)}) async-start(), calls=%async_computation.9 | async-start | bytes 43794432 | tf_op jit(solution)/shard_map/all_gather | solution.py:117
  161.1 650.2 %all-gather.27.cloned.1.call-start = ((), (), s32[]{:S(2)}) async-start(), calls=%async_computation.10 | async-start | bytes 43794432 | tf_op jit(solution)/shard_map/all_gather | solution.py:118
  164.3 886.4 %all-gather.29.cloned.1.call-start = ((), (), s32[]{:S(2)}) async-start(), calls=%async_computation.11 | async-start | bytes 43794432 | tf_op jit(solution)/shard_map/all_gather | solution.py:119
  165.6 1159.3 %reduce-scatter.9.cloned.1.call-start = ((), (), s32[]{:S(2)}) async-start(), calls=%async_computation.12 | async-start | bytes 9437184 | tf_op jit(solution)/shard_map/reduce_scatter | solution.py:224
  167.0 86.0 %copy-start.31 = (pred[128,1024]{0,1:T(8,128)(4,1)}, pred[128,1024]{0,1:T(8,128)(4,1)S(1)}, u32[]{:S(2)}) copy-start(pred[128,1024]{0,1:T(8,128)(4,1)S(1)} %or_and_fusion) | copy-start | bytes 393220
  167.7 84.0 %copy-start.40 = (bf16[128,8,256]{2,0,1:T(8,128)(2,1)}, bf16[128,8,256]{2,0,1:T(8,128)(2,1)S(1)}, u32[]{:S(2)}) copy-start(bf16[128,8,256]{2,0,1:T(8,128)(2,1)S(1)} %copy.123) | copy-start | bytes 1572868
  199.9 53.1 %copy-start.20 = (bf16[1024,4,256]{2,1,0:T(4,128)(2,1)}, bf16[1024,4,256]{2,1,0:T(4,128)(2,1)S(1)}, u32[]{:S(2)}) copy-start(bf16[1024,4,256]{2,1,0:T(4,128)(2,1)S(1)} %reshape.450) | copy-start | bytes 6291460
  255.5 82.1 %copy-start.28 = (bf16[4,256,2,128]{3,1,2,0:T(8,128)(2,1)}, bf16[4,256,2,128]{3,1,2,0:T(8,128)(2,1)S(1)}, u32[]{:S(2)}) copy-start(bf16[4,256,2,128]{3,1,2,0:T(8,128)(2,1)S(1)} %fusion.44) | copy-start | bytes 1572868
  337.5 253.9 %copy-start.60 = (f32[128]{0:T(128)}, f32[128]{0:T(128)S(1)}, u32[]{:S(2)}) copy-start(f32[128]{0:T(128)S(1)} %get-tuple-element.111) | copy-start | bytes 1540
  338.9 252.5 %copy-start.65 = (f32[128]{0:T(128)}, f32[128]{0:T(128)S(1)}, u32[]{:S(2)}) copy-start(f32[128]{0:T(128)S(1)} %get-tuple-element.67) | copy-start | bytes 1540
  339.0 252.5 %copy-start.51 = (f32[128]{0:T(128)}, f32[128]{0:T(128)S(1)}, u32[]{:S(2)}) copy-start(f32[128]{0:T(128)S(1)} %fusion.91) | copy-start | bytes 1540
  339.2 252.3 %copy-start.11 = (bf16[128,2304]{1,0:T(8,128)(2,1)}, bf16[128,2304]{1,0:T(8,128)(2,1)S(1)}, u32[]{:S(2)}) copy-start(bf16[128,2304]{1,0:T(8,128)(2,1)S(1)} %multiply_convert_fusion.2) | copy-start | bytes 1769476
  833.1 233.2 %copy-start.6 = (bf16[128,9216]{1,0:T(8,128)(2,1)}, bf16[128,9216]{1,0:T(8,128)(2,1)S(1)}, u32[]{:S(2)}) copy-start(bf16[128,9216]{1,0:T(8,128)(2,1)S(1)} %get-tuple-element.113) | copy-start | bytes 7077892
  1050.8 15.5 copy-start.46
  1093.7 21.5 copy-start.9
  1115.2 21.8 copy-start.66
  1115.2 21.8 copy-start.8
  1115.2 21.8 copy-start.27
  1115.2 21.8 copy-start.43
  1115.2 21.8 copy-start.52
  1115.3 21.8 copy-start.54
  1140.9 7.1 copy-start.24
  1140.9 7.3 copy-start.32
  1148.3 6.0 copy-start.21
  1177.2 171.8 %all-gather.35.cloned.1.call-start = ((), (), s32[]{:S(2)}) async-start(), calls=%async_computation.16 | async-start | bytes 2621440 | tf_op jit(solution)/shard_map/all_gather | solution.py:241
  1177.9 197.2 %all-gather.37.cloned.1.call-start = ((), (), s32[]{:S(2)}) async-start(), calls=%async_computation.17 | async-start | bytes 2949120 | tf_op jit(solution)/shard_map/all_gather | solution.py:242
  1178.5 222.9 %all-gather.31.cloned.1.call-start = ((), (), s32[]{:S(2)}) async-start(), calls=%async_computation.13 | async-start | bytes 2949120 | tf_op jit(solution)/shard_map/all_gather | solution.py:243
  1179.2 258.8 %all-gather.33.cloned.1.call-start = ((), (), s32[]{:S(2)}) async-start(), calls=%async_computation.14 | async-start | bytes 5242880 | tf_op jit(solution)/shard_map/all_gather | solution.py:244
  1191.4 136.4 %copy-start.33 = (bf16[16,8,8,256]{3,1,2,0:T(8,128)(2,1)}, bf16[16,8,8,256]{3,1,2,0:T(8,128)(2,1)S(1)}, u32[]{:S(2)}) copy-start(bf16[16,8,8,256]{3,1,2,0:T(8,128)(2,1)S(1)} %copy.168) | copy-start | bytes 1572868
  1328.9 135.4 %all-gather.45.cloned.1.call-start = ((), (), s32[]{:S(2)}) async-start(), calls=%async_computation.22 | async-start | bytes 2949120 | tf_op jit(solution)/shard_map/all_gather | solution.py:183
  1329.7 201.0 %all-gather.43.cloned.1.call-start = ((), (), s32[]{:S(2)}) async-start(), calls=%async_computation.21 | async-start | bytes 11796480 | tf_op jit(solution)/shard_map/all_gather | solution.py:182
  1330.3 226.6 %all-gather.39.cloned.1.call-start = ((), (), s32[]{:S(2)}) async-start(), calls=%async_computation.19 | async-start | bytes 2949120 | tf_op jit(solution)/shard_map/all_gather | solution.py:193
  1330.9 347.6 %all-gather.41.cloned.1.call-start = ((), (), s32[]{:S(2)}) async-start(), calls=%async_computation.20 | async-start | bytes 23592960 | tf_op jit(solution)/shard_map/all_gather | solution.py:194
  1335.3 442.9 %reduce-scatter.13.cloned.1.call-start = ((), (), s32[]{:S(2)}) async-start(), calls=%async_computation.18 | async-start | bytes 5308416 | tf_op jit(solution)/shard_map/reduce_scatter | solution.py:252
  1380.5 426.4 %reduce-scatter.17.cloned.1.call-start = ((), (), s32[]{:S(2)}) async-start(), calls=%async_computation.24 | async-start | bytes 1474560
  1397.8 576.8 %reduce-scatter.11.cloned.1.call-start = ((), (), s32[]{:S(2)}) async-start(), calls=%async_computation.15 | async-start | bytes 10616832 | tf_op jit(solution)/shard_map/reduce_scatter | solution.py:250
  1446.8 878.5 %reduce-scatter.15.cloned.1.call-start = ((), (), s32[]{:S(2)}) async-start(), calls=%async_computation.23 | async-start | bytes 23887872 | tf_op jit(solution)/shard_map/reduce_scatter | solution.py:254
  1543.2 2039.8 %all-reduce.4.cloned.1.call-start = ((), (), s32[]{:S(2)}) async-start(), calls=%async_computation.25 | async-start | bytes 84934656
  1701.8 76.4 %copy-start.25 = (f32[64,2304]{1,0:T(8,128)S(1)}, f32[64,2304]{1,0:T(8,128)}, u32[]{:S(2)}) copy-start(f32[64,2304]{1,0:T(8,128)} %param.26) | copy-start | bytes 1769476
  1701.8 76.4 %copy-start.38 = (f32[64,2304]{1,0:T(8,128)S(1)}, f32[64,2304]{1,0:T(8,128)}, u32[]{:S(2)}) copy-start(f32[64,2304]{1,0:T(8,128)} %param.38) | copy-start | bytes 1769476
  1701.8 76.4 %copy-start.39 = (f32[64,2304]{1,0:T(8,128)S(1)}, f32[64,2304]{1,0:T(8,128)}, u32[]{:S(2)}) copy-start(f32[64,2304]{1,0:T(8,128)} %param.32) | copy-start | bytes 1769476
  1701.8 79.5 %copy-start.64 = (f32[128]{0:T(128)S(1)}, f32[128]{0:T(128)}, u32[]{:S(2)}) copy-start(f32[128]{0:T(128)} %copy-done.63) | copy-start | bytes 1540
  1701.9 145.4 %copy-start.50 = (f32[72,4]{0,1:T(4,128)S(1)}, f32[72,4]{0,1:T(4,128)}, u32[]{:S(2)}) copy-start(f32[72,4]{0,1:T(4,128)} %param.30) | copy-start | bytes 3460
  1701.9 145.3 %copy-start.56 = (f32[72,4]{0,1:T(4,128)S(1)}, f32[72,4]{0,1:T(4,128)}, u32[]{:S(2)}) copy-start(f32[72,4]{0,1:T(4,128)} %param.42) | copy-start | bytes 3460
  1701.9 145.3 %copy-start.57 = (f32[72,4]{0,1:T(4,128)S(1)}, f32[72,4]{0,1:T(4,128)}, u32[]{:S(2)}) copy-start(f32[72,4]{0,1:T(4,128)} %param.36) | copy-start | bytes 3460
  1848.5 476.8 %copy-start.2 = (f32[288,2304]{1,0:T(8,128)S(1)}, f32[288,2304]{1,0:T(8,128)}, u32[]{:S(2)}) copy-start(f32[288,2304]{1,0:T(8,128)} %param.29) | copy-start | bytes 7962628
  3597.1 49.9 %copy-start.62 = (f32[6]{0:T(128)S(1)}, f32[6]{0:T(128)}, u32[]{:S(2)}) copy-start(f32[6]{0:T(128)} %constant.179) | copy-start | bytes 76
  3607.7 52.1 %copy-start.26 = (f32[64,2304]{1,0:T(8,128)S(1)}, f32[64,2304]{1,0:T(8,128)}, u32[]{:S(2)}) copy-start(f32[64,2304]{1,0:T(8,128)} %param.26) | copy-start | bytes 1769476
  3647.0 12.9 copy-start.29
  3647.0 12.9 copy-start.30
  3647.0 14.0 copy-start.47
  3656.2 4.8 copy-start.17
  (26 other events, 53.9 us)
Sparse Core Ops, SparseCore 0:
  11.5 127.4 all-gather.16
  149.0 47.4 all-gather.18
  199.2 49.5 all-gather.20
  252.1 80.2 all-gather.22
  335.7 236.3 all-gather.24
  575.4 235.8 all-gather.26
  814.8 235.8 all-gather.28
  1177.3 147.5 reduce-scatter.8
  1327.1 21.8 all-gather.34
  1351.0 24.0 all-gather.36
  1377.3 24.0 all-gather.30
  1403.5 34.4 all-gather.32
  1440.2 24.0 all-gather.44
  1466.4 64.2 all-gather.42
  1532.7 24.0 all-gather.38
  1558.4 120.0 all-gather.40
  1682.9 95.2 reduce-scatter.12
  1781.4 25.4 reduce-scatter.16
  1811.0 163.4 reduce-scatter.10
  1978.9 346.3 reduce-scatter.14
  2330.1 1252.8 all-reduce.3
where the time goes:
time: 3680 us
  waiting for transfers between devices  3140 us (85%)
  matrix products  243 us (7%)
  blocking collectives  149 us (4%)
  other arithmetic  90.7 us (2%)
    unnamed x23, waiting for transfers between devices  1280 us
    reduce_scatter x1, waiting for transfers between devices, per_device(): lax.psum_scatter(part_down, 'shard', scatter_dimension=0, tiled=True)  346 us
    all_gather x1, waiting for transfers between devices, per_device(): lax.all_gather(ffn_gate.astype(bf16), ('rep', 'shard'), axis=0, tiled=True)  233 us
    all_gather x1, waiting for transfers between devices, per_device(): lax.all_gather(ffn_up.astype(bf16), ('rep', 'shard'), axis=0, tiled=True)  220 us
    all_gather x1, waiting for transfers between devices, per_device(): lax.all_gather(ffn_down.astype(bf16), ('rep', 'shard'), axis=0, tiled=True)  218 us
    reduce_scatter x1, waiting for transfers between devices, per_device(): lax.psum_scatter(jnp.concatenate([d_key, d_value], axis=1), 'shard', scat...  133 us
    reduce_scatter x1, waiting for transfers between devices, per_device(): lax.psum_scatter(part_in, 'shard', scatter_dimension=0, tiled=True)  126 us
    all_gather x1, waiting for transfers between devices, per_device(): lax.all_gather(gate_up_grad, 'rep', axis=0, tiled=True)  122 us
  transfers between devices with their start and end apart: 21, of which 21 were waited for; matrix products, arithmetic and copies ran while one was open for 5% of the time, Pallas kernels for 0%

commit v1 on v0

--- a/solution.py
+++ b/solution.py
@@ -1,6 +1,10 @@
+import functools
+
 import jax
 import jax.numpy as jnp
 from jax import lax
+from jax.experimental import pallas as pl
+from jax.experimental.pallas import tpu as pltpu
 from jax.sharding import PartitionSpec as P
 
 HEADS = 8
@@ -305,61 +309,782 @@
     )
 
 
+MESH = pl.DeviceIdType.MESH
+VM = pltpu.VMEM
+HB = pl.ANY
+UNITS = 4
+VMEM_LIMIT = 60 << 20
+
+
+def ring_places(count):
+    inner = 2 if count == 8 else 4
+    outer = count // inner
+
+    def place(shard):
+        major = shard // inner
+        minor = shard % inner
+        return minor * outer + major + (minor % 2) * (outer - 1 - 2 * major)
+
+    def shard_at(spot):
+        minor = spot // outer
+        major = spot % outer
+        return (major + (minor % 2) * (outer - 1 - 2 * major)) * inner + minor
+
+    return place, shard_at
+
+
+def meet(devices):
+    barrier = pltpu.get_barrier_semaphore()
+    for device in devices:
+        pl.semaphore_signal(barrier, inc=1, device_id=device, device_id_type=MESH)
+    pl.semaphore_wait(barrier, len(devices))
+
+
+def remote(src, dst, send_sem, recv_sem, device):
+    return pltpu.make_async_remote_copy(
+        src_ref=src,
+        dst_ref=dst,
+        send_sem=send_sem,
+        recv_sem=recv_sem,
+        device_id=device,
+        device_id_type=MESH,
+    )
+
+
+class Ring:
+    def __init__(self, count):
+        place, shard_at = ring_places(count)
+        self.count = count
+        self.half = count // 2
+        self.rep = lax.axis_index("rep")
+        self.me = lax.axis_index("shard")
+        self.spot = place(self.me)
+        self.shard_at = shard_at
+        self.next = [(self.rep, self.at(1)), (self.rep, self.at(count - 1))]
+
+    def at(self, ahead):
+        return self.shard_at((self.spot + ahead) % self.count)
+
+    def away(self, way, hops):
+        return self.at(hops if way == 0 else self.count - hops)
+
+    def units(self, way, hop):
+        order = list(range(UNITS)) if way == 0 else list(range(UNITS))[::-1]
+        return order if hop < self.half else order[: UNITS // 2]
+
+
+def ring_gather_kernel(count, x_ref, out_ref, send, recv, local):
+    ring = Ring(count)
+    rows = x_ref.shape[0] // UNITS
+
+    def part(unit):
+        return pl.ds(unit * rows, rows)
+
+    def hop_copy(way, hop, unit):
+        origin = ring.away(1 - way, hop - 1) if hop > 1 else ring.me
+        src = x_ref.at[part(unit)] if hop == 1 else out_ref.at[origin, part(unit)]
+        return remote(
+            src,
+            out_ref.at[origin, part(unit)],
+            send.at[way, hop - 1, unit],
+            recv.at[way, hop - 1, unit],
+            ring.next[way],
+        )
+
+    meet(ring.next)
+    own = pltpu.make_async_copy(x_ref, out_ref.at[ring.me], local)
+    own.start()
+    started = []
+    for index in range(UNITS):
+        for way in (0, 1):
+            copy = hop_copy(way, 1, ring.units(way, 1)[index])
+            copy.start()
+            started.append(copy)
+    for hop in range(1, ring.half + 1):
+        for index in range(len(ring.units(0, hop))):
+            for way in (0, 1):
+                unit = ring.units(way, hop)[index]
+                hop_copy(way, hop, unit).wait_recv()
+                if hop < ring.half and unit in ring.units(way, hop + 1):
+                    copy = hop_copy(way, hop + 1, unit)
+                    copy.start()
+                    started.append(copy)
+    for copy in started:
+        copy.wait_send()
+    own.wait()
+
+
+def ring_gather(block, count, collective_id):
+    rows, columns = block.shape
+    hops = count // 2
+    gathered = pl.pallas_call(
+        functools.partial(ring_gather_kernel, count),
+        out_shape=jax.ShapeDtypeStruct((count, rows, columns), block.dtype),
+        in_specs=[pl.BlockSpec(memory_space=VM)],
+        out_specs=pl.BlockSpec(memory_space=VM),
+        scratch_shapes=[
+            pltpu.SemaphoreType.DMA((2, hops, UNITS)),
+            pltpu.SemaphoreType.DMA((2, hops, UNITS)),
+            pltpu.SemaphoreType.DMA,
+        ],
+        compiler_params=pltpu.CompilerParams(
+            collective_id=collective_id, has_side_effects=True, vmem_limit_bytes=VMEM_LIMIT
+        ),
+        name=f"ring_gather_{collective_id}",
+    )(block)
+    return gathered.reshape(count * rows, columns)
+
+
+def ring_reduce_kernel(count, x_ref, out_ref, held, landed, send, recv):
+    ring = Ring(count)
+    rows = out_ref.shape[0] // UNITS
+    hops = ring.half
+
+    def part(unit):
+        return pl.ds(unit * rows, rows)
+
+    def step_copy(way, step, unit):
+        return remote(
+            held.at[way, step, part(unit)],
+            landed.at[way, step, part(unit)],
+            send.at[way, step, unit],
+            recv.at[way, step, unit],
+            ring.next[way],
+        )
+
+    meet(ring.next)
+    started = []
+    for step in range(hops):
+        order = ring.units(0, hops - step), ring.units(1, hops - step)
+        before = [ring.units(way, hops - step + 1) if step else [] for way in (0, 1)]
+        for index in range(len(order[0])):
+            for way in (0, 1):
+                unit = order[way][index]
+                block = x_ref[ring.away(way, hops - step), part(unit), :].astype(jnp.float32)
+                if unit in before[way]:
+                    step_copy(way, step - 1, unit).wait_recv()
+                    block += landed[way, step - 1, part(unit), :].astype(jnp.float32)
+                held[way, step, part(unit), :] = block.astype(held.dtype)
+                copy = step_copy(way, step, unit)
+                copy.start()
+                started.append(copy)
+    for index in range(UNITS):
+        unit = index
+        total = x_ref[ring.me, part(unit), :].astype(jnp.float32)
+        for way in (0, 1):
+            step_copy(way, hops - 1, unit).wait_recv()
+            total += landed[way, hops - 1, part(unit), :].astype(jnp.float32)
+        out_ref[part(unit), :] = total
+    for copy in started:
+        copy.wait_send()
+
+
+def ring_reduce(partial, count, collective_id):
+    rows, columns = partial.shape[0] // count, partial.shape[1]
+    hops = count // 2
+    return pl.pallas_call(
+        functools.partial(ring_reduce_kernel, count),
+        out_shape=jax.ShapeDtypeStruct((rows, columns), jnp.float32),
+        in_specs=[pl.BlockSpec(memory_space=VM)],
+        out_specs=pl.BlockSpec(memory_space=VM),
+        scratch_shapes=[
+            pltpu.VMEM((2, hops, rows, columns), jnp.bfloat16),
+            pltpu.VMEM((2, hops, rows, columns), jnp.bfloat16),
+            pltpu.SemaphoreType.DMA((2, hops, UNITS)),
+            pltpu.SemaphoreType.DMA((2, hops, UNITS)),
+        ],
+        compiler_params=pltpu.CompilerParams(
+            collective_id=collective_id, has_side_effects=True, vmem_limit_bytes=VMEM_LIMIT
+        ),
+        name=f"ring_reduce_{collective_id}",
+    )(partial.reshape(count, rows, columns))
+
+
+def rep_partners(rep):
+    return (rep + 2) % 4, rep + 1 - 2 * (rep % 2)
+
+
+def everyone(rep, me, reps, count):
+    here = rep * count + me
+    total = reps * count
+    return [
+        (((here + k) % total) // count, ((here + k) % total) % count) for k in range(1, total)
+    ]
+
+
+def weights_kernel(
+    reps, count, in_ref, gu_ref, dn_ref, ou_ref, w_in, w_gu, w_dn, w_ou, a_send, a_recv, x_send, x_recv,
+    c_send, c_recv, d_send, d_recv, o_send, o_recv, n_send, n_recv, loc
+):
+    rep = lax.axis_index("rep")
+    me = lax.axis_index("shard")
+    across, beside = rep_partners(rep)
+    meet(everyone(rep, me, reps, count))
+    started = []
+
+    def go(copy):
+        copy.start()
+        started.append(copy)
+
+    per_head = count * reps // HEADS
+    mine = rep * count + me
+    target = mine // per_head
+    slot = mine % per_head
+    locals_ = []
+
+    def ou_copy(j):
+        return remote(ou_ref.at[j], w_ou.at[j, slot], o_send.at[j], o_recv.at[slot], (j, target))
+
+    def is_self(j):
+        return (rep == j) & (me == target)
+
+    for j in range(reps):
+        @pl.when(jnp.logical_not(is_self(j)))
+        def _():
+            ou_copy(j).start()
+
+        @pl.when(is_self(j))
+        def _():
+            pltpu.make_async_copy(ou_ref.at[j], w_ou.at[j, slot], o_recv.at[slot]).start()
+
+    pairs = ((in_ref, w_in), (gu_ref, w_gu))
+
+    def spread(which, k):
+        to = (me + k) % count
+        src, dst = pairs[which]
+        return remote(
+            src.at[to], dst.at[rep, me], a_send.at[which, k], a_recv.at[which, k], (rep, to)
+        )
+
+    def arrived(which, k):
+        frm = (me + count - k) % count
+        src, dst = pairs[which]
+        return remote(
+            src.at[frm], dst.at[rep, frm], a_send.at[which, k], a_recv.at[which, k], (rep, frm)
+        )
+
+    def forward(which, k, hop):
+        frm = (me + count - k) % count
+        src, dst = pairs[which]
+        block = src.at[me] if k == 0 else dst.at[rep, frm]
+        if hop == 0:
+            return remote(
+                block, dst.at[rep, frm], x_send.at[which, k], x_recv.at[which, k], (across, me)
+            )
+        if hop == 1:
+            return remote(
+                block, dst.at[rep, frm], c_send.at[which, k], c_recv.at[which, k], (beside, me)
+            )
+        return remote(
+            dst.at[across, frm], dst.at[across, frm], d_send.at[which, k], d_recv.at[which, k],
+            (beside, me),
+        )
+
+    for k in range(1, count):
+        go(spread(0, k))
+    go(forward(0, 0, 0))
+    go(forward(0, 0, 1))
+    dn_x = remote(dn_ref, w_dn.at[rep], n_send.at[0], n_recv.at[0], (across, me))
+    dn_c = remote(dn_ref, w_dn.at[rep], n_send.at[1], n_recv.at[1], (beside, me))
+    dn_d = remote(w_dn.at[across], w_dn.at[across], n_send.at[2], n_recv.at[2], (beside, me))
+    go(dn_x)
+    go(dn_c)
+    for k in range(1, count):
+        go(spread(1, k))
+    go(forward(1, 0, 0))
+    go(forward(1, 0, 1))
+    for index, (src, dst) in enumerate(
+        ((in_ref.at[me], w_in.at[rep, me]), (gu_ref.at[me], w_gu.at[rep, me]), (dn_ref, w_dn.at[rep]))
+    ):
+        copy = pltpu.make_async_copy(src, dst, loc.at[index])
+        copy.start()
+        locals_.append(copy)
+    for k in range(1, count):
+        arrived(0, k).wait_recv()
+        go(forward(0, k, 0))
+        go(forward(0, k, 1))
+    for k in range(count):
+        forward(0, k, 0).wait_recv()
+        go(forward(0, k, 2))
+    for i in range(per_head):
+        remote(
+            ou_ref.at[0], w_ou.at[rep, i], o_send.at[0], o_recv.at[i], (across, me)
+        ).wait_recv()
+    ou_x = remote(w_ou.at[rep], w_ou.at[rep], n_send.at[3], n_recv.at[3], (across, me))
+    ou_c = remote(w_ou.at[rep], w_ou.at[rep], n_send.at[4], n_recv.at[4], (beside, me))
+    ou_d = remote(w_ou.at[across], w_ou.at[across], n_send.at[5], n_recv.at[5], (beside, me))
+    go(ou_x)
+    go(ou_c)
+    for k in range(1, count):
+        arrived(1, k).wait_recv()
+        go(forward(1, k, 0))
+        go(forward(1, k, 1))
+    dn_x.wait_recv()
+    go(dn_d)
+    ou_x.wait_recv()
+    go(ou_d)
+    for k in range(count):
+        forward(1, k, 0).wait_recv()
+        go(forward(1, k, 2))
+    for which in (0, 1):
+        for k in range(count):
+            forward(which, k, 1).wait_recv()
+            forward(which, k, 2).wait_recv()
+    for copy in (dn_c, dn_d, ou_c, ou_d):
+        copy.wait_recv()
+    for copy in started:
+        copy.wait_send()
+    for j in range(reps):
+        @pl.when(jnp.logical_not(is_self(j)))
+        def _():
+            ou_copy(j).wait_send()
+    for copy in locals_:
+        copy.wait()
+
+
+def spread_weights(reps, count, w_in, w_gu, w_dn, w_ou, collective_id):
+    dma = pltpu.SemaphoreType.DMA
+    per_head = count * reps // HEADS
+    low = jnp.bfloat16
+    return pl.pallas_call(
+        functools.partial(weights_kernel, reps, count),
+        out_shape=[
+            jax.ShapeDtypeStruct((reps,) + w_in.shape, low),
+            jax.ShapeDtypeStruct((reps,) + w_gu.shape, low),
+            jax.ShapeDtypeStruct((reps,) + w_dn.shape, low),
+            jax.ShapeDtypeStruct((reps, per_head) + w_ou.shape[1:], low),
+        ],
+        in_specs=[pl.BlockSpec(memory_space=HB)] * 4,
+        out_specs=[pl.BlockSpec(memory_space=HB)] * 4,
+        scratch_shapes=[dma((2, count))] * 8 + [dma((reps,)), dma((per_head,)), dma((6,)), dma((6,)), dma((3,))],
+        compiler_params=pltpu.CompilerParams(
+            collective_id=collective_id, has_side_effects=True, vmem_limit_bytes=VMEM_LIMIT
+        ),
+        name="spread_weights",
+    )(w_in, w_gu, w_dn, w_ou)
+
+
+def rep_sum(part, from_core, to_across, from_across, sums, sems, rep, me, pieces, emit):
+    across, beside = rep_partners(rep)
+    core = rep % 2
+    chip = rep // 2
+    far = 1 - chip
+    c_send, c_recv, x_send, x_recv = sems
+    f32 = jnp.float32
+
+    def core_copy(side, piece):
+        owner_chip = far if side == 0 else chip
+        return remote(
+            part.at[owner_chip * 2 + 1 - core, piece],
+            from_core.at[side, piece],
+            c_send.at[side, piece],
+            c_recv.at[side, piece],
+            (beside, me),
+        )
+
+    def cross_copy(piece):
+        return remote(
+            to_across.at[piece], from_across.at[piece], x_send.at[piece], x_recv.at[piece], (across, me)
+        )
+
+    for side in (0, 1):
+        for piece in pieces:
+            core_copy(side, piece).start()
+    for piece in pieces:
+        core_copy(0, piece).wait_recv()
+        to_across[piece] = (
+            part[far * 2 + core, piece].astype(f32) + from_core[0, piece].astype(f32)
+        ).astype(to_across.dtype)
+        cross_copy(piece).start()
+    for piece in pieces:
+        core_copy(1, piece).wait_recv()
+        cross_copy(piece).wait_recv()
+        emit(
+            piece,
+            part[rep, piece].astype(f32)
+            + from_core[1, piece].astype(f32)
+            + from_across[piece].astype(f32),
+        )
+    for piece in pieces:
+        core_copy(0, piece).wait_send()
+        core_copy(1, piece).wait_send()
+        cross_copy(piece).wait_send()
+
+
+def grads_kernel(
+    reps, count, full, a_part, b_part, a_out, b_out, a_core, a_to, a_from, a_sum, b_core, b_to, b_from, b_sum,
+    ac_s, ac_r, ax_s, ax_r, bc_s, bc_r, bx_s, bx_r, s_send, s_recv, o_send, o_recv
+):
+    rep = lax.axis_index("rep")
+    me = lax.axis_index("shard")
+    meet(everyone(rep, me, reps, count))
+
+    a_pieces = [(me + k) % count for k in range(1, count)] + [me]
+
+    def a_send(k):
+        to = (me + k) % count
+        return remote(a_sum.at[to], a_out.at[me], s_send.at[k], s_recv.at[k], (rep, to))
+
+    def a_arrived(k):
+        frm = (me + count - k) % count
+        return remote(a_sum.at[frm], a_out.at[frm], s_send.at[k], s_recv.at[k], (rep, frm))
+
+    order = {id(piece): k for k, piece in zip(list(range(1, count)) + [0], a_pieces)}
+
+    def a_emit(piece, total):
+        k = order[id(piece)]
+        if k == 0:
+            a_out[me] = total.astype(a_out.dtype)
+        else:
+            a_sum[piece] = total.astype(a_sum.dtype)
+            a_send(k).start()
+
+    rep_sum(a_part, a_core, a_to, a_from, a_sum, (ac_s, ac_r, ax_s, ax_r), rep, me, a_pieces, a_emit)
+
+    b_pieces = list(range(b_part.shape[1]))
+    if full is None:
+        def b_emit(piece, total):
+            b_out[piece] = total
+    else:
+        def b_send(piece):
+            block = me * full + piece
+            owner = (block // count, block % count)
+            return remote(b_sum.at[piece], b_out.at[rep], o_send.at[piece], o_recv.at[rep], owner)
+
+        def b_self(piece):
+            return me * full + piece == rep * count + me
+
+        def b_emit(piece, total):
+            b_sum[piece] = total.astype(b_sum.dtype)
+
+            @pl.when(jnp.logical_not(b_self(piece)))
+            def _():
+                b_send(piece).start()
+
+            @pl.when(b_self(piece))
+            def _():
+                pltpu.make_async_copy(b_sum.at[piece], b_out.at[rep], o_recv.at[rep]).start()
+
+    rep_sum(b_part, b_core, b_to, b_from, b_sum, (bc_s, bc_r, bx_s, bx_r), rep, me, b_pieces, b_emit)
+
+    for k in range(1, count):
+        a_arrived(k).wait_recv()
+    for k in range(1, count):
+        a_send(k).wait_send()
+    if full is not None:
+        for j in range(reps):
+            remote(
+                b_sum.at[0], b_out.at[j], o_send.at[0], o_recv.at[j], (rep, (me + 1) % count)
+            ).wait_recv()
+        for piece in b_pieces:
+            @pl.when(jnp.logical_not(b_self(piece)))
+            def _():
+                b_send(piece).wait_send()
+
+
+def return_grads(reps, count, full, a_part, b_part, collective_id):
+    dma = pltpu.SemaphoreType.DMA
+    low = jnp.bfloat16
+    a_block = a_part.shape[1:]
+    b_block = b_part.shape[1:]
+    b_count = b_block[0]
+    b_shape = (
+        jax.ShapeDtypeStruct(b_block, jnp.float32)
+        if full is None
+        else jax.ShapeDtypeStruct((reps,) + b_block[1:], low)
+    )
+    b_sum = b_block if full is not None else (1, 16, 128)
+    scratch = [
+        pltpu.VMEM((2,) + a_block, low),
+        pltpu.VMEM(a_block, low),
+        pltpu.VMEM(a_block, low),
+        pltpu.VMEM(a_block, low),
+        pltpu.VMEM((2,) + b_block, low),
+        pltpu.VMEM(b_block, low),
+        pltpu.VMEM(b_block, low),
+        pltpu.VMEM(b_sum, low),
+        dma((2, count)),
+        dma((2, count)),
+        dma((count,)),
+        dma((count,)),
+        dma((2, b_count)),
+        dma((2, b_count)),
+        dma((b_count,)),
+        dma((b_count,)),
+        dma((count,)),
+        dma((count,)),
+        dma((b_count,)),
+        dma((reps,)),
+    ]
+    return pl.pallas_call(
+        functools.partial(grads_kernel, reps, count, full),
+        out_shape=[jax.ShapeDtypeStruct(a_block, low), b_shape],
+        in_specs=[pl.BlockSpec(memory_space=VM)] * 2,
+        out_specs=[pl.BlockSpec(memory_space=VM)] * 2,
+        scratch_shapes=scratch,
+        compiler_params=pltpu.CompilerParams(
+            collective_id=collective_id, has_side_effects=True, vmem_limit_bytes=VMEM_LIMIT
+        ),
+        name=f"return_grads_{collective_id}",
+    )(a_part, b_part)
+
+
+def small_kernel(reps, count, spread, x_ref, out_ref, send, recv):
+    rep = lax.axis_index("rep")
+    me = lax.axis_index("shard")
+    here = rep * count + me
+    total = reps * count
+    others = everyone(rep, me, reps, count)
+    meet(others)
+    copies = []
+    for k, device in enumerate(others):
+        to = (here + k + 1) % total
+        src = x_ref.at[to] if spread else x_ref
+        copy = remote(src, out_ref.at[here], send.at[k], recv.at[k], device)
+        copy.start()
+        copies.append(copy)
+    out_ref[here] = x_ref[here] if spread else x_ref[...]
+    for k in range(total - 1):
+        frm = (here + total - k - 1) % total
+        remote(out_ref.at[frm], out_ref.at[frm], send.at[k], recv.at[k], others[k]).wait_recv()
+    for copy in copies:
+        copy.wait_send()
+
+
+def small_exchange(tiles, reps, count, spread, collective_id):
+    total = reps * count
+    return pl.pallas_call(
+        functools.partial(small_kernel, reps, count, spread),
+        out_shape=jax.ShapeDtypeStruct((total,) + tiles.shape[-2:], tiles.dtype),
+        in_specs=[pl.BlockSpec(memory_space=VM)],
+        out_specs=pl.BlockSpec(memory_space=VM),
+        scratch_shapes=[pltpu.SemaphoreType.DMA((total - 1,)), pltpu.SemaphoreType.DMA((total - 1,))],
+        compiler_params=pltpu.CompilerParams(
+            collective_id=collective_id, has_side_effects=True, vmem_limit_bytes=VMEM_LIMIT
+        ),
+        name=f"small_exchange_{collective_id}",
+    )(tiles)
+
+
+def as_tile(flat):
+    width = flat.shape[-1]
+    filled = -(-width // 1024) * 1024
+    padded = jnp.pad(flat, [(0, 0)] * (flat.ndim - 1) + [(0, filled - width)])
+    return padded.reshape(flat.shape[:-1] + (filled // 128, 128))
+
+
+def turn(flat, cosine, sine):
+    half = flat.shape[1] // 2
+    first, second = flat[:, :half], flat[:, half:]
+    return jnp.concatenate([first * cosine - second * sine, second * cosine + first * sine], axis=1)
+
+
+def norm_back(value, gain_col, grad):
+    scale = lax.rsqrt(jnp.mean(value * value, axis=-1, keepdims=True) + 1e-06)
+    normed = value * scale
+    weighted = grad * (1.0 + gain_col)
+    inner = jnp.mean(weighted * normed, axis=-1, keepdims=True)
+    return scale * (weighted - normed * inner), jnp.sum(grad * normed, axis=0)
+
+
+def dot_tn(left, right):
+    return lax.dot_general(left, right, (((0,), (0,)), ((), ())), preferred_element_type=jnp.float32)
+
+
+def split_device(
+    tokens, cotangent, piece_starts, inproj, outproj, ffn_gate, ffn_up, ffn_down, norm_gains,
+    mean_inproj, mean_outproj, mean_gate, mean_up, mean_down, mean_gains,
+    square_inproj, square_outproj, square_gate, square_up, square_down, square_gains,
+):
+    bf16, f32 = jnp.bfloat16, jnp.float32
+    reps, count = lax.axis_size("rep"), lax.axis_size("shard")
+    rep = lax.axis_index("rep")
+    me = lax.axis_index("shard")
+    total = reps * count
+    rows, width = tokens.shape
+    seq_len = rows * count
+    group = HEADS // KV_HEADS
+    q_width, k_width = HEADS * HEAD_DIM, KV_HEADS * HEAD_DIM
+    d_rows = inproj.shape[0]
+    ff = ffn_gate.shape[1]
+    ff_block = ff // total
+    ff_part = ff // count
+    o_rows = outproj.shape[0]
+    per_head = HEAD_DIM // o_rows
+    piece = o_rows // reps
+
+    low_in = inproj.astype(bf16)
+    q_cols = low_in[:, :q_width].reshape(d_rows, HEADS, HEAD_DIM)
+    k_cols = jnp.repeat(low_in[:, q_width : q_width + k_width].reshape(d_rows, KV_HEADS, HEAD_DIM), group, axis=1)
+    v_cols = jnp.repeat(low_in[:, q_width + k_width :].reshape(d_rows, KV_HEADS, HEAD_DIM), group, axis=1)
+    cut_in = jnp.concatenate([q_cols, k_cols, v_cols], axis=2).transpose(1, 0, 2)
+
+    def cut_ff(weight):
+        return weight.astype(bf16).reshape(d_rows, reps, count, ff_block).transpose(2, 0, 1, 3).reshape(
+            count, d_rows, ff_part
+        )
+
+    cut_gu = jnp.concatenate([cut_ff(ffn_gate), cut_ff(ffn_up)], axis=1)
+    cut_out = outproj.astype(bf16).reshape(reps, piece, width)
+    got_in, got_gu, got_down, got_out = spread_weights(
+        reps, count, cut_in, cut_gu, ffn_down.astype(bf16), cut_out, 1
+    )
+    w_in = got_in.reshape(width, -1)
+    got_gu = got_gu.reshape(total, 2, d_rows, ff_part)
+    w_gate = got_gu[:, 0].reshape(width, ff_part)
+    w_up = got_gu[:, 1].reshape(width, ff_part)
+    w_down = got_down.reshape(ff_part, width)
+    w_out = got_out.transpose(1, 0, 2, 3).reshape(HEAD_DIM, width)
+    gain_tiles = small_exchange(as_tile(norm_gains.astype(bf16).astype(f32).reshape(-1)), reps, count, False, 2)
+    gains = gain_tiles.reshape(total, -1)[:, : d_rows * 4].reshape(width, 4)
+
+    all_tokens = ring_gather(tokens, count, 3)
+    normed_in = rms_norm(all_tokens.astype(f32), gains[:, 0]).astype(bf16)
+    projected = jnp.dot(normed_in, w_in, preferred_element_type=f32)
+    half = HEAD_DIM // 2
+    position = jnp.arange(seq_len, dtype=jnp.int32)
+    freq = 10000.0 ** (-(jnp.arange(half, dtype=f32) * 2.0 / HEAD_DIM))
+    angle = position.astype(f32)[:, None] * freq[None, :]
+    cosine, sine = jnp.cos(angle), jnp.sin(angle)
+    query_scale = HEAD_DIM ** (-0.5)
+    queries = (turn(projected[:, :HEAD_DIM], cosine, sine) * query_scale).astype(bf16)
+    keys = turn(projected[:, HEAD_DIM : 2 * HEAD_DIM], cosine, sine).astype(bf16)
+    values = projected[:, 2 * HEAD_DIM :].astype(bf16)
+    starts = lax.dynamic_slice_in_dim(piece_starts, rep, 1, 0)[0]
+    inside = (position[:, None] >= starts[None, :]) & (position[:, None] < starts[None, :] + PIC)
+    tag = jnp.sum(inside.astype(jnp.int32) * (jnp.arange(starts.shape[0], dtype=jnp.int32)[None, :] + 1), axis=1)
+    visible = (position[None, :] <= position[:, None]) | ((tag[:, None] == tag[None, :]) & (tag[:, None] > 0))
+    raw = lax.dot_general(queries, keys, (((1,), (1,)), ((), ())), preferred_element_type=f32)
+    bent = jnp.tanh(raw / 50.0)
+    masked = jnp.where(visible, 50.0 * bent, -1e30)
+    top_score = jnp.max(masked, axis=-1, keepdims=True)
+    expo = jnp.exp(masked - top_score)
+    probs = expo / jnp.sum(expo, axis=-1, keepdims=True)
+    probs_low = probs.astype(bf16)
+    attended = jnp.dot(probs_low, values, preferred_element_type=f32).astype(bf16)
+    attn_proj = ring_reduce(jnp.dot(attended, w_out, preferred_element_type=f32).astype(bf16), count, 4)
+
+    residual = tokens.astype(f32)
+    d_out = cotangent.astype(f32)
+    middle = residual + rms_norm(attn_proj, gains[:, 1])
+    normed_mid = ring_gather(rms_norm(middle, gains[:, 2]).astype(bf16), count, 5)
+    gate_lin = jnp.dot(normed_mid, w_gate, preferred_element_type=f32)
+    up_lin = jnp.dot(normed_mid, w_up, preferred_element_type=f32)
+    hidden = geglu(gate_lin, up_lin).astype(bf16)
+    ffn_proj = ring_reduce(jnp.dot(hidden, w_down, preferred_element_type=f32).astype(bf16), count, 6)
+    layer_out = (middle + rms_norm(ffn_proj, gains[:, 3])).astype(bf16)
+    d_ffn, d_gain3 = norm_back(ffn_proj, gains[:, 3], d_out)
+    d_ffn = ring_gather(d_ffn.astype(bf16), count, 7)
+    d_hidden = back_dot(d_ffn, w_down)
+    _, glu_back = jax.vjp(geglu, gate_lin, up_lin)
+    d_gate, d_up = glu_back(d_hidden)
+    d_gate, d_up = d_gate.astype(bf16), d_up.astype(bf16)
+    d_mid_in = ring_reduce((back_dot(d_gate, w_gate) + back_dot(d_up, w_up)).astype(bf16), count, 8)
+    part_down = dot_tn(hidden, d_ffn).astype(bf16).reshape(reps, 3, ff_block // 3, width)
+    part_gate = dot_tn(normed_mid, d_gate).astype(bf16).reshape(reps, count, d_rows, ff_part)
+    part_up = dot_tn(normed_mid, d_up).astype(bf16).reshape(reps, count, d_rows, ff_part)
+    sum_gu, grad_down = return_grads(
+        reps, count, None, jnp.concatenate([part_gate, part_up], axis=2), part_down, 9
+    )
+    grad_down = grad_down.reshape(ff_block, width)
+
+    def join_ff(parts):
+        return parts.reshape(count, d_rows, reps, ff_block).transpose(1, 2, 0, 3).reshape(d_rows, ff).astype(f32)
+
+    grad_gate, grad_up = join_ff(sum_gu[:, :d_rows]), join_ff(sum_gu[:, d_rows:])
+    d_mid_part, d_gain2 = norm_back(middle, gains[:, 2], d_mid_in)
+    d_middle = d_out + d_mid_part
+    d_attn, d_gain1 = norm_back(attn_proj, gains[:, 1], d_middle)
+    d_attn = ring_gather(d_attn.astype(bf16), count, 10)
+    d_attended = back_dot(d_attn, w_out).astype(bf16)
+    d_probs = back_dot(d_attended, values)
+    d_values = dot_tn(probs_low, d_attended)
+    d_scores = (
+        probs * (d_probs - jnp.sum(probs * d_probs, axis=-1, keepdims=True)) * (1.0 - bent * bent)
+    ).astype(bf16)
+    d_queries = jnp.dot(d_scores, keys, preferred_element_type=f32)
+    d_keys = dot_tn(d_scores, queries)
+    d_projected = jnp.concatenate(
+        [turn(d_queries, cosine, -sine) * query_scale, turn(d_keys, cosine, -sine), d_values], axis=1
+    ).astype(bf16)
+    d_normed_in = ring_reduce(back_dot(d_projected, w_in).astype(bf16), count, 11)
+    d_input_part, d_gain0 = norm_back(residual, gains[:, 0], d_normed_in)
+    input_grad = d_middle + d_input_part
+    part_in = dot_tn(normed_in, d_projected).astype(bf16).reshape(reps, count, d_rows, 3 * HEAD_DIM)
+    part_out = (
+        dot_tn(attended, d_attn).astype(bf16).reshape(per_head, reps, piece, width).transpose(1, 0, 2, 3)
+    )
+    sum_in, sum_out = return_grads(reps, count, per_head, part_in, part_out, 12)
+    sum_in = sum_in.astype(f32)
+    grad_q = sum_in[:, :, :HEAD_DIM].transpose(1, 0, 2).reshape(d_rows, q_width)
+
+    def join_kv(parts):
+        return parts.reshape(KV_HEADS, group, d_rows, HEAD_DIM).sum(axis=1).transpose(1, 0, 2).reshape(d_rows, k_width)
+
+    grad_inproj = jnp.concatenate(
+        [grad_q, join_kv(sum_in[:, :, HEAD_DIM : 2 * HEAD_DIM]), join_kv(sum_in[:, :, 2 * HEAD_DIM :])], axis=1
+    )
+    grad_outproj = sum_out.reshape(o_rows, width).astype(f32)
+    gain_grad = jnp.stack([d_gain0, d_gain1, d_gain2, d_gain3], axis=1).reshape(total, d_rows * 4)
+    gain_sum = jnp.sum(small_exchange(as_tile(gain_grad), reps, count, True, 13), axis=0)
+    grad_gains = gain_sum.reshape(-1)[: d_rows * 4].reshape(d_rows, 4)
+
+    masters = (inproj, outproj, ffn_gate, ffn_up, ffn_down, norm_gains)
+    gradients = (grad_inproj, grad_outproj, grad_gate, grad_up, grad_down, grad_gains)
+    firsts = (mean_inproj, mean_outproj, mean_gate, mean_up, mean_down, mean_gains)
+    seconds = (square_inproj, square_outproj, square_gate, square_up, square_down, square_gains)
+    results = [lamb_local(*item) for item in zip(masters, gradients, firsts, seconds)]
+    sums = jnp.stack(
+        [jnp.sum(master * master) for master in masters] + [jnp.sum(item[2] * item[2]) for item in results]
+    )
+    totals = jnp.sum(small_exchange(as_tile(sums), reps, count, False, 14), axis=0)
+    totals = totals.reshape(-1)[:12].reshape(2, 6)
+    counts = jnp.array([float(master.size * total) for master in masters], f32)
+    norm_table = jnp.sqrt(totals / counts[None, :] + 1e-06)
+    fresh = [
+        masters[index] - 0.3 * norm_table[0, index] / norm_table[1, index] * results[index][2]
+        for index in range(6)
+    ]
+    return (
+        layer_out,
+        input_grad,
+        *gradients,
+        *[item[0] for item in results],
+        *[item[1] for item in results],
+        *fresh,
+        norm_table,
+    )
+
+
+def fits(mesh, shapes):
+    reps, count = mesh.shape["rep"], mesh.shape["shard"]
+    total = reps * count
+    tokens, piece_starts, outproj, ffn_gate = shapes
+    o_rows = outproj[0] // total
+    return (
+        reps == 4
+        and count == HEADS
+        and piece_starts[0] == reps
+        and tokens[0] % (total * UNITS * 16) == 0
+        and HEAD_DIM % o_rows == 0
+        and o_rows % (16 * reps) == 0
+        and HEAD_DIM // o_rows == total // HEADS
+        and ffn_gate[1] % (total * 96) == 0
+    )
+
+
 def solution(mesh):
-    return jax.shard_map(
-        per_device,
-        mesh=mesh,
-        in_specs=(
-            P(("rep", "shard"), None),
-            P(("rep", "shard"), None),
-            P(),
-            P(("rep", "shard"), None),
-            P(("rep", "shard"), None),
-            P(("rep", "shard"), None),
-            P(("rep", "shard"), None),
-            P(("rep", "shard"), None),
-            P(("rep", "shard"), None),
-            P(("rep", "shard"), None),
-            P(("rep", "shard"), None),
-            P(("rep", "shard"), None),
-            P(("rep", "shard"), None),
-            P(("rep", "shard"), None),
-            P(("rep", "shard"), None),
-            P(("rep", "shard"), None),
-            P(("rep", "shard"), None),
-            P(("rep", "shard"), None),
-            P(("rep", "shard"), None),
-            P(("rep", "shard"), None),
-            P(("rep", "shard"), None),
-        ),
-        out_specs=(
-            P(("rep", "shard"), None),
-            P(("rep", "shard"), None),
-            P(("rep", "shard"), None),
-            P(("rep", "shard"), None),
-            P(("rep", "shard"), None),
-            P(("rep", "shard"), None),
-            P(("rep", "shard"), None),
-            P(("rep", "shard"), None),
-            P(("rep", "shard"), None),
-            P(("rep", "shard"), None),
-            P(("rep", "shard"), None),
-            P(("rep", "shard"), None),
-            P(("rep", "shard"), None),
-            P(("rep", "shard"), None),
-            P(("rep", "shard"), None),
-            P(("rep", "shard"), None),
-            P(("rep", "shard"), None),
-            P(("rep", "shard"), None),
-            P(("rep", "shard"), None),
-            P(("rep", "shard"), None),
-            P(("rep", "shard"), None),
-            P(("rep", "shard"), None),
-            P(("rep", "shard"), None),
-            P(("rep", "shard"), None),
-            P(("rep", "shard"), None),
-            P(("rep", "shard"), None),
-            P(),
-        ),
-        check_vma=False,
-    )
+    split = P(("rep", "shard"), None)
+
+    def step(*args):
+        shapes = args[0].shape, args[2].shape, args[4].shape, args[5].shape
+        body = split_device if fits(mesh, shapes) else per_device
+        return jax.shard_map(
+            body,
+            mesh=mesh,
+            in_specs=(split, split, P()) + (split,) * 18,
+            out_specs=(split,) * 26 + (P(),),
+            check_vma=False,
+        )(*args)
+
+    return step

time: 3680 us -> 1050 us (0.29)
  waiting for transfers between devices: 3140 us -> 0 us
  Pallas kernels: 0 us -> 722 us
  blocking collectives: 149 us -> 0 us
  matrix products: 243 us -> 117 us
  local copies, waits for them, and re-layouts: 32.4 us -> 86.7 us
    unnamed x23 -> x0, waiting for transfers between devices: 1280 us -> none
    all_gather x15 -> x0, waiting for transfers between devices: 1180 us -> none  [the longest x1 233 us: per_device(): lax.all_gather(ffn_gate.astype(bf16), ('rep', 'shard'), axis=0, tiled=True)]
    pallas_call x0 -> x14, Pallas kernels: none -> 722 us  [the longest x4 201 us: ring_gather(): pl.pallas_call(functools.partial(ring_gather_kernel, count), out_shape=ja...]
    reduce_scatter x4 -> x0, waiting for transfers between devices: 680 us -> none  [the longest x1 346 us: per_device(): lax.psum_scatter(part_down, 'shard', scatter_dimension=0, tiled=True)]
    dot_general x15, matrix products: 156 us -> 69.3 us  [the longest x7 29.6 us: dot_tn(): lax.dot_general(left, right, (((0,), (0,)), ((), ())), preferred_element_...]
    all_gather x1 -> x0, blocking collectives: 70.1 us -> none  [per_device(): lax.all_gather(norm_gains.astype(bf16), ('rep', 'shard'), axis=0, tiled=T...]
    dot_general x5 -> x6, matrix products: 87.2 us -> 47.7 us  [back_dot(): lax.dot_general(gradient, weight, (((1,), (1,)), ((), ())), preferred_ele...]
    psum x1 -> x0, blocking collectives: 39.3 us -> none  [per_device(): totals = lax.psum(jnp.stack([weight_sums, step_sums]), ('rep', 'shard'))]
  transfers between devices with their start and end apart: 21 -> 0, of which waited for: 21 -> 0; matrix products, arithmetic and copies ran while one was open for 5% -> 0% of each run, Pallas kernels for 0% -> 0%
where the time goes in v1:
time: 1050 us
  Pallas kernels  722 us (69%)
  matrix products  117 us (11%)
  other arithmetic  111 us (11%)
  local copies, waits for them, and re-layouts  86.7 us (8%)
  between operations  10.5 us (1%)
    pallas_call x4, Pallas kernels, ring_gather(): pl.pallas_call(functools.partial(ring_gather_kernel, count), out_shape=ja...  201 us
    pallas_call x4, Pallas kernels, ring_reduce(): pl.pallas_call(functools.partial(ring_reduce_kernel, count), out_shape=ja...  200 us
    pallas_call x2, Pallas kernels, return_grads(): pl.pallas_call(functools.partial(grads_kernel, reps, count, full), out_sh...  148 us
    pallas_call x1, Pallas kernels, spread_weights(): pl.pallas_call(functools.partial(weights_kernel, reps, count), out_shape=...  133 us
    dot_general x6, matrix products, back_dot(): lax.dot_general(gradient, weight, (((1,), (1,)), ((), ())), preferred_ele...  47.7 us
    pallas_call x3, Pallas kernels, small_exchange(): pl.pallas_call(functools.partial(small_kernel, reps, count, spread), out_...  39.9 us
    dot_general x7, matrix products, dot_tn(): lax.dot_general(left, right, (((0,), (0,)), ((), ())), preferred_element_...  29.6 us
    reduce_sum x6, other arithmetic, split_device(): jnp.sum(item[2] * item[2])  25.3 us

profile of v1, /device:TPU:0, one launch (start us, length us, event | category | flops | bytes accessed | tf_op | source)
XLA Modules:
  0.0 1047.2 jit_solution(12770767529200253908)
XLA Ops:
  5.6 13.1 %small_exchange_2.1 = f32[32,8,128]{2,1,0:T(8,128)} custom-call(f32[8,128]{1,0:T(8,128)} %bitcast_convert_fusion.1.x_ref), custom_call_target="tpu_custom_call" | custom-call | tf_op jit(solution)/shard_map/small_exchange_2/pallas_call | solution.py:856
  24.3 2.5 fusion.31
  27.0 3.9 reshape.359
  30.9 3.5 copy.195
  34.4 4.2 reshape.360
  39.8 3.9 reshape.361
  46.4 3.2 pad_maximum_fusion.1.gu_ref
  50.8 50.8 %ring_gather_3.1 = bf16[8,128,2304]{2,1,0:T(8,128)(2,1)} custom-call(bf16[128,2304]{1,0:T(8,128)(2,1)} %x_ref.1), custom_call_target="tpu_custom_call" | custom-call | tf_op jit(solution)/shard_map/ring_gather_3/pallas_call | solution.py:420
  101.6 3.5 multiply_reduce_fusion
  105.4 3.3 fusion.1
  108.7 3.2 multiply_convert_fusion
  111.9 132.8 %spread_weights.1 = (bf16[4,8,72,768]{3,2,1,0:T(8,128)(2,1)}, bf16[4,8,144,1152]{3,2,1,0:T(8,128)(2,1)}, bf16[4,288,2304]{2,1,0:T(8,128)(2,1)}, bf16[4,4,16,2304]{3,2,1,0:T(8,128)(2,1)}) custom-call(bf16[8,72,768]{2,1,0:T(8,128)(2,1)} %maximum_bitcast_fusion.in_ref, bf16[8,144,1152]{2,1,0:T(8,128)(2,1)} %pad_maximum_fusion.1.gu_ref, ...), custom_call_target="tpu_custom_call" | custom-call | tf_op jit(solution)/shard_map/spread_weights/pallas_call | solution.py:649
  244.8 6.9 fusion.97
  251.9 2.8 fusion.63
  256.5 2.7 fusion.11
  259.8 2.6 fusion.10
  265.3 3.5 convolution_convert_fusion.5
  268.8 51.6 %ring_reduce_4.1 = f32[128,2304]{1,0:T(8,128)} custom-call(bf16[8,128,2304]{2,1,0:T(8,128)(2,1)} %bitcast.143), custom_call_target="tpu_custom_call" | custom-call | tf_op jit(solution)/shard_map/ring_reduce_4/pallas_call | solution.py:485
  325.1 50.5 %ring_gather_5.1 = bf16[8,128,2304]{2,1,0:T(8,128)(2,1)} custom-call(bf16[128,2304]{1,0:T(8,128)(2,1)} %multiply_convert_fusion.5.x_ref), custom_call_target="tpu_custom_call" | custom-call | tf_op jit(solution)/shard_map/ring_gather_5/pallas_call | solution.py:420
  375.6 8.9 fusion.94
  384.5 10.0 fusion.98
  394.5 8.3 multiply_convert_fusion.2
  402.8 7.9 convolution_convert_fusion.4
  410.7 50.0 %ring_reduce_6.1 = f32[128,2304]{1,0:T(8,128)} custom-call(bf16[8,128,2304]{2,1,0:T(8,128)(2,1)} %bitcast.166), custom_call_target="tpu_custom_call" | custom-call | tf_op jit(solution)/shard_map/ring_reduce_6/pallas_call | solution.py:485
  465.4 48.7 %ring_gather_7.1 = bf16[8,128,2304]{2,1,0:T(8,128)(2,1)} custom-call(bf16[128,2304]{1,0:T(8,128)(2,1)} %get-tuple-element.205.x_ref), custom_call_target="tpu_custom_call" | custom-call | tf_op jit(solution)/shard_map/ring_gather_7/pallas_call | solution.py:420
  514.1 16.7 %multiply_convert_fusion.1 = (bf16[1024,1152]{1,0:T(8,128)(2,1)}, bf16[1024,1152]{1,0:T(8,128)(2,1)}) fusion(f32[1024,1152]{1,0:T(8,128)} %copy-done.89, f32[1024,1152]{1,0:T(8,128)} %get-tuple-element.235, bf16[1024,2304]{1,0:T(8,128)(2,1)} %bitcast.173, bf16[1152,2304]{1,0:T(8,128)(2,1)} %bitcast.199), kind=kOutput, calls=%fused_computation.23 | convolution fusion | flops 5464129536 | bytes 24182784 | tf_op jit(solution)/shard_map/dot_general | solution.py:53
  530.8 7.6 convolution_convert_fusion
  538.4 8.9 fusion.99
  547.3 10.1 add_convert_fusion
  557.4 48.1 %ring_reduce_8.1 = f32[128,2304]{1,0:T(8,128)} custom-call(bf16[8,128,2304]{2,1,0:T(8,128)(2,1)} %bitcast.165), custom_call_target="tpu_custom_call" | custom-call | tf_op jit(solution)/shard_map/ring_reduce_8/pallas_call | solution.py:485
  611.7 6.6 convolution_convert_fusion.1
  618.3 6.6 convolution_convert_fusion.2
  624.9 5.2 pad_maximum_fusion.a_part
  630.0 104.1 %return_grads_9.1 = (bf16[8,144,1152]{2,1,0:T(8,128)(2,1)}, f32[3,96,2304]{2,1,0:T(8,128)}) custom-call(bf16[4,8,144,1152]{3,2,1,0:T(8,128)(2,1)} %pad_maximum_fusion.a_part, bf16[4,3,96,2304]{3,2,1,0:T(8,128)(2,1)} %bitcast.150), custom_call_target="tpu_custom_call" | custom-call | tf_op jit(solution)/shard_map/return_grads_9/pallas_call | solution.py:819
  734.1 4.4 slice_convert_fusion
  738.6 3.9 reshape.398
  742.5 3.8 copy.175
  746.3 4.4 reshape.396
  750.7 4.1 reshape.397
  754.8 3.8 copy.174
  758.6 3.4 reshape.395
  762.1 51.3 %ring_gather_10.1 = bf16[8,128,2304]{2,1,0:T(8,128)(2,1)} custom-call(bf16[128,2304]{1,0:T(8,128)(2,1)} %multiply_convert_fusion.4.x_ref), custom_call_target="tpu_custom_call" | custom-call | tf_op jit(solution)/shard_map/ring_gather_10/pallas_call | solution.py:420
  813.4 4.3 convolution_convert_fusion.8
  823.5 3.5 multiply_convert_fusion.3
  829.1 2.4 fusion.57
  831.7 5.8 convolution_convert_fusion.6
  837.5 5.6 convolution_convert_fusion.3
  843.1 50.3 %ring_reduce_11.1 = f32[128,2304]{1,0:T(8,128)} custom-call(bf16[8,128,2304]{2,1,0:T(8,128)(2,1)} %bitcast.164), custom_call_target="tpu_custom_call" | custom-call | tf_op jit(solution)/shard_map/ring_reduce_11/pallas_call | solution.py:485
  893.5 44.1 %return_grads_12.1 = (bf16[8,72,768]{2,1,0:T(8,128)(2,1)}, bf16[4,16,2304]{2,1,0:T(8,128)(2,1)}) custom-call(bf16[4,8,72,768]{3,2,1,0:T(8,128)(2,1)} %bitcast.178, bf16[4,4,16,2304]{3,2,1,0:T(8,128)(2,1)} %bitcast.177), custom_call_target="tpu_custom_call" | custom-call | tf_op jit(solution)/shard_map/return_grads_12/pallas_call | solution.py:819
  940.2 2.7 fusion.26
  947.8 2.2 reshape.386
  951.6 16.7 %small_exchange_13.1 = f32[32,8,128]{2,1,0:T(8,128)} custom-call(f32[32,8,128]{2,1,0:T(8,128)} %bitcast.196), custom_call_target="tpu_custom_call" | custom-call | tf_op jit(solution)/shard_map/small_exchange_13/pallas_call | solution.py:856
  974.3 3.3 multiply_reduce_fusion.17
  977.7 4.6 multiply_reduce_fusion.8
  982.4 5.2 multiply_reduce_fusion.4
  988.4 5.2 multiply_reduce_fusion.3
  994.4 4.9 multiply_reduce_fusion.2
  999.3 7.8 stack.71
  1007.7 10.1 small_exchange_14.1
  1028.3 2.5 multiply_subtract_fusion.4
  1030.8 3.3 multiply_subtract_fusion.3
  1034.2 2.7 multiply_subtract_fusion
  1038.4 2.7 multiply_subtract_fusion.1
  1042.7 2.7 multiply_subtract_fusion.2
  (292 shorter events, 68.7 us)
Async XLA Ops:
  3.5 255.6 %copy-start.63 = (s32[1024]{0:T(1024)}, s32[1024]{0:T(1024)S(1)}, u32[]{:S(2)}) copy-start(s32[1024]{0:T(1024)S(1)} %fusion.75) | copy-start | bytes 12292
  26.9 81.8 %copy-start.60 = (f32[2304]{0:T(1024)}, f32[2304]{0:T(1024)S(1)}, u32[]{:S(2)}) copy-start(f32[2304]{0:T(1024)S(1)} %get-tuple-element.172) | copy-start | bytes 27652
  30.9 7.7 copy-start.8
  101.6 3.8 copy-start
  244.8 7.0 copy-start.49
  244.8 7.1 copy-start.73
  244.8 7.1 copy-start.82
  251.7 10.7 %copy-start.32 = (f32[1024,768]{0,1:T(8,128)}, f32[1024,768]{0,1:T(8,128)S(1)}, u32[]{:S(2)}) copy-start(f32[1024,768]{0,1:T(8,128)S(1)} %fusion.97) | copy-start | bytes 9437188
  251.8 13.4 %copy-start.37 = (bf16[4,4,16,2304]{3,2,1,0:T(8,128)(2,1)}, bf16[4,4,16,2304]{3,2,1,0:T(8,128)(2,1)S(1)}, u32[]{:S(2)}) copy-start(bf16[4,4,16,2304]{3,2,1,0:T(8,128)(2,1)S(1)} %copy.169) | copy-start | bytes 3538948
  256.5 5.9 copy-start.3
  268.8 53.1 %copy-start.30 = (bf16[128,2304]{1,0:T(8,128)(2,1)S(1)}, bf16[128,2304]{1,0:T(8,128)(2,1)}, u32[]{:S(2)}) copy-start(bf16[128,2304]{1,0:T(8,128)(2,1)} %x_ref.1) | copy-start | bytes 1769476
  268.8 53.1 %copy-start.65 = (f32[2304]{0:T(1024)S(1)}, f32[2304]{0:T(1024)}, u32[]{:S(2)}) copy-start(f32[2304]{0:T(1024)} %get-tuple-element.171) | copy-start | bytes 27652
  320.4 3.7 copy-start.66
  384.4 10.0 copy-start.35
  384.5 10.0 copy-start.38
  384.5 18.3 %slice-start.6 = ((s8[5308416]{0:T(1024)(128)(4,1)}), s8[4194304]{0:T(1024)(128)(4,1)S(1)}, s32[]{:S(2)}) async-start(s8[5308416]{0:T(1024)(128)(4,1)} %bitcast.200), calls=%async_computation.6 | async-start | bytes 8388608
  394.5 8.3 copy-start.89
  394.5 8.3 slice-start.7
  402.8 7.9 copy-start.87
  410.7 51.5 %copy-start.34 = (bf16[128,2304]{1,0:T(8,128)(2,1)S(1)}, bf16[128,2304]{1,0:T(8,128)(2,1)}, u32[]{:S(2)}) copy-start(bf16[128,2304]{1,0:T(8,128)(2,1)} %param.23) | copy-start | bytes 1769476
  410.7 51.5 %copy-start.67 = (f32[2304]{0:T(1024)S(1)}, f32[2304]{0:T(1024)}, u32[]{:S(2)}) copy-start(f32[2304]{0:T(1024)} %get-tuple-element.169) | copy-start | bytes 27652
  514.0 16.8 %copy-start.39 = (bf16[8,128,2304]{2,1,0:T(8,128)(2,1)S(1)}, bf16[8,128,2304]{2,1,0:T(8,128)(2,1)}, u32[]{:S(2)}) copy-start(bf16[8,128,2304]{2,1,0:T(8,128)(2,1)} %ring_gather_7.1) | copy-start | bytes 14155780
  514.0 16.7 %copy-start.88 = (bf16[1024,1152]{1,0:T(8,128)(2,1)S(1)}, bf16[1024,1152]{1,0:T(8,128)(2,1)}, u32[]{:S(2)}) copy-start(bf16[1024,1152]{1,0:T(8,128)(2,1)} %copy-done.87) | copy-start | bytes 7077892
  530.8 7.6 copy-start.91
  530.8 16.5 %slice-start = ((s8[5308416]{0:T(1024)(128)(4,1)}), s8[4194304]{0:T(1024)(128)(4,1)S(1)}, s32[]{:S(2)}) async-start(s8[5308416]{0:T(1024)(128)(4,1)} %bitcast.152), calls=%async_computation | async-start | bytes 8388608
  538.4 8.9 slice-start.1
  557.4 53.4 %slice-start.4 = ((s8[4718592]{0:T(1024)(128)(4,1)}), s8[524288]{0:T(1024)(128)(4,1)S(1)}, s32[]{:S(2)}) async-start(s8[4718592]{0:T(1024)(128)(4,1)} %bitcast.169), calls=%async_computation.4 | async-start | bytes 1048576
  611.7 6.6 copy-start.92
  762.1 220.2 %copy-start.16 = (f32[72,9216]{1,0:T(8,128)}, f32[72,9216]{1,0:T(8,128)S(1)}, u32[]{:S(2)}) copy-start(f32[72,9216]{1,0:T(8,128)S(1)} %reshape.395) | copy-start | bytes 7962628
  813.4 4.3 copy-start.40
  813.4 4.3 copy-start.42
  827.1 4.6 slice-start.2
  828.1 3.6 slice-start.3
  831.7 5.9 copy-start.86
  893.5 44.2 %copy-start.31 = (bf16[128,2304]{1,0:T(8,128)(2,1)S(1)}, bf16[128,2304]{1,0:T(8,128)(2,1)}, u32[]{:S(2)}) copy-start(bf16[128,2304]{1,0:T(8,128)(2,1)} %x_ref.1) | copy-start | bytes 1769476
  893.5 44.2 %copy-start.61 = (f32[2304]{0:T(1024)S(1)}, f32[2304]{0:T(1024)}, u32[]{:S(2)}) copy-start(f32[2304]{0:T(1024)} %copy-done.60) | copy-start | bytes 27652
  893.5 44.2 %copy-start.81 = (f32[128]{0:T(128)S(1)}, f32[128]{0:T(128)}, u32[]{:S(2)}) copy-start(f32[128]{0:T(128)} %get-tuple-element.238) | copy-start | bytes 1540
  893.5 46.0 %copy-start.75 = (f32[2304,1]{0,1:T(1,128)S(1)}, f32[2304,1]{0,1:T(1,128)}, u32[]{:S(2)}) copy-start(f32[2304,1]{0,1:T(1,128)} %stack.56) | copy-start | bytes 27652
  893.5 46.0 %copy-start.76 = (f32[2304,1]{0,1:T(1,128)S(1)}, f32[2304,1]{0,1:T(1,128)}, u32[]{:S(2)}) copy-start(f32[2304,1]{0,1:T(1,128)} %stack.55) | copy-start | bytes 27652
  937.7 5.2 copy-start.55
  943.3 28.9 %copy-start.77 = (f32[72,4]{0,1:T(4,128)S(1)}, f32[72,4]{0,1:T(4,128)}, u32[]{:S(2)}) copy-start(f32[72,4]{0,1:T(4,128)} %param.30) | copy-start | bytes 3460
  943.3 28.9 %copy-start.84 = (f32[72,4]{0,1:T(4,128)S(1)}, f32[72,4]{0,1:T(4,128)}, u32[]{:S(2)}) copy-start(f32[72,4]{0,1:T(4,128)} %param.42) | copy-start | bytes 3460
  944.2 30.1 %copy-start.33 = (f32[64,2304]{1,0:T(8,128)S(1)}, f32[64,2304]{1,0:T(8,128)}, u32[]{:S(2)}) copy-start(f32[64,2304]{1,0:T(8,128)} %param.26) | copy-start | bytes 1769476
  944.2 30.1 %copy-start.62 = (bf16[4,16,2304]{2,1,0:T(8,128)(2,1)S(1)}, bf16[4,16,2304]{2,1,0:T(8,128)(2,1)}, u32[]{:S(2)}) copy-start(bf16[4,16,2304]{2,1,0:T(8,128)(2,1)} %get-tuple-element.40) | copy-start | bytes 884740
  972.2 10.1 copy-start.80
  972.2 5.5 copy-start.25
  972.2 5.4 copy-start.50
  974.3 8.0 copy-start.44
  977.7 4.6 copy-start.12
  977.7 4.6 copy-start.43
  982.3 5.2 copy-start.9
  982.3 5.2 copy-start.15
  982.3 5.2 copy-start.45
  982.4 6.0 copy-start.46
  988.3 5.2 copy-start.7
  988.3 5.2 copy-start.17
  988.4 5.2 copy-start.47
  988.4 6.0 copy-start.48
  994.4 24.7 %copy-start.85 = (f32[6]{0:T(128)S(1)}, f32[6]{0:T(128)}, u32[]{:S(2)}) copy-start(f32[6]{0:T(128)} %constant.112) | copy-start | bytes 76
  1019.0 11.7 %copy-start.26 = (f32[72,4096]{1,0:T(8,128)S(1)}, f32[72,4096]{1,0:T(8,128)}, u32[]{:S(2)}) copy-start(f32[72,4096]{1,0:T(8,128)} %param.25) | copy-start | bytes 3538948
  1019.1 15.1 %copy-start.68 = (f32[2,6]{1,0:T(2,128)}, f32[2,6]{1,0:T(2,128)S(1)}, u32[]{:S(2)}) copy-start(f32[2,6]{1,0:T(2,128)S(1)} %fusion.77) | copy-start | bytes 148
  1028.3 5.8 copy-start.24
  1034.1 4.3 copy-start.22
  1038.4 4.3 copy-start.20
  (37 other events, 88.3 us)

commit v2 on v1

--- a/solution.py
+++ b/solution.py
@@ -500,6 +500,292 @@
     )(partial.reshape(count, rows, columns))
 
 
+class Flow:
+    def __init__(self, ring, rows, send, recv):
+        self.ring, self.rows, self.send, self.recv = ring, rows, send, recv
+        self.unit_rows = rows // UNITS
+        self.started = []
+
+    def span(self, slot, unit):
+        return pl.ds(slot * self.rows + unit * self.unit_rows, self.unit_rows)
+
+    def slot(self, way, hops):
+        if hops == 0:
+            return 0
+        return self.ring.count - 1 if hops == self.ring.half else 2 * hops - 1 + way
+
+    def go(self, copy):
+        copy.start()
+        self.started.append(copy)
+
+    def finish(self):
+        for copy in self.started:
+            copy.wait_send()
+
+    def gather_copy(self, buffer, way, hop, unit):
+        return remote(
+            buffer.at[self.span(self.slot(way, hop - 1), unit)],
+            buffer.at[self.span(self.slot(way, hop), unit)],
+            self.send.at[way, hop - 1, unit],
+            self.recv.at[way, hop - 1, unit],
+            self.ring.next[way],
+        )
+
+    def gather(self, buffer, group_work):
+        ring = self.ring
+        for index in range(UNITS):
+            for way in (0, 1):
+                self.go(self.gather_copy(buffer, way, 1, ring.units(way, 1)[index]))
+        queue = list(group_work(0, 1))
+        for hop in range(1, ring.half + 1):
+            length = len(ring.units(0, hop))
+            for index in range(length):
+                for way in (0, 1):
+                    unit = ring.units(way, hop)[index]
+                    self.gather_copy(buffer, way, hop, unit).wait_recv()
+                    if hop < ring.half and unit in ring.units(way, hop + 1):
+                        self.go(self.gather_copy(buffer, way, hop + 1, unit))
+                if queue:
+                    queue.pop(0)()
+            for piece in queue:
+                piece()
+            queue = list(group_work(2 * hop - 1, 2) if hop < ring.half else group_work(ring.count - 1, 1))
+        for piece in queue:
+            piece()
+        self.finish()
+
+    def reduce_copy(self, first, landed, way, step, unit):
+        span = pl.ds(unit * self.unit_rows, self.unit_rows)
+        src = first.at[span] if step == 0 else landed.at[way, step - 1, span]
+        return remote(
+            src,
+            landed.at[way, step, span],
+            self.send.at[way, step, unit],
+            self.recv.at[way, step, unit],
+            self.ring.next[way],
+        )
+
+    def reduce(self, first, landed, partial, group_work, finish):
+        ring = self.ring
+        hops = ring.half
+        f32 = jnp.float32
+        for piece in group_work(ring.count - 1, 1, 0):
+            piece()
+        queue = list(group_work(2 * (hops - 1) - 1, 2, 1))
+        for step in range(hops):
+            order = ring.units(0, hops - step), ring.units(1, hops - step)
+            before = [ring.units(way, hops - step + 1) if step else [] for way in (0, 1)]
+            for index in range(len(order[0])):
+                for way in (0, 1):
+                    unit = order[way][index]
+                    span = pl.ds(unit * self.unit_rows, self.unit_rows)
+                    if step == 0:
+                        first[span, :] = partial[0, pl.ds(unit * self.unit_rows, self.unit_rows), :].astype(first.dtype)
+                    else:
+                        side = 1 - way
+                        block = partial[
+                            step % 2, pl.ds(side * self.rows + unit * self.unit_rows, self.unit_rows), :
+                        ]
+                        if unit in before[way]:
+                            self.reduce_copy(first, landed, way, step - 1, unit).wait_recv()
+                            block = block + landed[way, step - 1, span, :].astype(f32)
+                        landed[way, step - 1, span, :] = block.astype(landed.dtype)
+                    self.go(self.reduce_copy(first, landed, way, step, unit))
+                if queue:
+                    queue.pop(0)()
+            for piece in queue:
+                piece()
+            ahead = hops - step - 2
+            queue = []
+            if step < hops - 1:
+                queue = list(group_work(2 * ahead - 1, 2, step % 2) if ahead > 0 else group_work(0, 1, step % 2))
+        for unit in range(UNITS):
+            span = pl.ds(unit * self.unit_rows, self.unit_rows)
+            total = partial[hops % 2, span, :]
+            for way in (0, 1):
+                self.reduce_copy(first, landed, way, hops - 1, unit).wait_recv()
+                total = total + landed[way, hops - 1, span, :].astype(f32)
+            finish(unit, total)
+        self.finish()
+
+
+def looped(piece, count):
+    def all_of_it():
+        def body(j, carry):
+            piece(j)
+            return carry
+
+        lax.fori_loop(0, count, body, 0)
+
+    return [all_of_it]
+
+
+def gelu_pair(gate):
+    inner = 0.7978845608028654 * (gate + 0.044715 * gate * gate * gate)
+    bend = jnp.tanh(inner)
+    value = 0.5 * gate * (1.0 + bend)
+    slope = 0.5 * (1.0 + bend) + 0.5 * gate * (1.0 - bend * bend) * 0.7978845608028654 * (
+        1.0 + 0.134145 * gate * gate
+    )
+    return value, slope
+
+
+def ffn_kernel(
+    count, attn_ref, tokens_ref, cot_ref, gains_ref, gu_ref, dn_ref,
+    layer_ref, dmid_ref, dattn_ref, gg_ref, h3_ref, hid_ref, dffn_ref, dgu_ref,
+    lin, partial, first, landed, middle, total_ref, s1, r1, s2, r2, s3, r3, s4, r4,
+):
+    f32, bf16 = jnp.float32, jnp.bfloat16
+    ring = Ring(count)
+    rows, width = attn_ref.shape
+    part = hid_ref.shape[1]
+    tile = part // 3
+    wide = width // 3
+    meet(ring.next)
+
+    def gain(index):
+        return 1.0 + gains_ref[index : index + 1, :]
+
+    def scale_of(value):
+        return lax.rsqrt(jnp.mean(value * value, axis=-1, keepdims=True) + 1e-06)
+
+    half = rows // 2
+    halves = [pl.ds(0, half), pl.ds(half, half)]
+    for span in halves:
+        proj = attn_ref[span, :]
+        mid = tokens_ref[span, :].astype(f32) + proj * scale_of(proj) * gain(1)
+        middle[span, :] = mid
+        h3_ref[span, :] = (mid * scale_of(mid) * gain(2)).astype(bf16)
+
+    def lin_work(slot, blocks):
+        at = pl.ds(slot * rows, blocks * rows)
+
+        def piece(j):
+            lo = pl.ds(pl.multiple_of(j * tile, 128), tile)
+            hi = pl.ds(pl.multiple_of(part + j * tile, 128), tile)
+            gate = jnp.dot(h3_ref[at, :], gu_ref[:, lo], preferred_element_type=f32)
+            up = jnp.dot(h3_ref[at, :], gu_ref[:, hi], preferred_element_type=f32)
+            value, slope = gelu_pair(gate)
+            hid_ref[at, lo] = (value * up).astype(bf16)
+            lin[at, lo] = (up * slope).astype(bf16)
+            lin[at, hi] = value.astype(bf16)
+
+        return looped(piece, 3)
+
+    def down_work(slot, blocks, side):
+        at = pl.ds(slot * rows, blocks * rows)
+
+        def piece(j):
+            cols = pl.ds(pl.multiple_of(j * wide, 128), wide)
+            partial[side, pl.ds(0, blocks * rows), cols] = jnp.dot(
+                hid_ref[at, :], dn_ref[:, cols], preferred_element_type=f32
+            )
+
+        return looped(piece, 3)
+
+    def nt(left, right):
+        return lax.dot_general(left, right, (((1,), (1,)), ((), ())), preferred_element_type=f32)
+
+    def back_work(slot, blocks):
+        at = pl.ds(slot * rows, blocks * rows)
+
+        def piece(j):
+            lo = pl.ds(pl.multiple_of(j * tile, 128), tile)
+            hi = pl.ds(pl.multiple_of(part + j * tile, 128), tile)
+            d_hidden = nt(dffn_ref[at, :], dn_ref[lo, :])
+            dgu_ref[at, lo] = (d_hidden * lin[at, lo].astype(f32)).astype(bf16)
+            dgu_ref[at, hi] = (d_hidden * lin[at, hi].astype(f32)).astype(bf16)
+
+        return looped(piece, 3)
+
+    def input_work(slot, blocks, side):
+        at = pl.ds(slot * rows, blocks * rows)
+
+        def piece(j):
+            cols = pl.ds(pl.multiple_of(j * wide, 128), wide)
+            partial[side, pl.ds(0, blocks * rows), cols] = nt(dgu_ref[at, :], gu_ref[cols, :])
+
+        return looped(piece, 3)
+
+    def keep(unit, total):
+        total_ref[pl.ds(unit * (rows // UNITS), rows // UNITS), :] = total
+
+    Flow(ring, rows, s1, r1).gather(h3_ref, lin_work)
+    Flow(ring, rows, s2, r2).reduce(first, landed, partial, down_work, keep)
+
+    def back_norm(value, index, grad):
+        scale = scale_of(value)
+        normed = value * scale
+        weighted = grad * gain(index)
+        inner = jnp.mean(weighted * normed, axis=-1, keepdims=True)
+        return scale * (weighted - normed * inner), jnp.sum(grad * normed, axis=0, keepdims=True)
+
+    gg = jnp.zeros((1, width), f32)
+    for span in halves:
+        proj = total_ref[span, :]
+        scale = scale_of(proj)
+        layer_ref[span, :] = (middle[span, :] + proj * scale * gain(3)).astype(bf16)
+        d_ffn, term = back_norm(proj, 3, cot_ref[span, :].astype(f32))
+        gg += term
+        dffn_ref[span, :] = d_ffn.astype(bf16)
+    gg_ref[3:4, :] = gg
+
+    Flow(ring, rows, s3, r3).gather(dffn_ref, back_work)
+    Flow(ring, rows, s4, r4).reduce(first, landed, partial, input_work, keep)
+
+    gg1 = jnp.zeros((1, width), f32)
+    gg2 = jnp.zeros((1, width), f32)
+    for span in halves:
+        d_mid, term = back_norm(middle[span, :], 2, total_ref[span, :])
+        gg2 += term
+        d_mid = d_mid + cot_ref[span, :].astype(f32)
+        dmid_ref[span, :] = d_mid
+        d_attn, term = back_norm(attn_ref[span, :], 1, d_mid)
+        gg1 += term
+        dattn_ref[span, :] = d_attn.astype(bf16)
+    gg_ref[1:2, :] = gg1
+    gg_ref[2:3, :] = gg2
+    gg_ref[0:1, :] = jnp.zeros((1, width), f32)
+    gg_ref[4:8, :] = jnp.zeros((4, width), f32)
+
+
+def feed_forward(attn_proj, tokens, cotangent, gain_rows, w_gu, w_down, count, collective_id):
+    f32, bf16 = jnp.float32, jnp.bfloat16
+    rows, width = attn_proj.shape
+    part = w_down.shape[0]
+    every = rows * count
+    dma = pltpu.SemaphoreType.DMA
+    shape = jax.ShapeDtypeStruct
+    return pl.pallas_call(
+        functools.partial(ffn_kernel, count),
+        out_shape=[
+            shape((rows, width), bf16),
+            shape((rows, width), f32),
+            shape((rows, width), bf16),
+            shape((8, width), f32),
+            shape((every, width), bf16),
+            shape((every, part), bf16),
+            shape((every, width), bf16),
+            shape((every, 2 * part), bf16),
+        ],
+        in_specs=[pl.BlockSpec(memory_space=VM)] * 6,
+        out_specs=[pl.BlockSpec(memory_space=VM)] * 8,
+        scratch_shapes=[
+            pltpu.VMEM((every, 2 * part), bf16),
+            pltpu.VMEM((2, 2 * rows, width), f32),
+            pltpu.VMEM((rows, width), bf16),
+            pltpu.VMEM((2, count // 2, rows, width), bf16),
+            pltpu.VMEM((rows, width), f32),
+            pltpu.VMEM((rows, width), f32),
+        ]
+        + [dma((2, count // 2, UNITS))] * 8,
+        compiler_params=pltpu.CompilerParams(
+            collective_id=collective_id, has_side_effects=True, vmem_limit_bytes=VMEM_LIMIT
+        ),
+        name="feed_forward",
+    )(attn_proj, tokens, cotangent, gain_rows, w_gu, w_down)
+
+
 def rep_partners(rep):
     return (rep + 2) % 4, rep + 1 - 2 * (rep % 2)
 
@@ -512,40 +798,53 @@
     ]
 
 
-def weights_kernel(
-    reps, count, in_ref, gu_ref, dn_ref, ou_ref, w_in, w_gu, w_dn, w_ou, a_send, a_recv, x_send, x_recv,
-    c_send, c_recv, d_send, d_recv, o_send, o_recv, n_send, n_recv, loc
+def opening_kernel(
+    reps, count, tok_ref, gain_ref, in_ref, gu_ref, dn_ref, ou_ref, tok_out, gain_out, w_in, w_gu, w_dn, w_ou,
+    t_send, t_recv, g_send, g_recv, a_send, a_recv, x_send, x_recv, c_send, c_recv, d_send, d_recv,
+    o_send, o_recv, n_send, n_recv, loc
 ):
-    rep = lax.axis_index("rep")
-    me = lax.axis_index("shard")
+    ring = Ring(count)
+    rep, me = ring.rep, ring.me
     across, beside = rep_partners(rep)
-    meet(everyone(rep, me, reps, count))
+    others = everyone(rep, me, reps, count)
+    meet(others)
     started = []
 
     def go(copy):
         copy.start()
         started.append(copy)
+
+    rows = tok_ref.shape[0] // UNITS
+
+    def hop_copy(way, hop, unit):
+        origin = ring.away(1 - way, hop - 1) if hop > 1 else me
+        span = pl.ds(unit * rows, rows)
+        return remote(
+            tok_ref.at[span] if hop == 1 else tok_out.at[origin, span],
+            tok_out.at[origin, span],
+            t_send.at[way, hop - 1, unit],
+            t_recv.at[way, hop - 1, unit],
+            ring.next[way],
+        )
+
+    def take_hop(hop):
+        for index in range(len(ring.units(0, hop))):
+            for way in (0, 1):
+                unit = ring.units(way, hop)[index]
+                hop_copy(way, hop, unit).wait_recv()
+                if hop < ring.half and unit in ring.units(way, hop + 1):
+                    go(hop_copy(way, hop + 1, unit))
 
     per_head = count * reps // HEADS
     mine = rep * count + me
     target = mine // per_head
     slot = mine % per_head
-    locals_ = []
 
     def ou_copy(j):
         return remote(ou_ref.at[j], w_ou.at[j, slot], o_send.at[j], o_recv.at[slot], (j, target))
 
     def is_self(j):
         return (rep == j) & (me == target)
-
-    for j in range(reps):
-        @pl.when(jnp.logical_not(is_self(j)))
-        def _():
-            ou_copy(j).start()
-
-        @pl.when(is_self(j))
-        def _():
-            pltpu.make_async_copy(ou_ref.at[j], w_ou.at[j, slot], o_recv.at[slot]).start()
 
     pairs = ((in_ref, w_in), (gu_ref, w_gu))
 
@@ -580,10 +879,33 @@
             (beside, me),
         )
 
+    def pass_on(which, k):
+        if k:
+            arrived(which, k).wait_recv()
+        go(forward(which, k, 0))
+        go(forward(which, k, 1))
+
+    def pass_beside(which, k):
+        forward(which, k, 0).wait_recv()
+        go(forward(which, k, 2))
+
     for k in range(1, count):
         go(spread(0, k))
-    go(forward(0, 0, 0))
-    go(forward(0, 0, 1))
+    pass_on(0, 0)
+    for index in range(UNITS):
+        for way in (0, 1):
+            go(hop_copy(way, 1, ring.units(way, 1)[index]))
+    for k, device in enumerate(others):
+        go(remote(gain_ref, gain_out.at[mine], g_send.at[k], g_recv.at[k], device))
+    for j in range(reps):
+        @pl.when(jnp.logical_not(is_self(j)))
+        def _():
+            ou_copy(j).start()
+
+        @pl.when(is_self(j))
+        def _():
+            pltpu.make_async_copy(ou_ref.at[j], w_ou.at[j, slot], o_recv.at[slot]).start()
+
     dn_x = remote(dn_ref, w_dn.at[rep], n_send.at[0], n_recv.at[0], (across, me))
     dn_c = remote(dn_ref, w_dn.at[rep], n_send.at[1], n_recv.at[1], (beside, me))
     dn_d = remote(w_dn.at[across], w_dn.at[across], n_send.at[2], n_recv.at[2], (beside, me))
@@ -591,21 +913,27 @@
     go(dn_c)
     for k in range(1, count):
         go(spread(1, k))
-    go(forward(1, 0, 0))
-    go(forward(1, 0, 1))
+    pass_on(1, 0)
+    locals_ = []
     for index, (src, dst) in enumerate(
-        ((in_ref.at[me], w_in.at[rep, me]), (gu_ref.at[me], w_gu.at[rep, me]), (dn_ref, w_dn.at[rep]))
+        (
+            (in_ref.at[me], w_in.at[rep, me]),
+            (gu_ref.at[me], w_gu.at[rep, me]),
+            (dn_ref, w_dn.at[rep]),
+            (tok_ref, tok_out.at[me]),
+            (gain_ref, gain_out.at[mine]),
+        )
     ):
         copy = pltpu.make_async_copy(src, dst, loc.at[index])
         copy.start()
         locals_.append(copy)
+
     for k in range(1, count):
-        arrived(0, k).wait_recv()
-        go(forward(0, k, 0))
-        go(forward(0, k, 1))
+        pass_on(0, k)
+    take_hop(1)
     for k in range(count):
-        forward(0, k, 0).wait_recv()
-        go(forward(0, k, 2))
+        pass_beside(0, k)
+    take_hop(2)
     for i in range(per_head):
         remote(
             ou_ref.at[0], w_ou.at[rep, i], o_send.at[0], o_recv.at[i], (across, me)
@@ -615,23 +943,28 @@
     ou_d = remote(w_ou.at[across], w_ou.at[across], n_send.at[5], n_recv.at[5], (beside, me))
     go(ou_x)
     go(ou_c)
-    for k in range(1, count):
-        arrived(1, k).wait_recv()
-        go(forward(1, k, 0))
-        go(forward(1, k, 1))
+    for k in range(1, count // 2):
+        pass_on(1, k)
     dn_x.wait_recv()
     go(dn_d)
+    take_hop(3)
+    for k in range(count // 2, count):
+        pass_on(1, k)
+    for hop in range(4, ring.half + 1):
+        take_hop(hop)
     ou_x.wait_recv()
     go(ou_d)
     for k in range(count):
-        forward(1, k, 0).wait_recv()
-        go(forward(1, k, 2))
+        pass_beside(1, k)
     for which in (0, 1):
         for k in range(count):
             forward(which, k, 1).wait_recv()
             forward(which, k, 2).wait_recv()
     for copy in (dn_c, dn_d, ou_c, ou_d):
         copy.wait_recv()
+    for k in range(len(others)):
+        frm = (mine + len(others) - k) % (reps * count)
+        remote(gain_ref, gain_out.at[frm], g_send.at[k], g_recv.at[k], others[k]).wait_recv()
     for copy in started:
         copy.wait_send()
     for j in range(reps):
@@ -642,191 +975,566 @@
         copy.wait()
 
 
-def spread_weights(reps, count, w_in, w_gu, w_dn, w_ou, collective_id):
+def opening(reps, count, tokens, gain_tile, w_in, w_gu, w_dn, w_ou, collective_id):
     dma = pltpu.SemaphoreType.DMA
     per_head = count * reps // HEADS
+    total = reps * count
     low = jnp.bfloat16
+    shape = jax.ShapeDtypeStruct
+    hops = dma((2, count // 2, UNITS))
     return pl.pallas_call(
-        functools.partial(weights_kernel, reps, count),
+        functools.partial(opening_kernel, reps, count),
         out_shape=[
-            jax.ShapeDtypeStruct((reps,) + w_in.shape, low),
-            jax.ShapeDtypeStruct((reps,) + w_gu.shape, low),
-            jax.ShapeDtypeStruct((reps,) + w_dn.shape, low),
-            jax.ShapeDtypeStruct((reps, per_head) + w_ou.shape[1:], low),
+            shape((count,) + tokens.shape, low),
+            shape((total,) + gain_tile.shape, gain_tile.dtype),
+            shape((reps,) + w_in.shape, low),
+            shape((reps,) + w_gu.shape, low),
+            shape((reps,) + w_dn.shape, low),
+            shape((reps, per_head) + w_ou.shape[1:], low),
         ],
-        in_specs=[pl.BlockSpec(memory_space=HB)] * 4,
-        out_specs=[pl.BlockSpec(memory_space=HB)] * 4,
-        scratch_shapes=[dma((2, count))] * 8 + [dma((reps,)), dma((per_head,)), dma((6,)), dma((6,)), dma((3,))],
+        in_specs=[pl.BlockSpec(memory_space=HB)] * 6,
+        out_specs=[pl.BlockSpec(memory_space=HB)] * 6,
+        scratch_shapes=[hops, hops, dma((total - 1,)), dma((total - 1,))]
+        + [dma((2, count))] * 8
+        + [dma((reps,)), dma((per_head,)), dma((6,)), dma((6,)), dma((5,))],
         compiler_params=pltpu.CompilerParams(
             collective_id=collective_id, has_side_effects=True, vmem_limit_bytes=VMEM_LIMIT
         ),
-        name="spread_weights",
-    )(w_in, w_gu, w_dn, w_ou)
-
-
-def rep_sum(part, from_core, to_across, from_across, sums, sems, rep, me, pieces, emit):
-    across, beside = rep_partners(rep)
-    core = rep % 2
-    chip = rep // 2
-    far = 1 - chip
-    c_send, c_recv, x_send, x_recv = sems
-    f32 = jnp.float32
-
-    def core_copy(side, piece):
-        owner_chip = far if side == 0 else chip
+        name="opening",
+    )(tokens, gain_tile, w_in, w_gu, w_dn, w_ou)
+
+
+def cut_kernel(reps, count, in_ref, gate_ref, up_ref, cut_in, cut_gu):
+    low = jnp.bfloat16
+    group = HEADS // KV_HEADS
+    block = gate_ref.shape[1] // (reps * count)
+    part = block * reps
+    for shard in range(count):
+        for index, ref in enumerate((gate_ref, up_ref)):
+            pieces = [ref[:, (r * count + shard) * block : (r * count + shard + 1) * block] for r in range(reps)]
+            cut_gu[shard, :, index * part : (index + 1) * part] = jnp.concatenate(pieces, axis=1).astype(low)
+        heads = shard, HEADS + shard // group, HEADS + KV_HEADS + shard // group
+        for index, head in enumerate(heads):
+            cut_in[shard, :, index * HEAD_DIM : (index + 1) * HEAD_DIM] = in_ref[
+                :, head * HEAD_DIM : (head + 1) * HEAD_DIM
+            ].astype(low)
+
+
+def cut_weights(reps, count, inproj, ffn_gate, ffn_up):
+    rows = inproj.shape[0]
+    shape = jax.ShapeDtypeStruct
+    return pl.pallas_call(
+        functools.partial(cut_kernel, reps, count),
+        out_shape=[
+            shape((count, rows, 3 * HEAD_DIM), jnp.bfloat16),
+            shape((count, rows, 2 * ffn_gate.shape[1] // count), jnp.bfloat16),
+        ],
+        in_specs=[pl.BlockSpec(memory_space=VM)] * 3,
+        out_specs=[pl.BlockSpec(memory_space=VM)] * 2,
+        compiler_params=pltpu.CompilerParams(vmem_limit_bytes=VMEM_LIMIT),
+        name="cut_weights",
+    )(inproj, ffn_gate, ffn_up)
+
+
+def join_kernel(reps, count, sum_ref, gate_ref, up_ref):
+    block = gate_ref.shape[1] // (reps * count)
+    part = block * reps
+    per = 4
+    for index, ref in enumerate((gate_ref, up_ref)):
+        for first in range(0, reps * count, per):
+            pieces = []
+            for b in range(first, first + per):
+                r, shard = b // count, b % count
+                start = index * part + r * block
+                pieces.append(sum_ref[shard, :, start : start + block].astype(jnp.float32))
+            ref[:, first * block : (first + per) * block] = jnp.concatenate(pieces, axis=1)
+
+
+def join_grads(reps, count, sums):
+    rows = sums.shape[1]
+    shape = jax.ShapeDtypeStruct((rows, sums.shape[2] * count // 2), jnp.float32)
+    return pl.pallas_call(
+        functools.partial(join_kernel, reps, count),
+        out_shape=[shape, shape],
+        in_specs=[pl.BlockSpec(memory_space=VM)],
+        out_specs=[pl.BlockSpec(memory_space=VM)] * 2,
+        compiler_params=pltpu.CompilerParams(vmem_limit_bytes=VMEM_LIMIT),
+        name="join_grads",
+    )(sums)
+
+
+class RepSum:
+    def __init__(self, part, from_core, to_across, from_across, sems, rep, me):
+        self.part, self.from_core = part, from_core
+        self.to_across, self.from_across = to_across, from_across
+        self.c_send, self.c_recv, self.x_send, self.x_recv = sems
+        self.across, self.beside = rep_partners(rep)
+        self.rep, self.me = rep, me
+        self.core = rep % 2
+        self.chip = rep // 2
+
+    def core_copy(self, side, piece):
+        chip = 1 - self.chip if side == 0 else self.chip
         return remote(
-            part.at[owner_chip * 2 + 1 - core, piece],
-            from_core.at[side, piece],
-            c_send.at[side, piece],
-            c_recv.at[side, piece],
-            (beside, me),
+            self.part(chip * 2 + 1 - self.core, piece),
+            self.from_core.at[side, piece],
+            self.c_send.at[side, piece],
+            self.c_recv.at[side, piece],
+            (self.beside, self.me),
         )
 
-    def cross_copy(piece):
+    def cross_copy(self, piece):
         return remote(
-            to_across.at[piece], from_across.at[piece], x_send.at[piece], x_recv.at[piece], (across, me)
+            self.to_across.at[piece],
+            self.from_across.at[piece],
+            self.x_send.at[piece],
+            self.x_recv.at[piece],
+            (self.across, self.me),
         )
 
-    for side in (0, 1):
+    def begin(self, pieces):
+        for side in (0, 1):
+            for piece in pieces:
+                self.core_copy(side, piece).start()
+
+    def cross(self, piece):
+        f32 = jnp.float32
+        self.core_copy(0, piece).wait_recv()
+        mine = self.part((1 - self.chip) * 2 + self.core, piece)[...].astype(f32)
+        self.to_across[piece] = (mine + self.from_core[0, piece].astype(f32)).astype(jnp.bfloat16)
+        self.cross_copy(piece).start()
+
+    def total(self, piece):
+        f32 = jnp.float32
+        self.core_copy(1, piece).wait_recv()
+        mine = self.part(self.rep, piece)[...].astype(f32) + self.from_core[1, piece].astype(f32)
+        self.cross_copy(piece).wait_recv()
+        return mine + self.from_across[piece].astype(f32)
+
+    def finish(self, pieces):
         for piece in pieces:
-            core_copy(side, piece).start()
-    for piece in pieces:
-        core_copy(0, piece).wait_recv()
-        to_across[piece] = (
-            part[far * 2 + core, piece].astype(f32) + from_core[0, piece].astype(f32)
-        ).astype(to_across.dtype)
-        cross_copy(piece).start()
-    for piece in pieces:
-        core_copy(1, piece).wait_recv()
-        cross_copy(piece).wait_recv()
-        emit(
-            piece,
-            part[rep, piece].astype(f32)
-            + from_core[1, piece].astype(f32)
-            + from_across[piece].astype(f32),
+            self.core_copy(0, piece).wait_send()
+            self.core_copy(1, piece).wait_send()
+            self.cross_copy(piece).wait_send()
+
+
+class Spread:
+    def __init__(self, blocks, out, send, recv, rep, me, count):
+        self.blocks, self.out, self.send, self.recv = blocks, out, send, recv
+        self.rep, self.me, self.count = rep, me, count
+
+    def copy(self, k):
+        to = (self.me + k) % self.count
+        return remote(
+            self.blocks.at[to], self.out.at[self.me], self.send.at[k], self.recv.at[k], (self.rep, to)
         )
-    for piece in pieces:
-        core_copy(0, piece).wait_send()
-        core_copy(1, piece).wait_send()
-        cross_copy(piece).wait_send()
-
-
-def grads_kernel(
-    reps, count, full, a_part, b_part, a_out, b_out, a_core, a_to, a_from, a_sum, b_core, b_to, b_from, b_sum,
-    ac_s, ac_r, ax_s, ax_r, bc_s, bc_r, bx_s, bx_r, s_send, s_recv, o_send, o_recv
+
+    def arrived(self, k):
+        frm = (self.me + self.count - k) % self.count
+        return remote(
+            self.blocks.at[frm], self.out.at[frm], self.send.at[k], self.recv.at[k], (self.rep, frm)
+        )
+
+    def finish(self):
+        for k in range(1, self.count):
+            self.arrived(k).wait_recv()
+        for k in range(1, self.count):
+            self.copy(k).wait_send()
+
+
+def near_devices(ring):
+    across, beside = rep_partners(ring.rep)
+    return [(ring.rep, (ring.me + k) % ring.count) for k in range(1, ring.count)] + [
+        (across, ring.me),
+        (beside, ring.me),
+    ]
+
+
+class Gather:
+    def __init__(self, ring, block, out, send, recv):
+        self.ring, self.block, self.out, self.send, self.recv = ring, block, out, send, recv
+        self.rows = block.shape[0] // UNITS
+        self.started = []
+
+    def copy(self, way, hop, unit):
+        ring = self.ring
+        origin = ring.away(1 - way, hop - 1) if hop > 1 else ring.me
+        span = pl.ds(unit * self.rows, self.rows)
+        return remote(
+            self.block.at[span] if hop == 1 else self.out.at[origin, span],
+            self.out.at[origin, span],
+            self.send.at[way, hop - 1, unit],
+            self.recv.at[way, hop - 1, unit],
+            ring.next[way],
+        )
+
+    def go(self, copy):
+        copy.start()
+        self.started.append(copy)
+
+    def begin(self):
+        for index in range(UNITS):
+            for way in (0, 1):
+                self.go(self.copy(way, 1, self.ring.units(way, 1)[index]))
+
+    def steps(self):
+        ring = self.ring
+
+        def step(hop, index):
+            for way in (0, 1):
+                unit = ring.units(way, hop)[index]
+                self.copy(way, hop, unit).wait_recv()
+                if hop < ring.half and unit in ring.units(way, hop + 1):
+                    self.go(self.copy(way, hop + 1, unit))
+
+        return [
+            functools.partial(step, hop, index)
+            for hop in range(1, ring.half + 1)
+            for index in range(len(ring.units(0, hop)))
+        ]
+
+    def finish(self):
+        for copy in self.started:
+            copy.wait_send()
+
+
+def tn(left, right):
+    return lax.dot_general(left, right, (((0,), (0,)), ((), ())), preferred_element_type=jnp.float32)
+
+
+DN_PIECES = 3
+
+
+def ffn_grads_kernel(
+    reps, count, dattn_ref, h3_ref, hid_ref, dffn_ref, dgu_ref, all_ref, sum_ref, down_ref,
+    g_part, g_core, g_to, g_from, d_part, d_core, d_to, d_from,
+    t_send, t_recv, gc_s, gc_r, gx_s, gx_r, dc_s, dc_r, dx_s, dx_r, s_send, s_recv, loc
 ):
-    rep = lax.axis_index("rep")
-    me = lax.axis_index("shard")
-    meet(everyone(rep, me, reps, count))
-
-    a_pieces = [(me + k) % count for k in range(1, count)] + [me]
-
-    def a_send(k):
-        to = (me + k) % count
-        return remote(a_sum.at[to], a_out.at[me], s_send.at[k], s_recv.at[k], (rep, to))
-
-    def a_arrived(k):
-        frm = (me + count - k) % count
-        return remote(a_sum.at[frm], a_out.at[frm], s_send.at[k], s_recv.at[k], (rep, frm))
-
-    order = {id(piece): k for k, piece in zip(list(range(1, count)) + [0], a_pieces)}
-
-    def a_emit(piece, total):
-        k = order[id(piece)]
-        if k == 0:
-            a_out[me] = total.astype(a_out.dtype)
+    bf16 = jnp.bfloat16
+    ring = Ring(count)
+    rep, me = ring.rep, ring.me
+    d_rows, columns = sum_ref.shape[1:]
+    part, width = d_part.shape
+    block = part // reps
+    wide = width // 3
+    tall = part // 3
+    meet(near_devices(ring))
+    gather = Gather(ring, dattn_ref, all_ref, t_send, t_recv)
+    gather.begin()
+    own = pltpu.make_async_copy(dattn_ref, all_ref.at[me], loc)
+    own.start()
+
+    def d_at(owner, piece):
+        rows = block // DN_PIECES
+        return d_part.at[pl.ds(owner * block + piece * rows, rows)]
+
+    down = RepSum(d_at, d_core, d_to, d_from, (dc_s, dc_r, dx_s, dx_r), rep, me)
+    gate_up = RepSum(
+        lambda owner, piece: g_part.at[owner, piece], g_core, g_to, g_from, (gc_s, gc_r, gx_s, gx_r), rep, me
+    )
+    spread = Spread(g_from, sum_ref, s_send, s_recv, rep, me, count)
+    d_pieces = list(range(DN_PIECES))
+    g_pieces = [(me + k) % count for k in range(1, count)] + [me]
+
+    def make_down(j):
+        def body(n, carry):
+            cols = pl.ds(pl.multiple_of(n * wide, 128), wide)
+            d_part[j * tall : (j + 1) * tall, cols] = tn(
+                hid_ref[:, j * tall : (j + 1) * tall], dffn_ref[:, cols]
+            ).astype(bf16)
+            return carry
+
+        lax.fori_loop(0, 3, body, 0)
+
+    def make_gate_up(owner):
+        rows = count * d_rows
+        step = columns // 3
+
+        def body(n, carry):
+            cols = pl.ds(pl.multiple_of(n * step, 128), step)
+            made = tn(h3_ref[:, owner * rows : (owner + 1) * rows], dgu_ref[:, cols])
+            g_part[owner, :, :, cols] = made.reshape(count, d_rows, step).astype(bf16)
+            return carry
+
+        lax.fori_loop(0, 3, body, 0)
+
+    work = [functools.partial(make_down, j) for j in range(3)]
+    work.append(lambda: down.begin(d_pieces))
+    work.append(functools.partial(make_gate_up, 0))
+    work.append(lambda: [down.cross(piece) for piece in d_pieces])
+    work += [functools.partial(make_gate_up, owner) for owner in range(1, reps)]
+    work.append(lambda: gate_up.begin(g_pieces))
+    steps = gather.steps()
+    for step in steps:
+        step()
+        if work:
+            work.pop(0)()
+    for piece in work:
+        piece()
+    for piece in g_pieces:
+        gate_up.cross(piece)
+    for piece in d_pieces:
+        rows = block // DN_PIECES
+        down_ref[pl.ds(piece * rows, rows), :] = down.total(piece)
+    for k, piece in enumerate(g_pieces):
+        total = gate_up.total(piece).astype(bf16)
+        if k < count - 1:
+            g_from[piece] = total
+            spread.copy(k + 1).start()
         else:
-            a_sum[piece] = total.astype(a_sum.dtype)
-            a_send(k).start()
-
-    rep_sum(a_part, a_core, a_to, a_from, a_sum, (ac_s, ac_r, ax_s, ax_r), rep, me, a_pieces, a_emit)
-
-    b_pieces = list(range(b_part.shape[1]))
-    if full is None:
-        def b_emit(piece, total):
-            b_out[piece] = total
-    else:
-        def b_send(piece):
-            block = me * full + piece
-            owner = (block // count, block % count)
-            return remote(b_sum.at[piece], b_out.at[rep], o_send.at[piece], o_recv.at[rep], owner)
-
-        def b_self(piece):
-            return me * full + piece == rep * count + me
-
-        def b_emit(piece, total):
-            b_sum[piece] = total.astype(b_sum.dtype)
-
-            @pl.when(jnp.logical_not(b_self(piece)))
-            def _():
-                b_send(piece).start()
-
-            @pl.when(b_self(piece))
-            def _():
-                pltpu.make_async_copy(b_sum.at[piece], b_out.at[rep], o_recv.at[rep]).start()
-
-    rep_sum(b_part, b_core, b_to, b_from, b_sum, (bc_s, bc_r, bx_s, bx_r), rep, me, b_pieces, b_emit)
-
-    for k in range(1, count):
-        a_arrived(k).wait_recv()
-    for k in range(1, count):
-        a_send(k).wait_send()
-    if full is not None:
-        for j in range(reps):
-            remote(
-                b_sum.at[0], b_out.at[j], o_send.at[0], o_recv.at[j], (rep, (me + 1) % count)
-            ).wait_recv()
-        for piece in b_pieces:
-            @pl.when(jnp.logical_not(b_self(piece)))
-            def _():
-                b_send(piece).wait_send()
-
-
-def return_grads(reps, count, full, a_part, b_part, collective_id):
+            sum_ref[me] = total
+    spread.finish()
+    down.finish(d_pieces)
+    gate_up.finish(g_pieces)
+    gather.finish()
+    own.wait()
+
+
+def ffn_grads(reps, count, d_attn, h3, hidden, d_ffn, d_gu, d_rows, collective_id):
     dma = pltpu.SemaphoreType.DMA
     low = jnp.bfloat16
-    a_block = a_part.shape[1:]
-    b_block = b_part.shape[1:]
-    b_count = b_block[0]
-    b_shape = (
-        jax.ShapeDtypeStruct(b_block, jnp.float32)
-        if full is None
-        else jax.ShapeDtypeStruct((reps,) + b_block[1:], low)
-    )
-    b_sum = b_block if full is not None else (1, 16, 128)
-    scratch = [
-        pltpu.VMEM((2,) + a_block, low),
-        pltpu.VMEM(a_block, low),
-        pltpu.VMEM(a_block, low),
-        pltpu.VMEM(a_block, low),
-        pltpu.VMEM((2,) + b_block, low),
-        pltpu.VMEM(b_block, low),
-        pltpu.VMEM(b_block, low),
-        pltpu.VMEM(b_sum, low),
-        dma((2, count)),
-        dma((2, count)),
-        dma((count,)),
-        dma((count,)),
-        dma((2, b_count)),
-        dma((2, b_count)),
-        dma((b_count,)),
-        dma((b_count,)),
-        dma((count,)),
-        dma((count,)),
-        dma((b_count,)),
-        dma((reps,)),
-    ]
+    shape = jax.ShapeDtypeStruct
+    width = d_attn.shape[1]
+    columns = d_gu.shape[1]
+    part = hidden.shape[1]
+    block = part // reps
+    blocks = (count, d_rows, columns)
+    lots = (DN_PIECES, block // DN_PIECES, width)
+    hops = dma((2, count // 2, UNITS))
     return pl.pallas_call(
-        functools.partial(grads_kernel, reps, count, full),
-        out_shape=[jax.ShapeDtypeStruct(a_block, low), b_shape],
-        in_specs=[pl.BlockSpec(memory_space=VM)] * 2,
-        out_specs=[pl.BlockSpec(memory_space=VM)] * 2,
-        scratch_shapes=scratch,
+        functools.partial(ffn_grads_kernel, reps, count),
+        out_shape=[
+            shape((count,) + d_attn.shape, low),
+            shape(blocks, low),
+            shape((block, width), jnp.float32),
+        ],
+        in_specs=[pl.BlockSpec(memory_space=VM)] * 5,
+        out_specs=[pl.BlockSpec(memory_space=HB)] + [pl.BlockSpec(memory_space=VM)] * 2,
+        scratch_shapes=[
+            pltpu.VMEM((reps,) + blocks, low),
+            pltpu.VMEM((2,) + blocks, low),
+            pltpu.VMEM(blocks, low),
+            pltpu.VMEM(blocks, low),
+            pltpu.VMEM((part, width), low),
+            pltpu.VMEM((2,) + lots, low),
+            pltpu.VMEM(lots, low),
+            pltpu.VMEM(lots, low),
+            hops,
+            hops,
+            dma((2, count)),
+            dma((2, count)),
+            dma((count,)),
+            dma((count,)),
+            dma((2, DN_PIECES)),
+            dma((2, DN_PIECES)),
+            dma((DN_PIECES,)),
+            dma((DN_PIECES,)),
+            dma((count,)),
+            dma((count,)),
+            dma,
+        ],
         compiler_params=pltpu.CompilerParams(
             collective_id=collective_id, has_side_effects=True, vmem_limit_bytes=VMEM_LIMIT
         ),
-        name=f"return_grads_{collective_id}",
-    )(a_part, b_part)
+        name="ffn_grads",
+    )(d_attn, h3, hidden, d_ffn, d_gu)
+
+
+def closing_kernel(
+    reps, count, x_ref, tokens_ref, dmid_ref, gains_ref, gg_ref, i_part, o_part, grad_ref, sum_ref, out_ref, gain_ref,
+    held, landed, total_ref, tiles, i_core, i_to, i_from, o_core, o_to, o_from,
+    r_send, r_recv, ic_s, ic_r, ix_s, ix_r, oc_s, oc_r, ox_s, ox_r, s_send, s_recv, p_send, p_recv, g_send, g_recv
+):
+    f32, bf16 = jnp.float32, jnp.bfloat16
+    ring = Ring(count)
+    rep, me = ring.rep, ring.me
+    hops = ring.half
+    here = rep * count + me
+    others = everyone(rep, me, reps, count)
+    rows = grad_ref.shape[0] // UNITS
+    width = grad_ref.shape[1]
+    full = o_part.shape[1]
+    meet(others)
+
+    o_pieces = list(range(full))
+    i_pieces = [(me + k) % count for k in range(1, count)] + [me]
+    ins = RepSum(lambda owner, piece: i_part.at[owner, piece], i_core, i_to, i_from, (ic_s, ic_r, ix_s, ix_r), rep, me)
+    outs = RepSum(lambda owner, piece: o_part.at[owner, piece], o_core, o_to, o_from, (oc_s, oc_r, ox_s, ox_r), rep, me)
+    spread = Spread(i_from, sum_ref, s_send, s_recv, rep, me, count)
+
+    def o_owner(piece):
+        where = me * full + piece
+        return where // count, where % count
+
+    def o_copy(piece):
+        return remote(o_from.at[piece], out_ref.at[rep], p_send.at[piece], p_recv.at[rep], o_owner(piece))
+
+    def o_self(piece):
+        return me * full + piece == here
+
+    def o_finish(piece):
+        total = outs.total(piece).astype(bf16)
+        o_from[piece] = total
+
+        @pl.when(jnp.logical_not(o_self(piece)))
+        def _():
+            o_copy(piece).start()
+
+        @pl.when(o_self(piece))
+        def _():
+            pltpu.make_async_copy(o_from.at[piece], out_ref.at[rep], p_recv.at[rep]).start()
+
+    def i_finish(k):
+        piece = i_pieces[k]
+        total = ins.total(piece).astype(bf16)
+        if k < count - 1:
+            i_from[piece] = total
+            spread.copy(k + 1).start()
+        else:
+            sum_ref[me] = total
+
+    work = [functools.partial(ins.cross, piece) for piece in i_pieces]
+    work += [functools.partial(outs.cross, piece) for piece in o_pieces]
+    work += [functools.partial(i_finish, k) for k in range(count)]
+    work += [functools.partial(o_finish, piece) for piece in o_pieces]
+
+    started = []
+
+    def part(unit):
+        return pl.ds(unit * rows, rows)
+
+    def step_copy(way, step, unit):
+        return remote(
+            held.at[way, step, part(unit)],
+            landed.at[way, step, part(unit)],
+            r_send.at[way, step, unit],
+            r_recv.at[way, step, unit],
+            ring.next[way],
+        )
+
+    for step in range(hops):
+        order = ring.units(0, hops - step), ring.units(1, hops - step)
+        before = [ring.units(way, hops - step + 1) if step else [] for way in (0, 1)]
+        for index in range(len(order[0])):
+            for way in (0, 1):
+                unit = order[way][index]
+                block = x_ref[ring.away(way, hops - step), part(unit), :].astype(f32)
+                if unit in before[way]:
+                    step_copy(way, step - 1, unit).wait_recv()
+                    block += landed[way, step - 1, part(unit), :].astype(f32)
+                held[way, step, part(unit), :] = block.astype(held.dtype)
+                copy = step_copy(way, step, unit)
+                copy.start()
+                started.append(copy)
+            if step == 0 and index == 0:
+                ins.begin(i_pieces)
+                outs.begin(o_pieces)
+            elif step and work:
+                work.pop(0)()
+                if work:
+                    work.pop(0)()
+    gg = jnp.zeros((1, width), f32)
+    gain = 1.0 + gains_ref[0:1, :]
+    for unit in range(UNITS):
+        span = part(unit)
+        total = x_ref[me, span, :].astype(f32)
+        for way in (0, 1):
+            step_copy(way, hops - 1, unit).wait_recv()
+            total += landed[way, hops - 1, span, :].astype(f32)
+        value = tokens_ref[span, :].astype(f32)
+        scale = lax.rsqrt(jnp.mean(value * value, axis=-1, keepdims=True) + 1e-06)
+        normed = value * scale
+        weighted = total * gain
+        inner = jnp.mean(weighted * normed, axis=-1, keepdims=True)
+        grad_ref[span, :] = dmid_ref[span, :] + scale * (weighted - normed * inner)
+        gg += jnp.sum(total * normed, axis=0, keepdims=True)
+    d_rows = sum_ref.shape[1]
+    total_ref[...] = gg_ref[...]
+    total_ref[0:1, :] = gg
+    every = total_ref[...]
+    for owner in range(reps * count):
+        tiles[owner, :, 0:d_rows] = every[:, owner * d_rows : (owner + 1) * d_rows]
+    for k, device in enumerate(others):
+        to = (here + k + 1) % (reps * count)
+        remote(tiles.at[to], gain_ref.at[here], g_send.at[k], g_recv.at[k], device).start()
+    gain_ref[here] = tiles[here]
+    for piece in work:
+        piece()
+    for k in range(len(others)):
+        frm = (here + len(others) - k) % (reps * count)
+        remote(tiles.at[frm], gain_ref.at[frm], g_send.at[k], g_recv.at[k], others[k]).wait_recv()
+    for j in range(reps):
+        remote(
+            o_from.at[0], out_ref.at[j], p_send.at[0], p_recv.at[j], (rep, (me + 1) % count)
+        ).wait_recv()
+    for piece in o_pieces:
+        @pl.when(jnp.logical_not(o_self(piece)))
+        def _():
+            o_copy(piece).wait_send()
+    spread.finish()
+    ins.finish(i_pieces)
+    outs.finish(o_pieces)
+    for k, device in enumerate(others):
+        to = (here + k + 1) % (reps * count)
+        remote(tiles.at[to], gain_ref.at[here], g_send.at[k], g_recv.at[k], device).wait_send()
+    for copy in started:
+        copy.wait_send()
+
+
+def closing(reps, count, partial, tokens, d_middle, gain_rows, gain_terms, part_in, part_out, collective_id):
+    dma = pltpu.SemaphoreType.DMA
+    low, f32 = jnp.bfloat16, jnp.float32
+    shape = jax.ShapeDtypeStruct
+    rows, width = tokens.shape
+    total = reps * count
+    half = count // 2
+    i_block = part_in.shape[1:]
+    o_block = part_out.shape[1:]
+    full = o_block[0]
+    hops = dma((2, half, UNITS))
+    return pl.pallas_call(
+        functools.partial(closing_kernel, reps, count),
+        out_shape=[
+            shape((rows, width), f32),
+            shape(i_block, low),
+            shape((reps,) + o_block[1:], low),
+            shape((total, 8, 128), f32),
+        ],
+        in_specs=[pl.BlockSpec(memory_space=VM)] * 7,
+        out_specs=[pl.BlockSpec(memory_space=VM)] * 4,
+        scratch_shapes=[
+            pltpu.VMEM((2, half, rows, width), low),
+            pltpu.VMEM((2, half, rows, width), low),
+            pltpu.VMEM((8, width), f32),
+            pltpu.VMEM((total, 8, 128), f32),
+            pltpu.VMEM((2,) + i_block, low),
+            pltpu.VMEM(i_block, low),
+            pltpu.VMEM(i_block, low),
+            pltpu.VMEM((2,) + o_block, low),
+            pltpu.VMEM(o_block, low),
+            pltpu.VMEM(o_block, low),
+            hops,
+            hops,
+            dma((2, count)),
+            dma((2, count)),
+            dma((count,)),
+            dma((count,)),
+            dma((2, full)),
+            dma((2, full)),
+            dma((full,)),
+            dma((full,)),
+            dma((count,)),
+            dma((count,)),
+            dma((full,)),
+            dma((reps,)),
+            dma((total - 1,)),
+            dma((total - 1,)),
+        ],
+        compiler_params=pltpu.CompilerParams(
+            collective_id=collective_id, has_side_effects=True, vmem_limit_bytes=VMEM_LIMIT
+        ),
+        name="closing",
+    )(partial.reshape(count, rows, width), tokens, d_middle, gain_rows, gain_terms, part_in, part_out)
 
 
 def small_kernel(reps, count, spread, x_ref, out_ref, send, recv):
@@ -913,32 +1621,20 @@
     per_head = HEAD_DIM // o_rows
     piece = o_rows // reps
 
-    low_in = inproj.astype(bf16)
-    q_cols = low_in[:, :q_width].reshape(d_rows, HEADS, HEAD_DIM)
-    k_cols = jnp.repeat(low_in[:, q_width : q_width + k_width].reshape(d_rows, KV_HEADS, HEAD_DIM), group, axis=1)
-    v_cols = jnp.repeat(low_in[:, q_width + k_width :].reshape(d_rows, KV_HEADS, HEAD_DIM), group, axis=1)
-    cut_in = jnp.concatenate([q_cols, k_cols, v_cols], axis=2).transpose(1, 0, 2)
-
-    def cut_ff(weight):
-        return weight.astype(bf16).reshape(d_rows, reps, count, ff_block).transpose(2, 0, 1, 3).reshape(
-            count, d_rows, ff_part
-        )
-
-    cut_gu = jnp.concatenate([cut_ff(ffn_gate), cut_ff(ffn_up)], axis=1)
+    cut_in, cut_gu = cut_weights(reps, count, inproj, ffn_gate, ffn_up)
     cut_out = outproj.astype(bf16).reshape(reps, piece, width)
-    got_in, got_gu, got_down, got_out = spread_weights(
-        reps, count, cut_in, cut_gu, ffn_down.astype(bf16), cut_out, 1
-    )
+    gain_tile = as_tile(norm_gains.astype(bf16).astype(f32).reshape(-1))
+    all_tokens, gain_tiles, got_in, got_gu, got_down, got_out = opening(
+        reps, count, tokens, gain_tile, cut_in, cut_gu, ffn_down.astype(bf16), cut_out, 1
+    )
+    all_tokens = all_tokens.reshape(seq_len, width)
     w_in = got_in.reshape(width, -1)
-    got_gu = got_gu.reshape(total, 2, d_rows, ff_part)
-    w_gate = got_gu[:, 0].reshape(width, ff_part)
-    w_up = got_gu[:, 1].reshape(width, ff_part)
+    w_gu = got_gu.reshape(width, 2 * ff_part)
     w_down = got_down.reshape(ff_part, width)
     w_out = got_out.transpose(1, 0, 2, 3).reshape(HEAD_DIM, width)
-    gain_tiles = small_exchange(as_tile(norm_gains.astype(bf16).astype(f32).reshape(-1)), reps, count, False, 2)
     gains = gain_tiles.reshape(total, -1)[:, : d_rows * 4].reshape(width, 4)
-
-    all_tokens = ring_gather(tokens, count, 3)
+    gain_rows = gains.T
+
     normed_in = rms_norm(all_tokens.astype(f32), gains[:, 0]).astype(bf16)
     projected = jnp.dot(normed_in, w_in, preferred_element_type=f32)
     half = HEAD_DIM // 2
@@ -964,38 +1660,14 @@
     attended = jnp.dot(probs_low, values, preferred_element_type=f32).astype(bf16)
     attn_proj = ring_reduce(jnp.dot(attended, w_out, preferred_element_type=f32).astype(bf16), count, 4)
 
-    residual = tokens.astype(f32)
-    d_out = cotangent.astype(f32)
-    middle = residual + rms_norm(attn_proj, gains[:, 1])
-    normed_mid = ring_gather(rms_norm(middle, gains[:, 2]).astype(bf16), count, 5)
-    gate_lin = jnp.dot(normed_mid, w_gate, preferred_element_type=f32)
-    up_lin = jnp.dot(normed_mid, w_up, preferred_element_type=f32)
-    hidden = geglu(gate_lin, up_lin).astype(bf16)
-    ffn_proj = ring_reduce(jnp.dot(hidden, w_down, preferred_element_type=f32).astype(bf16), count, 6)
-    layer_out = (middle + rms_norm(ffn_proj, gains[:, 3])).astype(bf16)
-    d_ffn, d_gain3 = norm_back(ffn_proj, gains[:, 3], d_out)
-    d_ffn = ring_gather(d_ffn.astype(bf16), count, 7)
-    d_hidden = back_dot(d_ffn, w_down)
-    _, glu_back = jax.vjp(geglu, gate_lin, up_lin)
-    d_gate, d_up = glu_back(d_hidden)
-    d_gate, d_up = d_gate.astype(bf16), d_up.astype(bf16)
-    d_mid_in = ring_reduce((back_dot(d_gate, w_gate) + back_dot(d_up, w_up)).astype(bf16), count, 8)
-    part_down = dot_tn(hidden, d_ffn).astype(bf16).reshape(reps, 3, ff_block // 3, width)
-    part_gate = dot_tn(normed_mid, d_gate).astype(bf16).reshape(reps, count, d_rows, ff_part)
-    part_up = dot_tn(normed_mid, d_up).astype(bf16).reshape(reps, count, d_rows, ff_part)
-    sum_gu, grad_down = return_grads(
-        reps, count, None, jnp.concatenate([part_gate, part_up], axis=2), part_down, 9
-    )
-    grad_down = grad_down.reshape(ff_block, width)
-
-    def join_ff(parts):
-        return parts.reshape(count, d_rows, reps, ff_block).transpose(1, 2, 0, 3).reshape(d_rows, ff).astype(f32)
-
-    grad_gate, grad_up = join_ff(sum_gu[:, :d_rows]), join_ff(sum_gu[:, d_rows:])
-    d_mid_part, d_gain2 = norm_back(middle, gains[:, 2], d_mid_in)
-    d_middle = d_out + d_mid_part
-    d_attn, d_gain1 = norm_back(attn_proj, gains[:, 1], d_middle)
-    d_attn = ring_gather(d_attn.astype(bf16), count, 10)
+    layer_out, d_middle, d_attn, gain_terms, normed_mid, hidden, d_ffn, d_gu = feed_forward(
+        attn_proj, tokens, cotangent, gain_rows, w_gu, w_down, count, 5
+    )
+    d_attn, sum_gu, grad_down = ffn_grads(
+        reps, count, d_attn, normed_mid, hidden, d_ffn, d_gu, d_rows, 9
+    )
+    d_attn = d_attn.reshape(seq_len, width)
+    grad_gate, grad_up = join_grads(reps, count, sum_gu)
     d_attended = back_dot(d_attn, w_out).astype(bf16)
     d_probs = back_dot(d_attended, values)
     d_values = dot_tn(probs_low, d_attended)
@@ -1007,14 +1679,14 @@
     d_projected = jnp.concatenate(
         [turn(d_queries, cosine, -sine) * query_scale, turn(d_keys, cosine, -sine), d_values], axis=1
     ).astype(bf16)
-    d_normed_in = ring_reduce(back_dot(d_projected, w_in).astype(bf16), count, 11)
-    d_input_part, d_gain0 = norm_back(residual, gains[:, 0], d_normed_in)
-    input_grad = d_middle + d_input_part
     part_in = dot_tn(normed_in, d_projected).astype(bf16).reshape(reps, count, d_rows, 3 * HEAD_DIM)
     part_out = (
         dot_tn(attended, d_attn).astype(bf16).reshape(per_head, reps, piece, width).transpose(1, 0, 2, 3)
     )
-    sum_in, sum_out = return_grads(reps, count, per_head, part_in, part_out, 12)
+    input_grad, sum_in, sum_out, gain_tiles = closing(
+        reps, count, back_dot(d_projected, w_in).astype(bf16), tokens, d_middle, gain_rows, gain_terms,
+        part_in, part_out, 12,
+    )
     sum_in = sum_in.astype(f32)
     grad_q = sum_in[:, :, :HEAD_DIM].transpose(1, 0, 2).reshape(d_rows, q_width)
 
@@ -1025,9 +1697,7 @@
         [grad_q, join_kv(sum_in[:, :, HEAD_DIM : 2 * HEAD_DIM]), join_kv(sum_in[:, :, 2 * HEAD_DIM :])], axis=1
     )
     grad_outproj = sum_out.reshape(o_rows, width).astype(f32)
-    gain_grad = jnp.stack([d_gain0, d_gain1, d_gain2, d_gain3], axis=1).reshape(total, d_rows * 4)
-    gain_sum = jnp.sum(small_exchange(as_tile(gain_grad), reps, count, True, 13), axis=0)
-    grad_gains = gain_sum.reshape(-1)[: d_rows * 4].reshape(d_rows, 4)
+    grad_gains = jnp.sum(gain_tiles, axis=0)[:4, :d_rows].T
 
     masters = (inproj, outproj, ffn_gate, ffn_up, ffn_down, norm_gains)
     gradients = (grad_inproj, grad_outproj, grad_gate, grad_up, grad_down, grad_gains)

time: 1050 us -> 845 us (0.80)
  matrix products: 117 us -> 30.7 us
  local copies, waits for them, and re-layouts: 86.7 us -> 26 us
  other arithmetic: 111 us -> 75.1 us
  Pallas kernels: 722 us -> 695 us
    pallas_call x7 -> x6, Pallas kernels: 482 us -> 608 us  [the longest x1 208 us: feed_forward(): pl.pallas_call(functools.partial(ffn_kernel, count), out_shape=[shape((ro...]
    pallas_call x4 -> x1, Pallas kernels: 200 us -> 77.1 us  [ring_reduce(): pl.pallas_call(functools.partial(ring_reduce_kernel, count), out_shape=ja...]
    dot_general x6 -> x3, matrix products: 47.7 us -> 11.6 us  [back_dot(): lax.dot_general(gradient, weight, (((1,), (1,)), ((), ())), preferred_ele...]
    pallas_call x3 -> x1, Pallas kernels: 39.9 us -> 10 us  [small_exchange(): pl.pallas_call(functools.partial(small_kernel, reps, count, spread), out_...]
    dot_general x3 -> x0, matrix products: 26.1 us -> none  [the longest x1 9.99 us: split_device(): gate_lin = jnp.dot(normed_mid, w_gate, preferred_element_type=f32)]
    convert_element_type x7 -> x1, local copies, waits for them, and re-layouts: 23.6 us -> 0.11 us  [split_device(): gain_tile = as_tile(norm_gains.astype(bf16).astype(f32).reshape(-1))]
    dot_general x7 -> x4, matrix products: 29.6 us -> 8.41 us  [dot_tn(): lax.dot_general(left, right, (((0,), (0,)), ((), ())), preferred_element_...]
    reshape x11 -> x1, local copies, waits for them, and re-layouts: 20.6 us -> 0.11 us  [split_device(): gain_tile = as_tile(norm_gains.astype(bf16).astype(f32).reshape(-1))]
where the time goes in v2:
time: 845 us; the launch traced here: 836 us
  Pallas kernels  695 us (82%)
  other arithmetic  75.1 us (9%)
  matrix products  30.7 us (4%)
  local copies, waits for them, and re-layouts  26 us (3%)
  between operations  9.58 us (1%)
    pallas_call x1, Pallas kernels, feed_forward(): pl.pallas_call(functools.partial(ffn_kernel, count), out_shape=[shape((ro...  208 us
    pallas_call x1, Pallas kernels, opening(): pl.pallas_call(functools.partial(opening_kernel, reps, count), out_shape=...  161 us
    pallas_call x1, Pallas kernels, ffn_grads(): pl.pallas_call(functools.partial(ffn_grads_kernel, reps, count), out_shap...  128 us
    pallas_call x1, Pallas kernels, closing(): pl.pallas_call(functools.partial(closing_kernel, reps, count), out_shape=...  99.6 us
    pallas_call x1, Pallas kernels, ring_reduce(): pl.pallas_call(functools.partial(ring_reduce_kernel, count), out_shape=ja...  77.1 us
    reduce_sum x5, other arithmetic, split_device(): jnp.sum(item[2] * item[2])  24.5 us

profile of v2, /device:TPU:0, one launch (start us, length us, event | category | flops | bytes accessed | tf_op | source)
XLA Modules:
  0.0 836.0 jit_solution(15493832825933440648)
XLA Ops:
  0.7 0.9 dynamic-slice_reduce_fusion
  1.6 1.4 multiply_reduce_fusion.13
  3.3 0.6 bitcast_convert_fusion.1.gain_ref
  3.9 1.8 convert_element_type.111
  5.7 2.9 convert_element_type.110.dn_ref
  8.7 5.5 cut_weights.1
  14.1 161.5 %opening.1 = (bf16[8,128,2304]{2,1,0:T(8,128)(2,1)}, f32[32,8,128]{2,1,0:T(8,128)}, bf16[4,8,72,768]{3,2,1,0:T(8,128)(2,1)}, bf16[4,8,72,2304]{3,2,1,0:T(8,128)(...) custom-call(bf16[128,2304]{1,0:T(8,128)(2,1)} %tokens_ref.3, ...), custom_call_target="tpu_custom_call" | custom-call | tf_op jit(solution)/shard_map/opening/pallas_call | solution.py:985
  175.6 0.9 copy.85
  176.5 3.3 multiply_reduce_fusion
  180.6 1.0 copy.73
  181.7 5.7 fusion.1
  187.5 1.1 multiply_convert_fusion
  188.6 0.9 copy-done.38
  189.5 4.0 fusion.70
  193.5 2.6 fusion.38
  196.2 1.6 fusion.62
  197.8 2.7 fusion.4
  200.5 2.7 fusion.3
  203.2 2.0 copy-done
  205.2 0.8 convolution_convert_fusion.6
  206.0 3.5 convolution_convert_fusion.1
  209.5 77.1 %ring_reduce_4.1.attn_ref = f32[128,2304]{1,0:T(8,128)} custom-call(bf16[8,128,2304]{2,1,0:T(8,128)(2,1)} %bitcast.89), custom_call_target="tpu_custom_call" | custom-call | tf_op jit(solution)/shard_map/ring_reduce_4/pallas_call | solution.py:485
  286.6 208.5 %feed_forward.1 = (bf16[128,2304]{1,0:T(8,128)(2,1)}, f32[128,2304]{1,0:T(8,128)}, bf16[128,2304]{1,0:T(8,128)(2,1)}, f32[8,2304]{1,0:T(8,128)}, bf16[1024,2304]...) custom-call(f32[128,2304]{1,0:T(8,128)} %ring_reduce_4.1.attn_ref, ...), custom_call_target="tpu_custom_call" | custom-call | tf_op jit(solution)/shard_map/feed_forward/pallas_call | solution.py:759
  495.1 127.7 %ffn_grads.1 = (bf16[8,128,2304]{2,1,0:T(8,128)(2,1)}, bf16[8,72,2304]{2,1,0:T(8,128)(2,1)}, f32[288,2304]{1,0:T(8,128)}) custom-call(bf16[128,2304]{1,0:T(8,128)(2,1)} %get-tuple-element.61.dattn_ref, bf16[1024,2304]{1,0:T(8,128)(2,1)} %get-tuple-element.62.h3_ref, bf16[1024,1152]{1,0:T(8,128)(2,1)} %get-tuple-element.63.hid_ref, ...), custom_call_target="tpu_custom_call" | custom-call | tf_op jit(solution)/shard_map/ffn_grads/pallas_call | solution.py:1304
  622.8 3.9 convolution_convert_fusion.4
  626.8 1.4 convolution_convert_fusion.3
  628.2 1.1 copy.84
  629.3 0.8 convolution_convert_fusion.5
  630.1 2.2 multiply_reduce_fusion.1
  632.6 3.4 multiply_convert_fusion.1
  636.1 0.8 fusion.47
  636.9 0.7 fusion.44
  637.6 2.9 fusion.32
  640.6 5.4 convolution_convert_fusion.2
  646.0 5.5 convolution_convert_fusion
  651.5 99.6 %closing.1 = (f32[128,2304]{1,0:T(8,128)}, bf16[8,72,768]{2,1,0:T(8,128)(2,1)}, bf16[4,16,2304]{2,1,0:T(8,128)(2,1)}, f32[32,8,128]{2,1,0:T(8,128)}) custom-call(bf16[8,128,2304]{2,1,0:T(8,128)(2,1)} %bitcast.97, bf16[128,2304]{1,0:T(8,128)(2,1)} %tokens_ref.3, f32[128,2304]{1,0:T(8,128)} %get-tuple-element.67.dmid_ref, f32[4,2304]{1,0:T(4,128)} %bitcast.109, ...), custom_call_target="tpu_custom_call" | custom-call | tf_op jit(solution)/shard_map/closing/pallas_call | solution.py:1495
  751.2 0.9 reduce_sum.186
  752.1 1.2 multiply_reduce_fusion.12
  753.3 1.3 convert_element_type.128
  755.1 0.9 copy-done.18
  756.3 2.0 multiply_reduce_fusion.10
  758.3 2.8 multiply_reduce_fusion.8
  761.7 0.8 copy-done.7
  762.5 4.9 multiply_reduce_fusion.2
  767.4 4.8 join_grads.1
  772.2 13.6 %multiply_reduce_fusion.3 = (f32[]{:T(128)}, f32[]{:T(128)}, f32[72,9216]{1,0:T(8,128)}, f32[72,9216]{1,0:T(8,128)}, f32[]{:T(128)}, /*index=5*/f32[]{:T(128)}, f32[72,9216]{1,0:T(8,128)}, f32[72,9216]{1,0:T(8,128)}) fusion(f32[72,9216]{1,0:T(8,128)} %up_ref.1, f32[72,9216]{1,0:T(8,128)} %get-tuple-element.173, f32[72,9216]{1,0:T(8,128)} %param.40, ...), kind=kLoop, calls=%fused_computation.32 | loop fusion | flops 18579452 | bytes 31850512 | tf_op jit(solution)/shard_map/reduce_sum | solution.py:1708
  785.8 7.8 stack.51
  793.6 0.6 pad_bitcast_fusion.x_ref
  794.2 10.0 %small_exchange_14.1 = f32[32,8,128]{2,1,0:T(8,128)} custom-call(f32[8,128]{1,0:T(8,128)} %pad_bitcast_fusion.x_ref), custom_call_target="tpu_custom_call" | custom-call | tf_op jit(solution)/shard_map/small_exchange_14/pallas_call | solution.py:1564
  804.2 0.9 reduce_sum.199
  805.3 0.7 fusion.69
  814.0 0.6 multiply_subtract_fusion.5
  814.6 2.5 multiply_subtract_fusion.4
  817.1 3.3 multiply_subtract_fusion.3
  820.5 2.7 multiply_subtract_fusion
  823.7 1.0 copy-done.14
  824.7 2.7 multiply_subtract_fusion.1
  827.5 0.7 copy-done.15
  828.1 0.9 copy-done.16
  829.0 2.8 multiply_subtract_fusion.2
  831.9 0.8 copy.91
  832.7 1.0 copy.92
  833.7 0.6 copy-done.8
  834.3 1.5 copy.93
  (106 shorter events, 3.6 us)
Async XLA Ops:
  179.9 1.8 copy-start.23
  181.7 5.8 slice-start
  181.7 5.8 slice-start.1
  187.5 2.0 copy-start.38
  193.5 9.7 %copy-start.17 = (f32[1024,768]{0,1:T(8,128)}, f32[1024,768]{0,1:T(8,128)S(1)}, u32[]{:S(2)}) copy-start(f32[1024,768]{0,1:T(8,128)S(1)} %fusion.70) | copy-start | bytes 9437188
  196.2 1.7 copy-start.29
  197.8 5.4 copy-start.2
  203.2 2.0 copy-start
  622.8 3.9 copy-start.37
  626.7 2.6 copy-start.1
  630.1 2.5 copy-start.3
  632.6 3.4 copy-start.30
  636.1 4.5 slice-start.2
  636.8 3.7 slice-start.3
  640.6 5.4 copy-start.39
  651.5 100.6 %copy-start.33 = (f32[72,4]{0,1:T(4,128)S(1)}, f32[72,4]{0,1:T(4,128)}, u32[]{:S(2)}) copy-start(f32[72,4]{0,1:T(4,128)} %param.30) | copy-start | bytes 3460
  651.5 100.6 %copy-start.34 = (f32[72,4]{0,1:T(4,128)S(1)}, f32[72,4]{0,1:T(4,128)}, u32[]{:S(2)}) copy-start(f32[72,4]{0,1:T(4,128)} %param.42) | copy-start | bytes 3460
  651.5 100.6 %copy-start.35 = (f32[72,4]{0,1:T(4,128)S(1)}, f32[72,4]{0,1:T(4,128)}, u32[]{:S(2)}) copy-start(f32[72,4]{0,1:T(4,128)} %param.36) | copy-start | bytes 3460
  754.7 3.7 copy-start.25
  754.8 1.1 copy-start.18
  754.8 1.3 copy-start.27
  754.8 1.5 copy-start.28
  754.8 1.5 copy-start.31
  754.9 3.4 copy-start.24
  755.0 3.3 copy-start.11
  756.3 4.8 copy-start.21
  756.3 4.8 copy-start.19
  756.3 4.8 copy-start.20
  758.3 3.4 copy-start.4
  758.3 4.1 copy-start.7
  772.2 33.0 %copy-start.36 = (f32[6]{0:T(128)S(1)}, f32[6]{0:T(128)}, u32[]{:S(2)}) copy-start(f32[6]{0:T(128)} %constant.90) | copy-start | bytes 76
  805.2 11.8 %copy-start.12 = (f32[72,4096]{1,0:T(8,128)S(1)}, f32[72,4096]{1,0:T(8,128)}, u32[]{:S(2)}) copy-start(f32[72,4096]{1,0:T(8,128)} %in_ref.1) | copy-start | bytes 3538948
  805.3 15.2 %copy-start.32 = (f32[2,6]{1,0:T(2,128)}, f32[2,6]{1,0:T(2,128)S(1)}, u32[]{:S(2)}) copy-start(f32[2,6]{1,0:T(2,128)S(1)} %fusion.52) | copy-start | bytes 148
  814.6 5.8 copy-start.10
  817.1 3.4 copy-start.9
  820.4 2.8 copy-start.5
  820.4 3.3 copy-start.13
  820.5 4.3 copy-start.14
  824.7 2.7 copy-start.6
  824.7 3.4 copy-start.15
  824.7 4.3 copy-start.16
  829.0 2.8 copy-start.26
  829.0 3.7 copy-start.22
  831.9 2.4 copy-start.8

commit v3 on v2

--- a/solution.py
+++ b/solution.py
@@ -373,75 +373,13 @@
         return order if hop < self.half else order[: UNITS // 2]
 
 
-def ring_gather_kernel(count, x_ref, out_ref, send, recv, local):
-    ring = Ring(count)
-    rows = x_ref.shape[0] // UNITS
+def reduce_on_ring(ring, rows, take, held, landed, send, recv, finish, pause):
+    f32 = jnp.float32
+    hops = ring.half
+    started = []
 
     def part(unit):
-        return pl.ds(unit * rows, rows)
-
-    def hop_copy(way, hop, unit):
-        origin = ring.away(1 - way, hop - 1) if hop > 1 else ring.me
-        src = x_ref.at[part(unit)] if hop == 1 else out_ref.at[origin, part(unit)]
-        return remote(
-            src,
-            out_ref.at[origin, part(unit)],
-            send.at[way, hop - 1, unit],
-            recv.at[way, hop - 1, unit],
-            ring.next[way],
-        )
-
-    meet(ring.next)
-    own = pltpu.make_async_copy(x_ref, out_ref.at[ring.me], local)
-    own.start()
-    started = []
-    for index in range(UNITS):
-        for way in (0, 1):
-            copy = hop_copy(way, 1, ring.units(way, 1)[index])
-            copy.start()
-            started.append(copy)
-    for hop in range(1, ring.half + 1):
-        for index in range(len(ring.units(0, hop))):
-            for way in (0, 1):
-                unit = ring.units(way, hop)[index]
-                hop_copy(way, hop, unit).wait_recv()
-                if hop < ring.half and unit in ring.units(way, hop + 1):
-                    copy = hop_copy(way, hop + 1, unit)
-                    copy.start()
-                    started.append(copy)
-    for copy in started:
-        copy.wait_send()
-    own.wait()
-
-
-def ring_gather(block, count, collective_id):
-    rows, columns = block.shape
-    hops = count // 2
-    gathered = pl.pallas_call(
-        functools.partial(ring_gather_kernel, count),
-        out_shape=jax.ShapeDtypeStruct((count, rows, columns), block.dtype),
-        in_specs=[pl.BlockSpec(memory_space=VM)],
-        out_specs=pl.BlockSpec(memory_space=VM),
-        scratch_shapes=[
-            pltpu.SemaphoreType.DMA((2, hops, UNITS)),
-            pltpu.SemaphoreType.DMA((2, hops, UNITS)),
-            pltpu.SemaphoreType.DMA,
-        ],
-        compiler_params=pltpu.CompilerParams(
-            collective_id=collective_id, has_side_effects=True, vmem_limit_bytes=VMEM_LIMIT
-        ),
-        name=f"ring_gather_{collective_id}",
-    )(block)
-    return gathered.reshape(count * rows, columns)
-
-
-def ring_reduce_kernel(count, x_ref, out_ref, held, landed, send, recv):
-    ring = Ring(count)
-    rows = out_ref.shape[0] // UNITS
-    hops = ring.half
-
-    def part(unit):
-        return pl.ds(unit * rows, rows)
+        return pl.ds(unit * (rows // UNITS), rows // UNITS)
 
     def step_copy(way, step, unit):
         return remote(
@@ -452,52 +390,29 @@
             ring.next[way],
         )
 
-    meet(ring.next)
-    started = []
     for step in range(hops):
         order = ring.units(0, hops - step), ring.units(1, hops - step)
         before = [ring.units(way, hops - step + 1) if step else [] for way in (0, 1)]
         for index in range(len(order[0])):
             for way in (0, 1):
                 unit = order[way][index]
-                block = x_ref[ring.away(way, hops - step), part(unit), :].astype(jnp.float32)
+                block = take(ring.away(way, hops - step), part(unit)).astype(f32)
                 if unit in before[way]:
                     step_copy(way, step - 1, unit).wait_recv()
-                    block += landed[way, step - 1, part(unit), :].astype(jnp.float32)
+                    block += landed[way, step - 1, part(unit), :].astype(f32)
                 held[way, step, part(unit), :] = block.astype(held.dtype)
                 copy = step_copy(way, step, unit)
                 copy.start()
                 started.append(copy)
-    for index in range(UNITS):
-        unit = index
-        total = x_ref[ring.me, part(unit), :].astype(jnp.float32)
+            if step or index == len(order[0]) - 1:
+                pause()
+    for unit in range(UNITS):
+        total = take(ring.me, part(unit)).astype(f32)
         for way in (0, 1):
             step_copy(way, hops - 1, unit).wait_recv()
-            total += landed[way, hops - 1, part(unit), :].astype(jnp.float32)
-        out_ref[part(unit), :] = total
-    for copy in started:
-        copy.wait_send()
-
-
-def ring_reduce(partial, count, collective_id):
-    rows, columns = partial.shape[0] // count, partial.shape[1]
-    hops = count // 2
-    return pl.pallas_call(
-        functools.partial(ring_reduce_kernel, count),
-        out_shape=jax.ShapeDtypeStruct((rows, columns), jnp.float32),
-        in_specs=[pl.BlockSpec(memory_space=VM)],
-        out_specs=pl.BlockSpec(memory_space=VM),
-        scratch_shapes=[
-            pltpu.VMEM((2, hops, rows, columns), jnp.bfloat16),
-            pltpu.VMEM((2, hops, rows, columns), jnp.bfloat16),
-            pltpu.SemaphoreType.DMA((2, hops, UNITS)),
-            pltpu.SemaphoreType.DMA((2, hops, UNITS)),
-        ],
-        compiler_params=pltpu.CompilerParams(
-            collective_id=collective_id, has_side_effects=True, vmem_limit_bytes=VMEM_LIMIT
-        ),
-        name=f"ring_reduce_{collective_id}",
-    )(partial.reshape(count, rows, columns))
+            total += landed[way, hops - 1, part(unit), :].astype(f32)
+        finish(part(unit), total)
+    return started
 
 
 class Flow:
@@ -631,7 +546,7 @@
 
 
 def ffn_kernel(
-    count, attn_ref, tokens_ref, cot_ref, gains_ref, gu_ref, dn_ref,
+    count, attn_ref, tokens_ref, cot_ref, gains_ref, gate_ref, up_ref, dn_ref,
     layer_ref, dmid_ref, dattn_ref, gg_ref, h3_ref, hid_ref, dffn_ref, dgu_ref,
     lin, partial, first, landed, middle, total_ref, s1, r1, s2, r2, s3, r3, s4, r4,
 ):
@@ -663,8 +578,8 @@
         def piece(j):
             lo = pl.ds(pl.multiple_of(j * tile, 128), tile)
             hi = pl.ds(pl.multiple_of(part + j * tile, 128), tile)
-            gate = jnp.dot(h3_ref[at, :], gu_ref[:, lo], preferred_element_type=f32)
-            up = jnp.dot(h3_ref[at, :], gu_ref[:, hi], preferred_element_type=f32)
+            gate = jnp.dot(h3_ref[at, :], gate_ref[:, lo], preferred_element_type=f32)
+            up = jnp.dot(h3_ref[at, :], up_ref[:, lo], preferred_element_type=f32)
             value, slope = gelu_pair(gate)
             hid_ref[at, lo] = (value * up).astype(bf16)
             lin[at, lo] = (up * slope).astype(bf16)
@@ -703,7 +618,9 @@
 
         def piece(j):
             cols = pl.ds(pl.multiple_of(j * wide, 128), wide)
-            partial[side, pl.ds(0, blocks * rows), cols] = nt(dgu_ref[at, :], gu_ref[cols, :])
+            partial[side, pl.ds(0, blocks * rows), cols] = nt(dgu_ref[at, :part], gate_ref[cols, :]) + nt(
+                dgu_ref[at, part:], up_ref[cols, :]
+            )
 
         return looped(piece, 3)
 
@@ -749,7 +666,7 @@
     gg_ref[4:8, :] = jnp.zeros((4, width), f32)
 
 
-def feed_forward(attn_proj, tokens, cotangent, gain_rows, w_gu, w_down, count, collective_id):
+def feed_forward(attn_proj, tokens, cotangent, gain_rows, w_gate, w_up, w_down, count, collective_id):
     f32, bf16 = jnp.float32, jnp.bfloat16
     rows, width = attn_proj.shape
     part = w_down.shape[0]
@@ -768,7 +685,7 @@
             shape((every, width), bf16),
             shape((every, 2 * part), bf16),
         ],
-        in_specs=[pl.BlockSpec(memory_space=VM)] * 6,
+        in_specs=[pl.BlockSpec(memory_space=VM)] * 7,
         out_specs=[pl.BlockSpec(memory_space=VM)] * 8,
         scratch_shapes=[
             pltpu.VMEM((every, 2 * part), bf16),
@@ -783,7 +700,179 @@
             collective_id=collective_id, has_side_effects=True, vmem_limit_bytes=VMEM_LIMIT
         ),
         name="feed_forward",
-    )(attn_proj, tokens, cotangent, gain_rows, w_gu, w_down)
+    )(attn_proj, tokens, cotangent, gain_rows, w_gate, w_up, w_down)
+
+
+def attention_kernel(
+    reps, count, h1_ref, in_ref, wo_ref, cos_ref, sin_ref, tagq_ref, tagk_ref, cut_ref,
+    proj_ref, q_ref, k_ref, v_ref, att_ref, probs_ref, damp_ref, up_ref,
+    part, held, landed, r_send, r_recv, w_sems, loc
+):
+    f32, bf16 = jnp.float32, jnp.bfloat16
+    ring = Ring(count)
+    rows = proj_ref.shape[0]
+    seq_len = h1_ref.shape[0]
+    tall = seq_len // 4
+    half = HEAD_DIM // 2
+    meet(near_devices(ring))
+    weights = Fetch(ring, cut_ref, up_ref, w_sems)
+    weights.begin()
+    own = pltpu.make_async_copy(cut_ref.at[ring.me], up_ref.at[ring.rep, ring.me], loc)
+    own.start()
+
+    def project(i, carry):
+        at = pl.ds(pl.multiple_of(i * tall, 16), tall)
+        flat = jnp.dot(h1_ref[at, :], in_ref[...], preferred_element_type=f32)
+        cosine, sine = cos_ref[at, :], sin_ref[at, :]
+
+        def turned(start):
+            first, second = flat[:, start : start + half], flat[:, start + half : start + HEAD_DIM]
+            return jnp.concatenate([first * cosine - second * sine, second * cosine + first * sine], axis=1)
+
+        q_ref[at, :] = (turned(0) * HEAD_DIM ** (-0.5)).astype(bf16)
+        k_ref[at, :] = turned(HEAD_DIM).astype(bf16)
+        v_ref[at, :] = flat[:, 2 * HEAD_DIM :].astype(bf16)
+        return carry
+
+    lax.fori_loop(0, 4, project, 0)
+
+    def attend(i, carry):
+        at = pl.ds(pl.multiple_of(i * tall, 16), tall)
+        raw = lax.dot_general(q_ref[at, :], k_ref[...], (((1,), (1,)), ((), ())), preferred_element_type=f32)
+        bent = jnp.tanh(raw * (1.0 / 50.0))
+        query_at = i * tall + lax.broadcasted_iota(jnp.int32, (tall, seq_len), 0)
+        key_at = lax.broadcasted_iota(jnp.int32, (tall, seq_len), 1)
+        tag = tagq_ref[at, :]
+        visible = (key_at <= query_at) | ((tag == tagk_ref[...]) & (tag > 0))
+        masked = jnp.where(visible, 50.0 * bent, -1e30)
+        expo = jnp.exp(masked - jnp.max(masked, axis=-1, keepdims=True))
+        probs = expo / jnp.sum(expo, axis=-1, keepdims=True)
+        low = probs.astype(bf16)
+        probs_ref[at, :] = low
+        damp_ref[at, :] = (probs * (1.0 - bent * bent)).astype(bf16)
+        attended = jnp.dot(low, v_ref[...], preferred_element_type=f32).astype(bf16)
+        att_ref[at, :] = attended
+        part[at, :] = jnp.dot(attended, wo_ref[...], preferred_element_type=f32)
+        return carry
+
+    lax.fori_loop(0, 4, attend, 0)
+
+    work = weights.steps()
+
+    def pause():
+        for _ in range(min(2, len(work))):
+            work.pop(0)()
+
+    def finish(span, total):
+        proj_ref[span, :] = total
+
+    def take(shard, span):
+        return part[pl.ds(pl.multiple_of(shard * rows + span.start, 16), span.size), :]
+
+    started = reduce_on_ring(ring, rows, take, held, landed, r_send, r_recv, finish, pause)
+    for piece in work:
+        piece()
+    weights.finish()
+    own.wait()
+    for copy in started:
+        copy.wait_send()
+
+
+def attention(reps, count, normed, w_in, w_out, cosine, sine, tag, cut_up, collective_id):
+    dma = pltpu.SemaphoreType.DMA
+    low, f32 = jnp.bfloat16, jnp.float32
+    shape = jax.ShapeDtypeStruct
+    seq_len, width = normed.shape
+    rows = seq_len // count
+    hops = count // 2
+    head = shape((seq_len, HEAD_DIM), low)
+    square = shape((seq_len, seq_len), low)
+    return pl.pallas_call(
+        functools.partial(attention_kernel, reps, count),
+        out_shape=[
+            shape((rows, width), f32), head, head, head, head, square, square,
+            shape((reps,) + cut_up.shape, low),
+        ],
+        in_specs=[pl.BlockSpec(memory_space=VM)] * 7 + [pl.BlockSpec(memory_space=HB)],
+        out_specs=[pl.BlockSpec(memory_space=VM)] * 7 + [pl.BlockSpec(memory_space=HB)],
+        scratch_shapes=[
+            pltpu.VMEM((seq_len, width), f32),
+            pltpu.VMEM((2, hops, rows, width), low),
+            pltpu.VMEM((2, hops, rows, width), low),
+            dma((2, hops, UNITS)),
+            dma((2, hops, UNITS)),
+            dma((8, count)),
+            dma,
+        ],
+        compiler_params=pltpu.CompilerParams(
+            collective_id=collective_id, has_side_effects=True, vmem_limit_bytes=VMEM_LIMIT
+        ),
+        name="attention",
+    )(normed, w_in, w_out, cosine, sine, tag[:, None], tag[None, :], cut_up)
+
+
+class Fetch:
+    def __init__(self, ring, cut, out, sems):
+        self.ring, self.cut, self.out = ring, cut, out
+        self.rep, self.me, self.count = ring.rep, ring.me, ring.count
+        self.across, self.beside = rep_partners(ring.rep)
+        self.sems = sems
+        self.started = []
+
+    def go(self, copy):
+        copy.start()
+        self.started.append(copy)
+
+    def spread(self, k):
+        to = (self.me + k) % self.count
+        return remote(
+            self.cut.at[to], self.out.at[self.rep, self.me], self.sems.at[0, k], self.sems.at[1, k], (self.rep, to)
+        )
+
+    def arrived(self, k):
+        frm = (self.me + self.count - k) % self.count
+        return remote(
+            self.cut.at[frm], self.out.at[self.rep, frm], self.sems.at[0, k], self.sems.at[1, k], (self.rep, frm)
+        )
+
+    def forward(self, k, hop):
+        frm = (self.me + self.count - k) % self.count
+        rep = self.across if hop == 2 else self.rep
+        block = self.out.at[rep, frm] if k or hop == 2 else self.cut.at[self.me]
+        to = self.across if hop == 0 else self.beside
+        return remote(
+            block,
+            self.out.at[rep, frm],
+            self.sems.at[2 + 2 * hop, k],
+            self.sems.at[3 + 2 * hop, k],
+            (to, self.me),
+        )
+
+    def pass_on(self, k):
+        if k:
+            self.arrived(k).wait_recv()
+        self.go(self.forward(k, 0))
+        self.go(self.forward(k, 1))
+
+    def pass_beside(self, k):
+        self.forward(k, 0).wait_recv()
+        self.go(self.forward(k, 2))
+
+    def begin(self):
+        for k in range(1, self.count):
+            self.go(self.spread(k))
+        self.pass_on(0)
+
+    def steps(self):
+        work = [functools.partial(self.pass_on, k) for k in range(1, self.count)]
+        return work + [functools.partial(self.pass_beside, k) for k in range(self.count)]
+
+    def finish(self):
+        for k in range(self.count):
+            self.forward(k, 1).wait_recv()
+            self.forward(k, 2).wait_recv()
+        for copy in self.started:
+            copy.wait_send()
 
 
 def rep_partners(rep):
@@ -799,14 +888,17 @@
 
 
 def opening_kernel(
-    reps, count, tok_ref, gain_ref, in_ref, gu_ref, dn_ref, ou_ref, tok_out, gain_out, w_in, w_gu, w_dn, w_ou,
-    t_send, t_recv, g_send, g_recv, a_send, a_recv, x_send, x_recv, c_send, c_recv, d_send, d_recv,
-    o_send, o_recv, n_send, n_recv, loc
+    reps, count, tok_ref, gain_ref, in_ref, gate_ref, dn_ref, ou_ref, h1_ref, gains_ref, w_in, w_gate, w_dn, w_ou,
+    tok_all, gain_all, t_send, t_recv, g_send, g_recv, i_sems, u_sems, o_send, o_recv, n_send, n_recv, loc
 ):
+    f32 = jnp.float32
     ring = Ring(count)
     rep, me = ring.rep, ring.me
     across, beside = rep_partners(rep)
     others = everyone(rep, me, reps, count)
+    mine = rep * count + me
+    d_rows = in_ref.shape[1]
+    rows = tok_ref.shape[0]
     meet(others)
     started = []
 
@@ -814,29 +906,16 @@
         copy.start()
         started.append(copy)
 
-    rows = tok_ref.shape[0] // UNITS
-
-    def hop_copy(way, hop, unit):
-        origin = ring.away(1 - way, hop - 1) if hop > 1 else me
-        span = pl.ds(unit * rows, rows)
-        return remote(
-            tok_ref.at[span] if hop == 1 else tok_out.at[origin, span],
-            tok_out.at[origin, span],
-            t_send.at[way, hop - 1, unit],
-            t_recv.at[way, hop - 1, unit],
-            ring.next[way],
-        )
-
-    def take_hop(hop):
-        for index in range(len(ring.units(0, hop))):
-            for way in (0, 1):
-                unit = ring.units(way, hop)[index]
-                hop_copy(way, hop, unit).wait_recv()
-                if hop < ring.half and unit in ring.units(way, hop + 1):
-                    go(hop_copy(way, hop + 1, unit))
+    for k, device in enumerate(others):
+        go(remote(gain_ref, gain_all.at[mine], g_send.at[k], g_recv.at[k], device))
+    gain_all[mine] = gain_ref[...]
+    ins = Fetch(ring, in_ref, w_in, i_sems)
+    gates = Fetch(ring, gate_ref, w_gate, u_sems)
+    gather = Gather(ring, tok_ref, tok_all, t_send, t_recv)
+    ins.begin()
+    gather.begin()
 
     per_head = count * reps // HEADS
-    mine = rep * count + me
     target = mine // per_head
     slot = mine % per_head
 
@@ -846,57 +925,6 @@
     def is_self(j):
         return (rep == j) & (me == target)
 
-    pairs = ((in_ref, w_in), (gu_ref, w_gu))
-
-    def spread(which, k):
-        to = (me + k) % count
-        src, dst = pairs[which]
-        return remote(
-            src.at[to], dst.at[rep, me], a_send.at[which, k], a_recv.at[which, k], (rep, to)
-        )
-
-    def arrived(which, k):
-        frm = (me + count - k) % count
-        src, dst = pairs[which]
-        return remote(
-            src.at[frm], dst.at[rep, frm], a_send.at[which, k], a_recv.at[which, k], (rep, frm)
-        )
-
-    def forward(which, k, hop):
-        frm = (me + count - k) % count
-        src, dst = pairs[which]
-        block = src.at[me] if k == 0 else dst.at[rep, frm]
-        if hop == 0:
-            return remote(
-                block, dst.at[rep, frm], x_send.at[which, k], x_recv.at[which, k], (across, me)
-            )
-        if hop == 1:
-            return remote(
-                block, dst.at[rep, frm], c_send.at[which, k], c_recv.at[which, k], (beside, me)
-            )
-        return remote(
-            dst.at[across, frm], dst.at[across, frm], d_send.at[which, k], d_recv.at[which, k],
-            (beside, me),
-        )
-
-    def pass_on(which, k):
-        if k:
-            arrived(which, k).wait_recv()
-        go(forward(which, k, 0))
-        go(forward(which, k, 1))
-
-    def pass_beside(which, k):
-        forward(which, k, 0).wait_recv()
-        go(forward(which, k, 2))
-
-    for k in range(1, count):
-        go(spread(0, k))
-    pass_on(0, 0)
-    for index in range(UNITS):
-        for way in (0, 1):
-            go(hop_copy(way, 1, ring.units(way, 1)[index]))
-    for k, device in enumerate(others):
-        go(remote(gain_ref, gain_out.at[mine], g_send.at[k], g_recv.at[k], device))
     for j in range(reps):
         @pl.when(jnp.logical_not(is_self(j)))
         def _():
@@ -911,28 +939,47 @@
     dn_d = remote(w_dn.at[across], w_dn.at[across], n_send.at[2], n_recv.at[2], (beside, me))
     go(dn_x)
     go(dn_c)
-    for k in range(1, count):
-        go(spread(1, k))
-    pass_on(1, 0)
+    gates.begin()
     locals_ = []
     for index, (src, dst) in enumerate(
-        (
-            (in_ref.at[me], w_in.at[rep, me]),
-            (gu_ref.at[me], w_gu.at[rep, me]),
-            (dn_ref, w_dn.at[rep]),
-            (tok_ref, tok_out.at[me]),
-            (gain_ref, gain_out.at[mine]),
-        )
+        ((in_ref.at[me], w_in.at[rep, me]), (gate_ref.at[me], w_gate.at[rep, me]), (dn_ref, w_dn.at[rep]))
     ):
         copy = pltpu.make_async_copy(src, dst, loc.at[index])
         copy.start()
         locals_.append(copy)
 
+    for k in range(len(others)):
+        frm = (mine + len(others) - k) % (reps * count)
+        remote(gain_ref, gain_all.at[frm], g_send.at[k], g_recv.at[k], others[k]).wait_recv()
+    gains_ref[...] = jnp.concatenate([gain_all[device, :, 0:d_rows] for device in range(reps * count)], axis=1)
+    gain = 1.0 + gains_ref[0:1, :]
+
+    def norm(value):
+        value = value.astype(f32)
+        return (value * lax.rsqrt(jnp.mean(value * value, axis=-1, keepdims=True) + 1e-06) * gain).astype(h1_ref.dtype)
+
+    def norm_block(shard):
+        for unit in range(UNITS):
+            span = pl.ds(unit * (rows // UNITS), rows // UNITS)
+            h1_ref[shard, span, :] = norm(tok_all[shard, span, :])
+
+    for unit in range(UNITS):
+        span = pl.ds(unit * (rows // UNITS), rows // UNITS)
+        h1_ref[me, span, :] = norm(tok_ref[span, :])
+
+    hops = gather.steps()
+
+    def take_hop(hop):
+        for _ in range(len(ring.units(0, hop))):
+            hops.pop(0)()
+        for way in (0, 1) if hop < ring.half else (0,):
+            norm_block(ring.away(1 - way, hop))
+
     for k in range(1, count):
-        pass_on(0, k)
+        ins.pass_on(k)
     take_hop(1)
     for k in range(count):
-        pass_beside(0, k)
+        ins.pass_beside(k)
     take_hop(2)
     for i in range(per_head):
         remote(
@@ -943,30 +990,26 @@
     ou_d = remote(w_ou.at[across], w_ou.at[across], n_send.at[5], n_recv.at[5], (beside, me))
     go(ou_x)
     go(ou_c)
-    for k in range(1, count // 2):
-        pass_on(1, k)
     dn_x.wait_recv()
     go(dn_d)
+    for k in range(1, count // 2):
+        gates.pass_on(k)
     take_hop(3)
     for k in range(count // 2, count):
-        pass_on(1, k)
+        gates.pass_on(k)
     for hop in range(4, ring.half + 1):
         take_hop(hop)
     ou_x.wait_recv()
     go(ou_d)
     for k in range(count):
-        pass_beside(1, k)
-    for which in (0, 1):
-        for k in range(count):
-            forward(which, k, 1).wait_recv()
-            forward(which, k, 2).wait_recv()
+        gates.pass_beside(k)
+    ins.finish()
+    gates.finish()
     for copy in (dn_c, dn_d, ou_c, ou_d):
         copy.wait_recv()
-    for k in range(len(others)):
-        frm = (mine + len(others) - k) % (reps * count)
-        remote(gain_ref, gain_out.at[frm], g_send.at[k], g_recv.at[k], others[k]).wait_recv()
     for copy in started:
         copy.wait_send()
+    gather.finish()
     for j in range(reps):
         @pl.when(jnp.logical_not(is_self(j)))
         def _():
@@ -975,44 +1018,57 @@
         copy.wait()
 
 
-def opening(reps, count, tokens, gain_tile, w_in, w_gu, w_dn, w_ou, collective_id):
+def opening(reps, count, tokens, gain_tile, w_in, w_gate, w_dn, w_ou, collective_id):
     dma = pltpu.SemaphoreType.DMA
     per_head = count * reps // HEADS
     total = reps * count
     low = jnp.bfloat16
     shape = jax.ShapeDtypeStruct
     hops = dma((2, count // 2, UNITS))
+    width = tokens.shape[1]
+    gathered = (count,) + tokens.shape
     return pl.pallas_call(
         functools.partial(opening_kernel, reps, count),
         out_shape=[
-            shape((count,) + tokens.shape, low),
-            shape((total,) + gain_tile.shape, gain_tile.dtype),
+            shape(gathered, low),
+            shape((8, width), jnp.float32),
             shape((reps,) + w_in.shape, low),
-            shape((reps,) + w_gu.shape, low),
+            shape((reps,) + w_gate.shape, low),
             shape((reps,) + w_dn.shape, low),
             shape((reps, per_head) + w_ou.shape[1:], low),
         ],
-        in_specs=[pl.BlockSpec(memory_space=HB)] * 6,
-        out_specs=[pl.BlockSpec(memory_space=HB)] * 6,
-        scratch_shapes=[hops, hops, dma((total - 1,)), dma((total - 1,))]
-        + [dma((2, count))] * 8
-        + [dma((reps,)), dma((per_head,)), dma((6,)), dma((6,)), dma((5,))],
+        in_specs=[pl.BlockSpec(memory_space=VM)] * 2 + [pl.BlockSpec(memory_space=HB)] * 4,
+        out_specs=[pl.BlockSpec(memory_space=VM)] * 2 + [pl.BlockSpec(memory_space=HB)] * 4,
+        scratch_shapes=[
+            pltpu.VMEM(gathered, low),
+            pltpu.VMEM((total,) + gain_tile.shape, jnp.float32),
+            hops,
+            hops,
+            dma((total - 1,)),
+            dma((total - 1,)),
+            dma((8, count)),
+            dma((8, count)),
+            dma((reps,)),
+            dma((per_head,)),
+            dma((6,)),
+            dma((6,)),
+            dma((3,)),
+        ],
         compiler_params=pltpu.CompilerParams(
             collective_id=collective_id, has_side_effects=True, vmem_limit_bytes=VMEM_LIMIT
         ),
         name="opening",
-    )(tokens, gain_tile, w_in, w_gu, w_dn, w_ou)
-
-
-def cut_kernel(reps, count, in_ref, gate_ref, up_ref, cut_in, cut_gu):
+    )(tokens, gain_tile, w_in, w_gate, w_dn, w_ou)
+
+
+def cut_kernel(reps, count, in_ref, gate_ref, up_ref, cut_in, cut_gate, cut_up):
     low = jnp.bfloat16
     group = HEADS // KV_HEADS
     block = gate_ref.shape[1] // (reps * count)
-    part = block * reps
     for shard in range(count):
-        for index, ref in enumerate((gate_ref, up_ref)):
+        for ref, cut in ((gate_ref, cut_gate), (up_ref, cut_up)):
             pieces = [ref[:, (r * count + shard) * block : (r * count + shard + 1) * block] for r in range(reps)]
-            cut_gu[shard, :, index * part : (index + 1) * part] = jnp.concatenate(pieces, axis=1).astype(low)
+            cut[shard] = jnp.concatenate(pieces, axis=1).astype(low)
         heads = shard, HEADS + shard // group, HEADS + KV_HEADS + shard // group
         for index, head in enumerate(heads):
             cut_in[shard, :, index * HEAD_DIM : (index + 1) * HEAD_DIM] = in_ref[
@@ -1027,10 +1083,11 @@
         functools.partial(cut_kernel, reps, count),
         out_shape=[
             shape((count, rows, 3 * HEAD_DIM), jnp.bfloat16),
-            shape((count, rows, 2 * ffn_gate.shape[1] // count), jnp.bfloat16),
+            shape((count, rows, ffn_gate.shape[1] // count), jnp.bfloat16),
+            shape((count, rows, ffn_up.shape[1] // count), jnp.bfloat16),
         ],
         in_specs=[pl.BlockSpec(memory_space=VM)] * 3,
-        out_specs=[pl.BlockSpec(memory_space=VM)] * 2,
+        out_specs=[pl.BlockSpec(memory_space=VM)] * 3,
         compiler_params=pltpu.CompilerParams(vmem_limit_bytes=VMEM_LIMIT),
         name="cut_weights",
     )(inproj, ffn_gate, ffn_up)
@@ -1348,11 +1405,8 @@
     f32, bf16 = jnp.float32, jnp.bfloat16
     ring = Ring(count)
     rep, me = ring.rep, ring.me
-    hops = ring.half
     here = rep * count + me
     others = everyone(rep, me, reps, count)
-    rows = grad_ref.shape[0] // UNITS
-    width = grad_ref.shape[1]
     full = o_part.shape[1]
     meet(others)
 
@@ -1398,56 +1452,32 @@
     work += [functools.partial(i_finish, k) for k in range(count)]
     work += [functools.partial(o_finish, piece) for piece in o_pieces]
 
-    started = []
-
-    def part(unit):
-        return pl.ds(unit * rows, rows)
-
-    def step_copy(way, step, unit):
-        return remote(
-            held.at[way, step, part(unit)],
-            landed.at[way, step, part(unit)],
-            r_send.at[way, step, unit],
-            r_recv.at[way, step, unit],
-            ring.next[way],
-        )
-
-    for step in range(hops):
-        order = ring.units(0, hops - step), ring.units(1, hops - step)
-        before = [ring.units(way, hops - step + 1) if step else [] for way in (0, 1)]
-        for index in range(len(order[0])):
-            for way in (0, 1):
-                unit = order[way][index]
-                block = x_ref[ring.away(way, hops - step), part(unit), :].astype(f32)
-                if unit in before[way]:
-                    step_copy(way, step - 1, unit).wait_recv()
-                    block += landed[way, step - 1, part(unit), :].astype(f32)
-                held[way, step, part(unit), :] = block.astype(held.dtype)
-                copy = step_copy(way, step, unit)
-                copy.start()
-                started.append(copy)
-            if step == 0 and index == 0:
-                ins.begin(i_pieces)
-                outs.begin(o_pieces)
-            elif step and work:
-                work.pop(0)()
-                if work:
-                    work.pop(0)()
-    gg = jnp.zeros((1, width), f32)
+    terms = []
     gain = 1.0 + gains_ref[0:1, :]
-    for unit in range(UNITS):
-        span = part(unit)
-        total = x_ref[me, span, :].astype(f32)
-        for way in (0, 1):
-            step_copy(way, hops - 1, unit).wait_recv()
-            total += landed[way, hops - 1, span, :].astype(f32)
+    opened = []
+
+    def pause():
+        if not opened:
+            opened.append(True)
+            ins.begin(i_pieces)
+            outs.begin(o_pieces)
+            return
+        for _ in range(min(2, len(work))):
+            work.pop(0)()
+
+    def finish(span, total):
         value = tokens_ref[span, :].astype(f32)
         scale = lax.rsqrt(jnp.mean(value * value, axis=-1, keepdims=True) + 1e-06)
         normed = value * scale
         weighted = total * gain
         inner = jnp.mean(weighted * normed, axis=-1, keepdims=True)
         grad_ref[span, :] = dmid_ref[span, :] + scale * (weighted - normed * inner)
-        gg += jnp.sum(total * normed, axis=0, keepdims=True)
+        terms.append(jnp.sum(total * normed, axis=0, keepdims=True))
+
+    started = reduce_on_ring(
+        ring, grad_ref.shape[0], lambda shard, span: x_ref[shard, span, :], held, landed, r_send, r_recv, finish, pause
+    )
+    gg = functools.reduce(jnp.add, terms)
     d_rows = sum_ref.shape[1]
     total_ref[...] = gg_ref[...]
     total_ref[0:1, :] = gg
@@ -1621,47 +1651,34 @@
     per_head = HEAD_DIM // o_rows
     piece = o_rows // reps
 
-    cut_in, cut_gu = cut_weights(reps, count, inproj, ffn_gate, ffn_up)
+    cut_in, cut_gate, cut_up = cut_weights(reps, count, inproj, ffn_gate, ffn_up)
     cut_out = outproj.astype(bf16).reshape(reps, piece, width)
-    gain_tile = as_tile(norm_gains.astype(bf16).astype(f32).reshape(-1))
-    all_tokens, gain_tiles, got_in, got_gu, got_down, got_out = opening(
-        reps, count, tokens, gain_tile, cut_in, cut_gu, ffn_down.astype(bf16), cut_out, 1
-    )
-    all_tokens = all_tokens.reshape(seq_len, width)
+    gain_tile = jnp.pad(norm_gains.astype(bf16).astype(f32).T, ((0, 4), (0, 128 - d_rows)))
+    normed_in, gain_rows, got_in, got_gate, got_down, got_out = opening(
+        reps, count, tokens, gain_tile, cut_in, cut_gate, ffn_down.astype(bf16), cut_out, 1
+    )
+    normed_in = normed_in.reshape(seq_len, width)
     w_in = got_in.reshape(width, -1)
-    w_gu = got_gu.reshape(width, 2 * ff_part)
+    w_gate = got_gate.reshape(width, ff_part)
     w_down = got_down.reshape(ff_part, width)
     w_out = got_out.transpose(1, 0, 2, 3).reshape(HEAD_DIM, width)
-    gains = gain_tiles.reshape(total, -1)[:, : d_rows * 4].reshape(width, 4)
-    gain_rows = gains.T
-
-    normed_in = rms_norm(all_tokens.astype(f32), gains[:, 0]).astype(bf16)
-    projected = jnp.dot(normed_in, w_in, preferred_element_type=f32)
+
     half = HEAD_DIM // 2
     position = jnp.arange(seq_len, dtype=jnp.int32)
     freq = 10000.0 ** (-(jnp.arange(half, dtype=f32) * 2.0 / HEAD_DIM))
     angle = position.astype(f32)[:, None] * freq[None, :]
     cosine, sine = jnp.cos(angle), jnp.sin(angle)
     query_scale = HEAD_DIM ** (-0.5)
-    queries = (turn(projected[:, :HEAD_DIM], cosine, sine) * query_scale).astype(bf16)
-    keys = turn(projected[:, HEAD_DIM : 2 * HEAD_DIM], cosine, sine).astype(bf16)
-    values = projected[:, 2 * HEAD_DIM :].astype(bf16)
     starts = lax.dynamic_slice_in_dim(piece_starts, rep, 1, 0)[0]
     inside = (position[:, None] >= starts[None, :]) & (position[:, None] < starts[None, :] + PIC)
     tag = jnp.sum(inside.astype(jnp.int32) * (jnp.arange(starts.shape[0], dtype=jnp.int32)[None, :] + 1), axis=1)
-    visible = (position[None, :] <= position[:, None]) | ((tag[:, None] == tag[None, :]) & (tag[:, None] > 0))
-    raw = lax.dot_general(queries, keys, (((1,), (1,)), ((), ())), preferred_element_type=f32)
-    bent = jnp.tanh(raw / 50.0)
-    masked = jnp.where(visible, 50.0 * bent, -1e30)
-    top_score = jnp.max(masked, axis=-1, keepdims=True)
-    expo = jnp.exp(masked - top_score)
-    probs = expo / jnp.sum(expo, axis=-1, keepdims=True)
-    probs_low = probs.astype(bf16)
-    attended = jnp.dot(probs_low, values, preferred_element_type=f32).astype(bf16)
-    attn_proj = ring_reduce(jnp.dot(attended, w_out, preferred_element_type=f32).astype(bf16), count, 4)
+    attn_proj, queries, keys, values, attended, probs, damp, got_up = attention(
+        reps, count, normed_in, w_in, w_out, cosine, sine, tag, cut_up, 4
+    )
+    w_up = got_up.reshape(width, ff_part)
 
     layer_out, d_middle, d_attn, gain_terms, normed_mid, hidden, d_ffn, d_gu = feed_forward(
-        attn_proj, tokens, cotangent, gain_rows, w_gu, w_down, count, 5
+        attn_proj, tokens, cotangent, gain_rows, w_gate, w_up, w_down, count, 5
     )
     d_attn, sum_gu, grad_down = ffn_grads(
         reps, count, d_attn, normed_mid, hidden, d_ffn, d_gu, d_rows, 9
@@ -1670,10 +1687,9 @@
     grad_gate, grad_up = join_grads(reps, count, sum_gu)
     d_attended = back_dot(d_attn, w_out).astype(bf16)
     d_probs = back_dot(d_attended, values)
-    d_values = dot_tn(probs_low, d_attended)
-    d_scores = (
-        probs * (d_probs - jnp.sum(probs * d_probs, axis=-1, keepdims=True)) * (1.0 - bent * bent)
-    ).astype(bf16)
+    d_values = dot_tn(probs, d_attended)
+    inner = jnp.sum(probs.astype(f32) * d_probs, axis=-1, keepdims=True)
+    d_scores = (damp.astype(f32) * (d_probs - inner)).astype(bf16)
     d_queries = jnp.dot(d_scores, keys, preferred_element_type=f32)
     d_keys = dot_tn(d_scores, queries)
     d_projected = jnp.concatenate(

time: 845 us -> 796 us (0.942)
  other arithmetic: 75.1 us -> 55.8 us
  Pallas kernels: 695 us -> 677 us
  matrix products: 30.7 us -> 19.3 us
    pallas_call x1, Pallas kernels: 161 us -> 122 us  [opening(): pl.pallas_call(functools.partial(opening_kernel, reps, count), out_shape=...]
    pallas_call x1, Pallas kernels: 77.1 us -> 97.5 us  [attention(): pl.pallas_call(functools.partial(attention_kernel, reps, count), out_shap...]
    dot_general x4 -> x0, matrix products: 9.96 us -> none  [the longest x1 3.99 us: split_device(): projected = jnp.dot(normed_in, w_in, preferred_element_type=f32)]
    convert_element_type x3 -> x1, other arithmetic: 10.3 us -> 0.55 us  [split_device(): d_scores = (damp.astype(f32) * (d_probs - inner)).astype(bf16)]
where the time goes in v3:
time: 796 us; the launch traced here: 787 us
  Pallas kernels  677 us (85%)
  other arithmetic  55.8 us (7%)
  local copies, waits for them, and re-layouts  25.3 us (3%)
  matrix products  19.3 us (2%)
  between operations  9.21 us (1%)
    pallas_call x1, Pallas kernels, feed_forward(): pl.pallas_call(functools.partial(ffn_kernel, count), out_shape=[shape((ro...  211 us
    pallas_call x1, Pallas kernels, ffn_grads(): pl.pallas_call(functools.partial(ffn_grads_kernel, reps, count), out_shap...  126 us
    pallas_call x1, Pallas kernels, opening(): pl.pallas_call(functools.partial(opening_kernel, reps, count), out_shape=...  122 us
    pallas_call x1, Pallas kernels, closing(): pl.pallas_call(functools.partial(closing_kernel, reps, count), out_shape=...  100 us
    pallas_call x1, Pallas kernels, attention(): pl.pallas_call(functools.partial(attention_kernel, reps, count), out_shap...  97.5 us
    reduce_sum x5, other arithmetic, split_device(): jnp.sum(item[2] * item[2])  23.9 us

profile of v3, /device:TPU:0, one launch (start us, length us, event | category | flops | bytes accessed | tf_op | source)
XLA Modules:
  0.0 786.7 jit_solution(423352812087803513)
XLA Ops:
  0.7 0.9 dynamic-slice_reduce_fusion
  1.6 1.4 multiply_reduce_fusion.12
  3.0 0.1 fusion.16
  3.1 0.6 pad_convert_fusion.gain_ref
  3.7 1.8 convert_element_type.73
  5.5 1.0 copy.93.tagq_ref
  6.5 3.0 multiply_sine_fusion
  9.5 2.9 convert_element_type.72.dn_ref
  12.5 5.4 cut_weights.1
  17.9 122.0 %opening.1 = (bf16[8,128,2304]{2,1,0:T(8,128)(2,1)}, f32[8,2304]{1,0:T(8,128)}, bf16[4,8,72,768]{3,2,1,0:T(8,128)(2,1)}, bf16[4,8,72,1152]{3,2,1,0:T(8,128)(2,1)...) custom-call(bf16[128,2304]{1,0:T(8,128)(2,1)} %tokens_ref.3, f32[8,128]{1,0:T(8,128)} %pad_convert_fusion.gain_ref, ...), custom_call_target="tpu_custom_call" | custom-call | tf_op jit(solution)/shard_map/opening/pallas_call | solution.py:1030
  139.9 2.4 copy.92
  142.3 97.5 %attention.1 = (f32[128,2304]{1,0:T(8,128)}, bf16[1024,256]{1,0:T(8,128)(2,1)}, bf16[1024,256]{1,0:T(8,128)(2,1)}, bf16[1024,256]{1,0:T(8,128)(2,1)}, bf16[1024,...) custom-call(bf16[1024,2304]{1,0:T(8,128)(2,1)} %bitcast.82, ...), custom_call_target="tpu_custom_call" | custom-call | tf_op jit(solution)/shard_map/attention/pallas_call | solution.py:790
  239.8 210.8 %feed_forward.1 = (bf16[128,2304]{1,0:T(8,128)(2,1)}, f32[128,2304]{1,0:T(8,128)}, bf16[128,2304]{1,0:T(8,128)(2,1)}, f32[8,2304]{1,0:T(8,128)}, bf16[1024,2304]...) custom-call(f32[128,2304]{1,0:T(8,128)} %get-tuple-element.67.attn_ref, ...), custom_call_target="tpu_custom_call" | custom-call | tf_op jit(solution)/shard_map/feed_forward/pallas_call | solution.py:676
  450.7 126.1 %ffn_grads.1 = (bf16[8,128,2304]{2,1,0:T(8,128)(2,1)}, bf16[8,72,2304]{2,1,0:T(8,128)(2,1)}, f32[288,2304]{1,0:T(8,128)}) custom-call(bf16[128,2304]{1,0:T(8,128)(2,1)} %get-tuple-element.74.dattn_ref, bf16[1024,2304]{1,0:T(8,128)(2,1)} %get-tuple-element.75.h3_ref, bf16[1024,1152]{1,0:T(8,128)(2,1)} %get-tuple-element.76.hid_ref, ...), custom_call_target="tpu_custom_call" | custom-call | tf_op jit(solution)/shard_map/ffn_grads/pallas_call | solution.py:1361
  576.9 3.9 convolution_convert_fusion.3
  580.8 1.4 convolution_convert_fusion.2
  582.2 1.1 copy.113
  583.3 0.8 convolution_convert_fusion.4
  584.1 0.3 copy-done.27
  584.4 0.8 multiply_reduce_fusion
  585.2 0.8 copy-done.20
  586.0 0.5 multiply_convert_fusion
  586.5 0.5 copy-done.37
  587.0 0.7 fusion.29
  587.8 0.3 copy-done.36
  588.1 0.7 fusion.28
  588.8 2.6 fusion.10
  591.5 5.4 convolution_convert_fusion.1
  596.9 5.5 convolution_convert_fusion
  602.4 100.1 %closing.1 = (f32[128,2304]{1,0:T(8,128)}, bf16[8,72,768]{2,1,0:T(8,128)(2,1)}, bf16[4,16,2304]{2,1,0:T(8,128)(2,1)}, f32[32,8,128]{2,1,0:T(8,128)}) custom-call(bf16[8,128,2304]{2,1,0:T(8,128)(2,1)} %bitcast.78, bf16[128,2304]{1,0:T(8,128)(2,1)} %tokens_ref.3, f32[128,2304]{1,0:T(8,128)} %get-tuple-element.84.dmid_ref, ...), custom_call_target="tpu_custom_call" | custom-call | tf_op jit(solution)/shard_map/closing/pallas_call | solution.py:1525
  702.5 0.9 reduce_sum.166
  703.5 1.2 multiply_reduce_fusion.11
  704.7 1.3 convert_element_type.82
  706.0 0.1 bitcast_reduce_fusion
  706.4 0.7 copy-done.26
  707.1 0.2 copy-done.13
  707.3 0.2 copy-done.25
  707.6 2.0 multiply_reduce_fusion.9
  709.6 2.8 multiply_reduce_fusion.7
  712.4 0.7 copy-done
  713.1 0.8 copy-done.3
  713.8 4.9 multiply_reduce_fusion.1
  718.7 4.8 join_grads.1
  723.6 13.0 %multiply_reduce_fusion.2 = (f32[]{:T(128)}, f32[]{:T(128)}, f32[72,9216]{1,0:T(8,128)}, f32[72,9216]{1,0:T(8,128)}, f32[]{:T(128)}, /*index=5*/f32[]{:T(128)}, f32[72,9216]{1,0:T(8,128)}, f32[72,9216]{1,0:T(8,128)}) fusion(f32[72,9216]{1,0:T(8,128)} %up_ref.1, f32[72,9216]{1,0:T(8,128)} %get-tuple-element.185, f32[72,9216]{1,0:T(8,128)} %param.40, ...), kind=kLoop, calls=%fused_computation.19 | loop fusion | flops 18579452 | bytes 31850512 | tf_op jit(solution)/shard_map/reduce_sum | solution.py:1724
  736.6 7.8 stack.51
  744.4 0.6 pad_bitcast_fusion.x_ref
  745.0 10.3 %small_exchange_14.1 = f32[32,8,128]{2,1,0:T(8,128)} custom-call(f32[8,128]{1,0:T(8,128)} %pad_bitcast_fusion.x_ref), custom_call_target="tpu_custom_call" | custom-call | tf_op jit(solution)/shard_map/small_exchange_14/pallas_call | solution.py:1594
  755.2 0.9 reduce_sum.179
  756.2 0.1 reshape.167
  756.3 0.6 fusion.27
  764.8 0.6 multiply_subtract_fusion.5
  765.3 2.5 multiply_subtract_fusion.4
  767.8 3.3 multiply_subtract_fusion.3
  771.2 2.7 multiply_subtract_fusion
  774.0 0.5 copy-done.9
  774.5 1.0 copy-done.10
  775.5 2.7 multiply_subtract_fusion.1
  778.2 0.7 copy-done.11
  778.9 0.9 copy-done.12
  779.8 2.7 multiply_subtract_fusion.2
  782.5 0.8 copy.119
  783.3 1.0 copy.120
  784.4 0.6 copy-done.4
  784.9 1.5 copy.121
  (82 shorter events, 0.5 us)
Async XLA Ops:
  3.1 9.4 %copy-start.30 = (s32[1024]{0:T(1024)}, s32[1024]{0:T(1024)S(1)}, u32[]{:S(2)}) copy-start(s32[1024]{0:T(1024)S(1)} %fusion.16) | copy-start | bytes 12292
  450.7 126.2 %copy-start.14 = (bf16[4,4,16,2304]{3,2,1,0:T(8,128)(2,1)S(1)}, bf16[4,4,16,2304]{3,2,1,0:T(8,128)(2,1)}, u32[]{:S(2)}) copy-start(bf16[4,4,16,2304]{3,2,1,0:T(8,128)(2,1)} %copy.92) | copy-start | bytes 3538948
  576.8 3.9 copy-start.35
  576.8 3.9 copy-start.38
  580.8 2.6 copy-start.19
  583.3 1.0 copy-start.27
  584.4 1.6 copy-start.20
  586.0 1.0 copy-start.37
  587.0 1.0 copy-start.36
  587.0 4.5 slice-start
  588.1 3.5 slice-start.1
  591.5 5.4 copy-start.15
  602.4 101.0 %copy-start.31 = (f32[72,4]{0,1:T(4,128)S(1)}, f32[72,4]{0,1:T(4,128)}, u32[]{:S(2)}) copy-start(f32[72,4]{0,1:T(4,128)} %param.30) | copy-start | bytes 3460
  602.4 101.0 %copy-start.32 = (f32[72,4]{0,1:T(4,128)S(1)}, f32[72,4]{0,1:T(4,128)}, u32[]{:S(2)}) copy-start(f32[72,4]{0,1:T(4,128)} %param.42) | copy-start | bytes 3460
  602.4 101.0 %copy-start.33 = (f32[72,4]{0,1:T(4,128)S(1)}, f32[72,4]{0,1:T(4,128)}, u32[]{:S(2)}) copy-start(f32[72,4]{0,1:T(4,128)} %param.36) | copy-start | bytes 3460
  706.0 1.1 copy-start.26
  706.1 1.2 copy-start.13
  706.1 1.3 copy-start.25
  706.2 1.4 copy-start.28
  706.2 3.4 copy-start.23
  706.3 3.3 copy-start.22
  706.3 3.2 copy-start.7
  707.6 4.8 copy-start.18
  707.6 4.8 copy-start.16
  707.6 4.8 copy-start.17
  709.5 3.5 copy-start
  709.5 4.3 copy-start.3
  723.6 32.7 %copy-start.34 = (f32[6]{0:T(128)S(1)}, f32[6]{0:T(128)}, u32[]{:S(2)}) copy-start(f32[6]{0:T(128)} %constant.74) | copy-start | bytes 76
  756.3 11.6 %copy-start.8 = (f32[72,4096]{1,0:T(8,128)S(1)}, f32[72,4096]{1,0:T(8,128)}, u32[]{:S(2)}) copy-start(f32[72,4096]{1,0:T(8,128)} %in_ref.1) | copy-start | bytes 3538948
  756.3 14.9 %copy-start.29 = (f32[2,6]{1,0:T(2,128)}, f32[2,6]{1,0:T(2,128)S(1)}, u32[]{:S(2)}) copy-start(f32[2,6]{1,0:T(2,128)S(1)} %fusion.18) | copy-start | bytes 148
  765.3 5.8 copy-start.6
  767.8 3.4 copy-start.5
  771.2 2.8 copy-start.1
  771.2 3.3 copy-start.9
  771.2 4.3 copy-start.10
  775.5 2.7 copy-start.2
  775.5 3.4 copy-start.11
  775.5 4.3 copy-start.12
  779.8 2.7 copy-start.24
  779.8 3.5 copy-start.21
  782.5 2.4 copy-start.4

commit v4 on v3

--- a/solution.py
+++ b/solution.py
@@ -373,7 +373,7 @@
         return order if hop < self.half else order[: UNITS // 2]
 
 
-def reduce_on_ring(ring, rows, take, held, landed, send, recv, finish, pause):
+def reduce_on_ring(ring, rows, take, first, landed, send, recv, finish, pause):
     f32 = jnp.float32
     hops = ring.half
     started = []
@@ -383,7 +383,7 @@
 
     def step_copy(way, step, unit):
         return remote(
-            held.at[way, step, part(unit)],
+            landed.at[way, step - 1, part(unit)] if step else first.at[part(unit)],
             landed.at[way, step, part(unit)],
             send.at[way, step, unit],
             recv.at[way, step, unit],
@@ -400,7 +400,10 @@
                 if unit in before[way]:
                     step_copy(way, step - 1, unit).wait_recv()
                     block += landed[way, step - 1, part(unit), :].astype(f32)
-                held[way, step, part(unit), :] = block.astype(held.dtype)
+                if step:
+                    landed[way, step - 1, part(unit), :] = block.astype(landed.dtype)
+                else:
+                    first[part(unit), :] = block.astype(first.dtype)
                 copy = step_copy(way, step, unit)
                 copy.start()
                 started.append(copy)
@@ -706,7 +709,7 @@
 def attention_kernel(
     reps, count, h1_ref, in_ref, wo_ref, cos_ref, sin_ref, tagq_ref, tagk_ref, cut_ref,
     proj_ref, q_ref, k_ref, v_ref, att_ref, probs_ref, damp_ref, up_ref,
-    part, held, landed, r_send, r_recv, w_sems, loc
+    part, first, landed, r_send, r_recv, w_sems, loc
 ):
     f32, bf16 = jnp.float32, jnp.bfloat16
     ring = Ring(count)
@@ -769,7 +772,7 @@
     def take(shard, span):
         return part[pl.ds(pl.multiple_of(shard * rows + span.start, 16), span.size), :]
 
-    started = reduce_on_ring(ring, rows, take, held, landed, r_send, r_recv, finish, pause)
+    started = reduce_on_ring(ring, rows, take, first, landed, r_send, r_recv, finish, pause)
     for piece in work:
         piece()
     weights.finish()
@@ -797,7 +800,7 @@
         out_specs=[pl.BlockSpec(memory_space=VM)] * 7 + [pl.BlockSpec(memory_space=HB)],
         scratch_shapes=[
             pltpu.VMEM((seq_len, width), f32),
-            pltpu.VMEM((2, hops, rows, width), low),
+            pltpu.VMEM((rows, width), low),
             pltpu.VMEM((2, hops, rows, width), low),
             dma((2, hops, UNITS)),
             dma((2, hops, UNITS)),
@@ -1091,33 +1094,6 @@
         compiler_params=pltpu.CompilerParams(vmem_limit_bytes=VMEM_LIMIT),
         name="cut_weights",
     )(inproj, ffn_gate, ffn_up)
-
-
-def join_kernel(reps, count, sum_ref, gate_ref, up_ref):
-    block = gate_ref.shape[1] // (reps * count)
-    part = block * reps
-    per = 4
-    for index, ref in enumerate((gate_ref, up_ref)):
-        for first in range(0, reps * count, per):
-            pieces = []
-            for b in range(first, first + per):
-                r, shard = b // count, b % count
-                start = index * part + r * block
-                pieces.append(sum_ref[shard, :, start : start + block].astype(jnp.float32))
-            ref[:, first * block : (first + per) * block] = jnp.concatenate(pieces, axis=1)
-
-
-def join_grads(reps, count, sums):
-    rows = sums.shape[1]
-    shape = jax.ShapeDtypeStruct((rows, sums.shape[2] * count // 2), jnp.float32)
-    return pl.pallas_call(
-        functools.partial(join_kernel, reps, count),
-        out_shape=[shape, shape],
-        in_specs=[pl.BlockSpec(memory_space=VM)],
-        out_specs=[pl.BlockSpec(memory_space=VM)] * 2,
-        compiler_params=pltpu.CompilerParams(vmem_limit_bytes=VMEM_LIMIT),
-        name="join_grads",
-    )(sums)
 
 
 class RepSum:
@@ -1398,9 +1374,12 @@
 
 
 def closing_kernel(
-    reps, count, x_ref, tokens_ref, dmid_ref, gains_ref, gg_ref, i_part, o_part, grad_ref, sum_ref, out_ref, gain_ref,
-    held, landed, total_ref, tiles, i_core, i_to, i_from, o_core, o_to, o_from,
-    r_send, r_recv, ic_s, ic_r, ix_s, ix_r, oc_s, oc_r, ox_s, ox_r, s_send, s_recv, p_send, p_recv, g_send, g_recv
+    reps, count, dattn_ref, h1_ref, in_ref, wo_ref, q_ref, k_ref, v_ref, att_ref, probs_ref, damp_ref, cos_ref, sin_ref,
+    tokens_ref, dmid_ref, gains_ref, gg_ref, grad_ref, sum_ref, out_ref, gain_ref,
+    x_part, dproj, d_key, d_value, i_part, o_part, first, landed, total_ref, tiles, i_core, i_to, i_from,
+    o_core, o_to, o_from,
+    r_send, r_recv, ic_s, ic_r, ix_s, ix_r, oc_s, oc_r, ox_s, ox_r, s_send, s_recv, p_send, p_recv,
+    g_send, g_recv
 ):
     f32, bf16 = jnp.float32, jnp.bfloat16
     ring = Ring(count)
@@ -1408,7 +1387,64 @@
     here = rep * count + me
     others = everyone(rep, me, reps, count)
     full = o_part.shape[1]
+    d_rows = sum_ref.shape[1]
+    seq_len, width = dattn_ref.shape
+    rows = grad_ref.shape[0]
+    half = HEAD_DIM // 2
     meet(others)
+
+    def nt(left, right):
+        return lax.dot_general(left, right, (((1,), (1,)), ((), ())), preferred_element_type=f32)
+
+    def unturned(flat, at):
+        cosine, sine = cos_ref[at, :], sin_ref[at, :]
+        low, high = flat[:, :half], flat[:, half:]
+        return jnp.concatenate([low * cosine + high * sine, high * cosine - low * sine], axis=1)
+
+    tall = seq_len // 4
+    d_key[...] = jnp.zeros_like(d_key)
+    d_value[...] = jnp.zeros_like(d_value)
+
+    def attend(i, carry):
+        at = pl.ds(pl.multiple_of(i * tall, 16), tall)
+        d_att = nt(dattn_ref[at, :], wo_ref[...]).astype(bf16)
+        d_probs = nt(d_att, v_ref[...])
+        probs = probs_ref[at, :]
+        inner = jnp.sum(probs.astype(f32) * d_probs, axis=-1, keepdims=True)
+        d_scores = (damp_ref[at, :].astype(f32) * (d_probs - inner)).astype(bf16)
+        d_query = jnp.dot(d_scores, k_ref[...], preferred_element_type=f32)
+        dproj[at, :HEAD_DIM] = (unturned(d_query, at) * HEAD_DIM ** (-0.5)).astype(bf16)
+        d_key[...] += tn(d_scores, q_ref[at, :])
+        d_value[...] += tn(probs, d_att)
+        return carry
+
+    lax.fori_loop(0, 4, attend, 0)
+
+    def project(i, carry):
+        at = pl.ds(pl.multiple_of(i * tall, 16), tall)
+        dproj[at, HEAD_DIM : 2 * HEAD_DIM] = unturned(d_key[at, :], at).astype(bf16)
+        dproj[at, 2 * HEAD_DIM :] = d_value[at, :].astype(bf16)
+        x_part[at, :] = nt(dproj[at, :], in_ref[...]).astype(bf16)
+        return carry
+
+    lax.fori_loop(0, 4, project, 0)
+
+    def make_out():
+        per = width // 3
+
+        def body(n, carry):
+            cols = pl.ds(pl.multiple_of(n * per, 128), per)
+            made = tn(att_ref[...], dattn_ref[:, cols]).reshape(full, reps, HEAD_DIM // full // reps, per)
+            for owner in range(reps):
+                o_part[owner, :, :, cols] = made[:, owner].astype(bf16)
+            return carry
+
+        lax.fori_loop(0, 3, body, 0)
+
+    def make_in(owner):
+        deep = count * d_rows
+        made = tn(h1_ref[:, owner * deep : (owner + 1) * deep], dproj[...])
+        i_part[owner] = made.reshape(count, d_rows, 3 * HEAD_DIM).astype(bf16)
 
     o_pieces = list(range(full))
     i_pieces = [(me + k) % count for k in range(1, count)] + [me]
@@ -1447,23 +1483,22 @@
         else:
             sum_ref[me] = total
 
-    work = [functools.partial(ins.cross, piece) for piece in i_pieces]
+    work = [functools.partial(make_in, owner) for owner in range(reps)]
+    work += [lambda: ins.begin(i_pieces), make_out, lambda: outs.begin(o_pieces)]
+    work += [functools.partial(ins.cross, piece) for piece in i_pieces]
     work += [functools.partial(outs.cross, piece) for piece in o_pieces]
     work += [functools.partial(i_finish, k) for k in range(count)]
     work += [functools.partial(o_finish, piece) for piece in o_pieces]
 
     terms = []
     gain = 1.0 + gains_ref[0:1, :]
-    opened = []
 
     def pause():
-        if not opened:
-            opened.append(True)
-            ins.begin(i_pieces)
-            outs.begin(o_pieces)
-            return
         for _ in range(min(2, len(work))):
             work.pop(0)()
+
+    def take(shard, span):
+        return x_part[pl.ds(pl.multiple_of(shard * rows + span.start, 16), span.size), :]
 
     def finish(span, total):
         value = tokens_ref[span, :].astype(f32)
@@ -1474,16 +1509,13 @@
         grad_ref[span, :] = dmid_ref[span, :] + scale * (weighted - normed * inner)
         terms.append(jnp.sum(total * normed, axis=0, keepdims=True))
 
-    started = reduce_on_ring(
-        ring, grad_ref.shape[0], lambda shard, span: x_ref[shard, span, :], held, landed, r_send, r_recv, finish, pause
-    )
-    gg = functools.reduce(jnp.add, terms)
-    d_rows = sum_ref.shape[1]
+    started = reduce_on_ring(ring, rows, take, first, landed, r_send, r_recv, finish, pause)
     total_ref[...] = gg_ref[...]
-    total_ref[0:1, :] = gg
+    total_ref[0:1, :] = functools.reduce(jnp.add, terms)
     every = total_ref[...]
     for owner in range(reps * count):
         tiles[owner, :, 0:d_rows] = every[:, owner * d_rows : (owner + 1) * d_rows]
+        tiles[owner, :, d_rows:] = jnp.zeros((8, 128 - d_rows), f32)
     for k, device in enumerate(others):
         to = (here + k + 1) % (reps * count)
         remote(tiles.at[to], gain_ref.at[here], g_send.at[k], g_recv.at[k], device).start()
@@ -1511,29 +1543,40 @@
         copy.wait_send()
 
 
-def closing(reps, count, partial, tokens, d_middle, gain_rows, gain_terms, part_in, part_out, collective_id):
+def closing(
+    reps, count, d_attn, normed, w_in, w_out, queries, keys, values, attended, probs, damp, cosine, sine,
+    tokens, d_middle, gain_rows, gain_terms, piece, collective_id
+):
     dma = pltpu.SemaphoreType.DMA
     low, f32 = jnp.bfloat16, jnp.float32
     shape = jax.ShapeDtypeStruct
     rows, width = tokens.shape
+    seq_len = normed.shape[0]
     total = reps * count
     half = count // 2
-    i_block = part_in.shape[1:]
-    o_block = part_out.shape[1:]
-    full = o_block[0]
+    d_rows = width // total
+    full = HEAD_DIM // (reps * piece)
+    i_block = (count, d_rows, 3 * HEAD_DIM)
+    o_block = (full, piece, width)
     hops = dma((2, half, UNITS))
     return pl.pallas_call(
         functools.partial(closing_kernel, reps, count),
         out_shape=[
             shape((rows, width), f32),
             shape(i_block, low),
-            shape((reps,) + o_block[1:], low),
+            shape((reps, piece, width), low),
             shape((total, 8, 128), f32),
         ],
-        in_specs=[pl.BlockSpec(memory_space=VM)] * 7,
+        in_specs=[pl.BlockSpec(memory_space=VM)] * 16,
         out_specs=[pl.BlockSpec(memory_space=VM)] * 4,
         scratch_shapes=[
-            pltpu.VMEM((2, half, rows, width), low),
+            pltpu.VMEM((seq_len, width), low),
+            pltpu.VMEM((seq_len, 3 * HEAD_DIM), low),
+            pltpu.VMEM((seq_len, HEAD_DIM), f32),
+            pltpu.VMEM((seq_len, HEAD_DIM), f32),
+            pltpu.VMEM((reps,) + i_block, low),
+            pltpu.VMEM((reps,) + o_block, low),
+            pltpu.VMEM((rows, width), low),
             pltpu.VMEM((2, half, rows, width), low),
             pltpu.VMEM((8, width), f32),
             pltpu.VMEM((total, 8, 128), f32),
@@ -1564,69 +1607,260 @@
             collective_id=collective_id, has_side_effects=True, vmem_limit_bytes=VMEM_LIMIT
         ),
         name="closing",
-    )(partial.reshape(count, rows, width), tokens, d_middle, gain_rows, gain_terms, part_in, part_out)
-
-
-def small_kernel(reps, count, spread, x_ref, out_ref, send, recv):
+    )(
+        d_attn, normed, w_in, w_out, queries, keys, values, attended, probs, damp, cosine, sine,
+        tokens, d_middle, gain_rows, gain_terms,
+    )
+
+
+def tiles_of(ref):
+    rows, columns = ref.shape
+    tall = 72 if rows % 72 == 0 else 64 if rows % 64 == 0 else 8
+    wide = 384 if columns % 384 == 0 else 256
+    return rows // tall, columns // wide, tall, wide
+
+
+def tile_at(ref, n):
+    _, across, tall, wide = tiles_of(ref)
+    down, right = n // across, n % across
+    return pl.ds(pl.multiple_of(down * tall, 8), tall), pl.ds(pl.multiple_of(right * wide, 128), wide)
+
+
+LAMB_ORDER = (4, 2, 3, 0, 1)
+
+
+def lamb_kernel(reps, count, sum_in, sum_out, sum_gu, gain_tiles, g_master, g_mean, g_square, *refs):
+    f32 = jnp.float32
+    names = 5
+    hbm_in, refs = [refs[3 * i : 3 * i + 3] for i in range(names)], refs[3 * names :]
+    grad_dn, refs = refs[0], refs[1:]
+    (sums_out, gg_out, gm_out, gs_out, gp_out), refs = refs[:5], refs[5:]
+    hbm_out, refs = [refs[4 * i : 4 * i + 4] for i in range(names)], refs[4 * names :]
+    masters, means, squares, grads = (refs[names * i : names * (i + 1)] for i in range(4))
+    in_sem, out_sem, dn_sem = refs[4 * names :]
+    total = reps * count
+    group = HEADS // KV_HEADS
+
+    def fetch(i, j):
+        return pltpu.make_async_copy(hbm_in[i][j], (masters, means, squares)[j][i], in_sem.at[i, j])
+
+    fetch_dn = pltpu.make_async_copy(grad_dn, grads[4], dn_sem)
+    fetch_dn.start()
+    for i in LAMB_ORDER:
+        for j in range(3):
+            fetch(i, j).start()
+
+    def store(i, j):
+        return pltpu.make_async_copy((grads, means, squares, masters)[j][i], hbm_out[i][j], out_sem.at[i, j])
+
+    def join(index, ref):
+        block = ref.shape[1] // total
+        part = block * reps
+        for first in range(0, total, 4):
+            pieces = []
+            for b in range(first, first + 4):
+                start = index * part + (b // count) * block
+                pieces.append(sum_gu[b % count, :, start : start + block].astype(f32))
+            ref[:, first * block : (first + 4) * block] = jnp.concatenate(pieces, axis=1)
+
+    def make_grad(i):
+        if i == 0:
+            for head in range(HEADS):
+                grads[0][:, head * HEAD_DIM : (head + 1) * HEAD_DIM] = sum_in[head, :, :HEAD_DIM].astype(f32)
+            for kind in (1, 2):
+                for head in range(KV_HEADS):
+                    start = (HEADS + (kind - 1) * KV_HEADS + head) * HEAD_DIM
+                    parts = [
+                        sum_in[head * group + g, :, kind * HEAD_DIM : (kind + 1) * HEAD_DIM].astype(f32)
+                        for g in range(group)
+                    ]
+                    grads[0][:, start : start + HEAD_DIM] = functools.reduce(jnp.add, parts)
+        elif i == 1:
+            rows = sum_out.shape[1]
+            for j in range(reps):
+                grads[1][j * rows : (j + 1) * rows, :] = sum_out[j].astype(f32)
+        elif i in (2, 3):
+            join(i - 2, grads[i])
+        else:
+            fetch_dn.wait()
+
+    def lamb(master, grad, mean, square):
+        new_mean = 0.5 * mean + 0.5 * grad
+        new_square = 0.5 * square + 0.5 * grad * grad
+        return new_mean, new_square, new_mean / (jnp.sqrt(new_square) + 1e-06) + 0.01 * master
+
+    def sweep(i):
+        down, across, tall, wide = tiles_of(masters[i])
+
+        def body(n, carry):
+            at = tile_at(masters[i], n)
+            master = masters[i][at]
+            new_mean, new_square, step = lamb(master, grads[i][at], means[i][at], squares[i][at])
+            means[i][at] = new_mean
+            squares[i][at] = new_square
+            masters[i][at] = step
+
+            def fold(value):
+                return jnp.sum((value * value).reshape(tall // 8, 8, wide), axis=0)
+
+            return carry[0] + fold(master), carry[1] + fold(step)
+
+        zero = jnp.zeros((8, wide), f32)
+        return lax.fori_loop(0, down * across, body, (zero, zero))
+
+    at_row = lax.broadcasted_iota(jnp.int32, (8, 128), 0)
+    at_lane = lax.broadcasted_iota(jnp.int32, (8, 128), 1)
+
+    def note(sums, i, pair):
+        for row in (0, 1):
+            sums = sums + jnp.where((at_row == row) & (at_lane == i), jnp.sum(pair[row]), 0.0)
+        return sums
+
+    sums = jnp.zeros((8, 128), f32)
+    for i in LAMB_ORDER:
+        make_grad(i)
+        for j in range(3):
+            fetch(i, j).wait()
+        pair = sweep(i)
+        for j in range(4):
+            store(i, j).start()
+        sums = note(sums, i, pair)
+    gain_total = functools.reduce(jnp.add, [gain_tiles[device] for device in range(total)])
+    d_rows, kinds = g_master.shape
+    gain_grad = gain_total.T[:d_rows, :kinds]
+    gain_master = g_master[...]
+    new_mean, new_square, gain_step = lamb(gain_master, gain_grad, g_mean[...], g_square[...])
+    gg_out[...] = gain_grad
+    gm_out[...] = new_mean
+    gs_out[...] = new_square
+    gp_out[...] = gain_step
+    sums_out[...] = note(sums, 5, (gain_master * gain_master, gain_step * gain_step))
+    for i in LAMB_ORDER:
+        for j in range(4):
+            store(i, j).wait()
+
+
+def table_kernel(reps, count, sizes, x_ref, out_ref, near, far, held, n_send, n_recv, f_send, f_recv):
+    f32 = jnp.float32
     rep = lax.axis_index("rep")
     me = lax.axis_index("shard")
-    here = rep * count + me
-    total = reps * count
-    others = everyone(rep, me, reps, count)
-    meet(others)
+    meet(
+        [(rep, (me + k) % count) for k in range(1, count)] + [((rep + k) % reps, me) for k in range(1, reps)]
+    )
     copies = []
-    for k, device in enumerate(others):
-        to = (here + k + 1) % total
-        src = x_ref.at[to] if spread else x_ref
-        copy = remote(src, out_ref.at[here], send.at[k], recv.at[k], device)
+    for k in range(1, count):
+        copies.append(remote(x_ref, near.at[me], n_send.at[k], n_recv.at[k], (rep, (me + k) % count)))
+    for copy in copies:
         copy.start()
-        copies.append(copy)
-    out_ref[here] = x_ref[here] if spread else x_ref[...]
-    for k in range(total - 1):
-        frm = (here + total - k - 1) % total
-        remote(out_ref.at[frm], out_ref.at[frm], send.at[k], recv.at[k], others[k]).wait_recv()
-    for copy in copies:
+    near[me] = x_ref[...]
+    for k in range(1, count):
+        frm = (me + count - k) % count
+        remote(x_ref, near.at[frm], n_send.at[k], n_recv.at[k], (rep, frm)).wait_recv()
+    sums = functools.reduce(jnp.add, [near[shard] for shard in range(count)])
+    held[...] = sums
+    more = []
+    for k in range(1, reps):
+        more.append(remote(held, far.at[rep], f_send.at[k], f_recv.at[k], ((rep + k) % reps, me)))
+    for copy in more:
+        copy.start()
+    far[rep] = sums
+    for k in range(1, reps):
+        frm = (rep + reps - k) % reps
+        remote(held, far.at[frm], f_send.at[k], f_recv.at[k], (frm, me)).wait_recv()
+    totals = functools.reduce(jnp.add, [far[other] for other in range(reps)])
+    at_lane = lax.broadcasted_iota(jnp.int32, (8, 128), 1)
+    counts = jnp.ones((8, 128), f32)
+    for i, size in enumerate(sizes):
+        counts = jnp.where(at_lane == i, float(size), counts)
+    out_ref[...] = jnp.sqrt(totals / counts + 1e-06)
+    for copy in copies + more:
         copy.wait_send()
 
 
-def small_exchange(tiles, reps, count, spread, collective_id):
-    total = reps * count
-    return pl.pallas_call(
-        functools.partial(small_kernel, reps, count, spread),
-        out_shape=jax.ShapeDtypeStruct((total,) + tiles.shape[-2:], tiles.dtype),
-        in_specs=[pl.BlockSpec(memory_space=VM)],
-        out_specs=pl.BlockSpec(memory_space=VM),
-        scratch_shapes=[pltpu.SemaphoreType.DMA((total - 1,)), pltpu.SemaphoreType.DMA((total - 1,))],
-        compiler_params=pltpu.CompilerParams(
-            collective_id=collective_id, has_side_effects=True, vmem_limit_bytes=VMEM_LIMIT
-        ),
-        name=f"small_exchange_{collective_id}",
-    )(tiles)
-
-
-def as_tile(flat):
-    width = flat.shape[-1]
-    filled = -(-width // 1024) * 1024
-    padded = jnp.pad(flat, [(0, 0)] * (flat.ndim - 1) + [(0, filled - width)])
-    return padded.reshape(flat.shape[:-1] + (filled // 128, 128))
-
-
-def turn(flat, cosine, sine):
-    half = flat.shape[1] // 2
-    first, second = flat[:, :half], flat[:, half:]
-    return jnp.concatenate([first * cosine - second * sine, second * cosine + first * sine], axis=1)
-
-
-def norm_back(value, gain_col, grad):
-    scale = lax.rsqrt(jnp.mean(value * value, axis=-1, keepdims=True) + 1e-06)
-    normed = value * scale
-    weighted = grad * (1.0 + gain_col)
-    inner = jnp.mean(weighted * normed, axis=-1, keepdims=True)
-    return scale * (weighted - normed * inner), jnp.sum(grad * normed, axis=0)
-
-
-def dot_tn(left, right):
-    return lax.dot_general(left, right, (((0,), (0,)), ((), ())), preferred_element_type=jnp.float32)
+def fresh_kernel(table_ref, g_master, g_step, *refs):
+    names = 5
+    hbm_in, refs = [refs[2 * i : 2 * i + 2] for i in range(names)], refs[2 * names :]
+    gp_out, refs = refs[0], refs[1:]
+    hbm_out, refs = refs[:names], refs[names:]
+    masters, steps, refs = refs[:names], refs[names : 2 * names], refs[2 * names :]
+    in_sem, out_sem = refs
+
+    def fetch(i, j):
+        return pltpu.make_async_copy(hbm_in[i][j], (masters, steps)[j][i], in_sem.at[i, j])
+
+    def store(i):
+        return pltpu.make_async_copy(masters[i], hbm_out[i], out_sem.at[i])
+
+    for i in LAMB_ORDER:
+        for j in (0, 1):
+            fetch(i, j).start()
+    rate = 0.3 * table_ref[0:1, :] / table_ref[1:2, :]
+    gp_out[...] = g_master[...] - rate[:, 5:6] * g_step[...]
+    for i in LAMB_ORDER:
+        down, across, _, _ = tiles_of(masters[i])
+        scale = rate[:, i : i + 1]
+        for j in (0, 1):
+            fetch(i, j).wait()
+
+        def body(n, carry):
+            at = tile_at(masters[i], n)
+            masters[i][at] = masters[i][at] - scale * steps[i][at]
+            return carry
+
+        lax.fori_loop(0, down * across, body, 0)
+        store(i).start()
+    for i in LAMB_ORDER:
+        store(i).wait()
+
+
+def lamb_step(reps, count, sums, grad_down, gains, states, collective_id):
+    dma = pltpu.SemaphoreType.DMA
+    f32 = jnp.float32
+    shape = jax.ShapeDtypeStruct
+    shapes = [state[0].shape for state in states]
+    like_gains = shape(gains[0].shape, f32)
+    tile = shape((8, 128), f32)
+    vm, hb = pl.BlockSpec(memory_space=VM), pl.BlockSpec(memory_space=HB)
+    local = pltpu.CompilerParams(vmem_limit_bytes=VMEM_LIMIT)
+    outs = pl.pallas_call(
+        functools.partial(lamb_kernel, reps, count),
+        out_shape=[tile] + [like_gains] * 4 + [shape(item, f32) for item in shapes for _ in range(4)],
+        in_specs=[vm] * 7 + [hb] * 16,
+        out_specs=[vm] * 5 + [hb] * 20,
+        scratch_shapes=[pltpu.VMEM(item, f32) for _ in range(4) for item in shapes] + [dma((5, 3)), dma((5, 4)), dma],
+        compiler_params=local,
+        name="lamb_moments",
+    )(*sums, *gains, *[item for state in states for item in state], grad_down)
+    sums, gain_parts, parts = outs[0], outs[1:5], [outs[5 + 4 * i : 9 + 4 * i] for i in range(5)]
+    sizes = [item[0] * item[1] * reps * count for item in shapes + [like_gains.shape]]
+    table = pl.pallas_call(
+        functools.partial(table_kernel, reps, count, sizes),
+        out_shape=tile,
+        in_specs=[vm],
+        out_specs=vm,
+        scratch_shapes=[
+            pltpu.VMEM((count, 8, 128), f32),
+            pltpu.VMEM((reps, 8, 128), f32),
+            pltpu.VMEM((8, 128), f32),
+            dma((count,)),
+            dma((count,)),
+            dma((reps,)),
+            dma((reps,)),
+        ],
+        compiler_params=pltpu.CompilerParams(collective_id=collective_id, has_side_effects=True),
+        name="norm_table",
+    )(sums)
+    fresh = pl.pallas_call(
+        fresh_kernel,
+        out_shape=[like_gains] + [shape(item, f32) for item in shapes],
+        in_specs=[vm] * 3 + [hb] * 10,
+        out_specs=[vm] + [hb] * 5,
+        scratch_shapes=[pltpu.VMEM(item, f32) for _ in range(2) for item in shapes] + [dma((5, 2)), dma((5,))],
+        compiler_params=local,
+        name="lamb_masters",
+    )(table, gains[0], gain_parts[3], *[item for i in range(5) for item in (states[i][0], parts[i][3])])
+    rest = [[parts[i][j] for i in range(5)] + [gain_parts[j]] for j in range(3)]
+    return table[:2, :6], rest[0], rest[1], rest[2], list(fresh[1:]) + [fresh[0]]
 
 
 def split_device(
@@ -1668,7 +1902,6 @@
     freq = 10000.0 ** (-(jnp.arange(half, dtype=f32) * 2.0 / HEAD_DIM))
     angle = position.astype(f32)[:, None] * freq[None, :]
     cosine, sine = jnp.cos(angle), jnp.sin(angle)
-    query_scale = HEAD_DIM ** (-0.5)
     starts = lax.dynamic_slice_in_dim(piece_starts, rep, 1, 0)[0]
     inside = (position[:, None] >= starts[None, :]) & (position[:, None] < starts[None, :] + PIC)
     tag = jnp.sum(inside.astype(jnp.int32) * (jnp.arange(starts.shape[0], dtype=jnp.int32)[None, :] + 1), axis=1)
@@ -1684,59 +1917,31 @@
         reps, count, d_attn, normed_mid, hidden, d_ffn, d_gu, d_rows, 9
     )
     d_attn = d_attn.reshape(seq_len, width)
-    grad_gate, grad_up = join_grads(reps, count, sum_gu)
-    d_attended = back_dot(d_attn, w_out).astype(bf16)
-    d_probs = back_dot(d_attended, values)
-    d_values = dot_tn(probs, d_attended)
-    inner = jnp.sum(probs.astype(f32) * d_probs, axis=-1, keepdims=True)
-    d_scores = (damp.astype(f32) * (d_probs - inner)).astype(bf16)
-    d_queries = jnp.dot(d_scores, keys, preferred_element_type=f32)
-    d_keys = dot_tn(d_scores, queries)
-    d_projected = jnp.concatenate(
-        [turn(d_queries, cosine, -sine) * query_scale, turn(d_keys, cosine, -sine), d_values], axis=1
-    ).astype(bf16)
-    part_in = dot_tn(normed_in, d_projected).astype(bf16).reshape(reps, count, d_rows, 3 * HEAD_DIM)
-    part_out = (
-        dot_tn(attended, d_attn).astype(bf16).reshape(per_head, reps, piece, width).transpose(1, 0, 2, 3)
-    )
     input_grad, sum_in, sum_out, gain_tiles = closing(
-        reps, count, back_dot(d_projected, w_in).astype(bf16), tokens, d_middle, gain_rows, gain_terms,
-        part_in, part_out, 12,
-    )
-    sum_in = sum_in.astype(f32)
-    grad_q = sum_in[:, :, :HEAD_DIM].transpose(1, 0, 2).reshape(d_rows, q_width)
-
-    def join_kv(parts):
-        return parts.reshape(KV_HEADS, group, d_rows, HEAD_DIM).sum(axis=1).transpose(1, 0, 2).reshape(d_rows, k_width)
-
-    grad_inproj = jnp.concatenate(
-        [grad_q, join_kv(sum_in[:, :, HEAD_DIM : 2 * HEAD_DIM]), join_kv(sum_in[:, :, 2 * HEAD_DIM :])], axis=1
-    )
-    grad_outproj = sum_out.reshape(o_rows, width).astype(f32)
-    grad_gains = jnp.sum(gain_tiles, axis=0)[:4, :d_rows].T
-
-    masters = (inproj, outproj, ffn_gate, ffn_up, ffn_down, norm_gains)
-    gradients = (grad_inproj, grad_outproj, grad_gate, grad_up, grad_down, grad_gains)
-    firsts = (mean_inproj, mean_outproj, mean_gate, mean_up, mean_down, mean_gains)
-    seconds = (square_inproj, square_outproj, square_gate, square_up, square_down, square_gains)
-    results = [lamb_local(*item) for item in zip(masters, gradients, firsts, seconds)]
-    sums = jnp.stack(
-        [jnp.sum(master * master) for master in masters] + [jnp.sum(item[2] * item[2]) for item in results]
-    )
-    totals = jnp.sum(small_exchange(as_tile(sums), reps, count, False, 14), axis=0)
-    totals = totals.reshape(-1)[:12].reshape(2, 6)
-    counts = jnp.array([float(master.size * total) for master in masters], f32)
-    norm_table = jnp.sqrt(totals / counts[None, :] + 1e-06)
-    fresh = [
-        masters[index] - 0.3 * norm_table[0, index] / norm_table[1, index] * results[index][2]
-        for index in range(6)
-    ]
+        reps, count, d_attn, normed_in, w_in, w_out, queries, keys, values, attended, probs, damp, cosine, sine,
+        tokens, d_middle, gain_rows, gain_terms, piece, 12,
+    )
+    norm_table, gradients, new_means, new_squares, fresh = lamb_step(
+        reps,
+        count,
+        (sum_in, sum_out, sum_gu, gain_tiles),
+        grad_down,
+        (norm_gains, mean_gains, square_gains),
+        (
+            (inproj, mean_inproj, square_inproj),
+            (outproj, mean_outproj, square_outproj),
+            (ffn_gate, mean_gate, square_gate),
+            (ffn_up, mean_up, square_up),
+            (ffn_down, mean_down, square_down),
+        ),
+        14,
+    )
     return (
         layer_out,
         input_grad,
         *gradients,
-        *[item[0] for item in results],
-        *[item[1] for item in results],
+        *new_means,
+        *new_squares,
         *fresh,
         norm_table,
     )

time: 796 us -> 756 us (0.950)
  Pallas kernels: 677 us -> 731 us
  other arithmetic: 55.8 us -> 7.12 us
  matrix products: 19.3 us -> 0 us
  local copies, waits for them, and re-layouts: 25.3 us -> 12 us
  between operations: 9.21 us -> 1.03 us
    pallas_call x2 -> x3, Pallas kernels: 15.1 us -> 56.1 us  [the longest x1 28 us: lamb_step(): pl.pallas_call(functools.partial(lamb_kernel, reps, count), out_shape=[ti...]
    reduce_sum x9 -> x0, other arithmetic: 27.3 us -> none  [the longest x5 23.9 us: split_device(): jnp.sum(item[2] * item[2])]
    dot_general x8 -> x0, matrix products: 19.3 us -> none  [the longest x3 10.2 us: back_dot(): lax.dot_general(gradient, weight, (((1,), (1,)), ((), ())), preferred_ele...]
    sub x7 -> x0, other arithmetic: 17.2 us -> none  [the longest x6 14.6 us: split_device(): masters[index]]
    pallas_call x1, Pallas kernels: 100 us -> 113 us  [closing(): pl.pallas_call(functools.partial(closing_kernel, reps, count), out_shape=...]
where the time goes in v4:
time: 756 us; the launch traced here: 751 us
  Pallas kernels  731 us (97%)
  local copies, waits for them, and re-layouts  12 us (2%)
    pallas_call x1, Pallas kernels, feed_forward(): pl.pallas_call(functools.partial(ffn_kernel, count), out_shape=[shape((ro...  211 us
    pallas_call x1, Pallas kernels, ffn_grads(): pl.pallas_call(functools.partial(ffn_grads_kernel, reps, count), out_shap...  126 us
    pallas_call x1, Pallas kernels, opening(): pl.pallas_call(functools.partial(opening_kernel, reps, count), out_shape=...  122 us
    pallas_call x1, Pallas kernels, closing(): pl.pallas_call(functools.partial(closing_kernel, reps, count), out_shape=...  113 us
    pallas_call x1, Pallas kernels, attention(): pl.pallas_call(functools.partial(attention_kernel, reps, count), out_shap...  97.6 us
    pallas_call x1, Pallas kernels, lamb_step(): pl.pallas_call(functools.partial(lamb_kernel, reps, count), out_shape=[ti...  28 us

profile of v4, /device:TPU:0, one launch (start us, length us, event | category | flops | bytes accessed | tf_op | source)
XLA Modules:
  0.0 751.2 jit_solution(7422095178548472702)
XLA Ops:
  0.7 0.9 dynamic-slice_reduce_fusion
  1.6 0.1 fusion
  1.7 0.0 copy-start.4
  1.7 1.0 copy.68.tagq_ref
  2.7 0.0 copy-start
  2.7 5.6 cut_weights.1
  8.3 0.0 copy-done.4
  8.3 0.0 copy-start.1
  8.3 0.0 copy-start.8
  8.3 0.0 copy-done
  8.3 1.2 convert_element_type.27.dn_ref
  9.5 0.0 copy-done.1
  9.5 0.7 convert_element_type.28
  10.2 0.0 copy-done.8
  10.2 0.6 pad_convert_fusion.gain_ref
  10.8 122.0 %opening.1 = (bf16[8,128,2304]{2,1,0:T(8,128)(2,1)}, f32[8,2304]{1,0:T(8,128)}, bf16[4,8,72,768]{3,2,1,0:T(8,128)(2,1)}, bf16[4,8,72,1152]{3,2,1,0:T(8,128)(2,1)...) custom-call(bf16[128,2304]{1,0:T(8,128)(2,1)} %tokens_ref.3, f32[8,128]{1,0:T(8,128)} %pad_convert_fusion.gain_ref, ...), custom_call_target="tpu_custom_call" | custom-call | tf_op jit(solution)/shard_map/opening/pallas_call | solution.py:1033
  132.8 2.4 copy.67
  135.2 3.6 multiply_sine_fusion
  138.8 97.6 %attention.1 = (f32[128,2304]{1,0:T(8,128)}, bf16[1024,256]{1,0:T(8,128)(2,1)}, bf16[1024,256]{1,0:T(8,128)(2,1)}, bf16[1024,256]{1,0:T(8,128)(2,1)}, bf16[1024,...) custom-call(bf16[1024,2304]{1,0:T(8,128)(2,1)} %bitcast.13, ...), custom_call_target="tpu_custom_call" | custom-call | tf_op jit(solution)/shard_map/attention/pallas_call | solution.py:793
  236.4 211.2 %feed_forward.1 = (bf16[128,2304]{1,0:T(8,128)(2,1)}, f32[128,2304]{1,0:T(8,128)}, bf16[128,2304]{1,0:T(8,128)(2,1)}, f32[8,2304]{1,0:T(8,128)}, bf16[1024,2304]...) custom-call(f32[128,2304]{1,0:T(8,128)} %get-tuple-element.96.attn_ref, ...), custom_call_target="tpu_custom_call" | custom-call | tf_op jit(solution)/shard_map/feed_forward/pallas_call | solution.py:679
  447.6 126.0 %ffn_grads.1 = (bf16[8,128,2304]{2,1,0:T(8,128)(2,1)}, bf16[8,72,2304]{2,1,0:T(8,128)(2,1)}, f32[288,2304]{1,0:T(8,128)}) custom-call(bf16[128,2304]{1,0:T(8,128)(2,1)} %get-tuple-element.102.dattn_ref, bf16[1024,2304]{1,0:T(8,128)(2,1)} %get-tuple-element.103.h3_ref, bf16[1024,1152]{1,0:T(8,128)(2,1)} %get-tuple-element.104.hid_ref, ...), custom_call_target="tpu_custom_call" | custom-call | tf_op jit(solution)/shard_map/ffn_grads/pallas_call | solution.py:1337
  573.6 0.0 copy-start.9
  573.6 0.0 copy-start.10
  573.7 112.6 %closing.1 = (f32[128,2304]{1,0:T(8,128)}, bf16[8,72,768]{2,1,0:T(8,128)(2,1)}, bf16[4,16,2304]{2,1,0:T(8,128)(2,1)}, f32[32,8,128]{2,1,0:T(8,128)}) custom-call(bf16[1024,2304]{1,0:T(8,128)(2,1)} %bitcast.22, bf16[1024,2304]{1,0:T(8,128)(2,1)} %bitcast.14, bf16[2304,768]{1,0:T(8,128)(2,1)} %bitcast.16, bf16[256,2304]{1,0:T(8,128)(2,1)} %bitcast.18, ...), custom_call_target="tpu_custom_call" | custom-call | tf_op jit(solution)/shard_map/closing/pallas_call | solution.py:1562
  686.2 0.7 copy.69.g_master
  686.9 0.0 copy-done.9
  686.9 0.7 copy.70.g_mean
  687.7 0.0 copy-done.10
  687.7 0.7 copy.71.g_square
  688.4 28.0 %lamb_moments.1 = (f32[8,128]{1,0:T(8,128)}, f32[72,4]{1,0:T(8,128)}, f32[72,4]{1,0:T(8,128)}, f32[72,4]{1,0:T(8,128)}, f32[72,4]{1,0:T(8,128)}, /*index=5*/f32[...) custom-call(bf16[8,72,768]{2,1,0:T(8,128)(2,1)} %get-tuple-element.1, ...), custom_call_target="tpu_custom_call" | custom-call | tf_op jit(solution)/shard_map/lamb_moments/pallas_call | solution.py:1825
  716.4 13.5 %norm_table.1.table_ref = f32[8,128]{1,0:T(8,128)} custom-call(f32[8,128]{1,0:T(8,128)} %get-tuple-element.140.x_ref), custom_call_target="tpu_custom_call" | custom-call | tf_op jit(solution)/shard_map/norm_table/pallas_call | solution.py:1836
  729.9 0.0 copy-start.7
  729.9 0.0 copy-start.6
  729.9 0.0 copy-start.5
  729.9 0.0 copy-start.3
  729.9 0.0 copy-start.2
  729.9 14.6 %lamb_masters.1 = (f32[72,4]{1,0:T(8,128)}, f32[72,4096]{1,0:T(8,128)}, f32[64,2304]{1,0:T(8,128)}, f32[72,9216]{1,0:T(8,128)}, f32[72,9216]{1,0:T(8,128)}, /*index=5*/f32[288,2304]{1,0:T(8,128)}) custom-call(f32[8,128]{1,0:T(8,128)} %norm_table.1.table_ref, f32[72,4]{1,0:T(8,128)} %copy.69.g_master, f32[72,4]{1,0:T(8,128)} %get-tuple-element.141.g_step, ...), custom_call_target="tpu_custom_call" | custom-call | tf_op jit(solution)/shard_map/lamb_masters/pallas_call | solution.py:1853
  744.5 1.4 copy.76
  746.0 1.2 slice.3
  747.2 0.0 copy-done.7
  747.2 0.7 copy.73
  747.9 0.0 copy-done.6
  747.9 0.7 copy.74
  748.5 0.0 copy-done.5
  748.5 0.7 copy.75
  749.2 0.0 copy-done.3
  749.2 0.8 copy.79
  750.0 0.0 copy-done.2
  750.0 1.0 copy.80
  (4 shorter events, 0.0 us)
Async XLA Ops:
  1.7 6.6 copy-start.4
  2.7 5.6 copy-start
  8.3 1.2 copy-start.1
  8.3 2.0 copy-start.8
  573.6 113.3 %copy-start.9 = (f32[72,4]{0,1:T(4,128)S(1)}, f32[72,4]{0,1:T(4,128)}, u32[]{:S(2)}) copy-start(f32[72,4]{0,1:T(4,128)} %param.35) | copy-start | bytes 3460
  573.6 114.0 %copy-start.10 = (f32[72,4]{0,1:T(4,128)S(1)}, f32[72,4]{0,1:T(4,128)}, u32[]{:S(2)}) copy-start(f32[72,4]{0,1:T(4,128)} %param.41) | copy-start | bytes 3460
  729.9 17.3 %copy-start.7 = (f32[72,4]{1,0:T(8,128)S(1)}, f32[72,4]{1,0:T(8,128)}, u32[]{:S(2)}) copy-start(f32[72,4]{1,0:T(8,128)} %get-tuple-element.214) | copy-start | bytes 3460
  729.9 18.0 %copy-start.6 = (f32[72,4]{1,0:T(8,128)S(1)}, f32[72,4]{1,0:T(8,128)}, u32[]{:S(2)}) copy-start(f32[72,4]{1,0:T(8,128)} %get-tuple-element.220) | copy-start | bytes 3460
  729.9 18.6 %copy-start.5 = (f32[72,4]{1,0:T(8,128)S(1)}, f32[72,4]{1,0:T(8,128)}, u32[]{:S(2)}) copy-start(f32[72,4]{1,0:T(8,128)} %get-tuple-element.226) | copy-start | bytes 3460
  729.9 19.2 %copy-start.3 = (bf16[128,2304]{1,0:T(8,128)(2,1)S(1)}, bf16[128,2304]{1,0:T(8,128)(2,1)}, u32[]{:S(2)}) copy-start(bf16[128,2304]{1,0:T(8,128)(2,1)} %get-tuple-element.265) | copy-start | bytes 1769476
  729.9 20.1 %copy-start.2 = (f32[128,2304]{1,0:T(8,128)S(1)}, f32[128,2304]{1,0:T(8,128)}, u32[]{:S(2)}) copy-start(f32[128,2304]{1,0:T(8,128)} %get-tuple-element.266) | copy-start | bytes 3538948

commit v5 on v4

--- a/solution.py
+++ b/solution.py
@@ -5,6 +5,7 @@
 from jax import lax
 from jax.experimental import pallas as pl
 from jax.experimental.pallas import tpu as pltpu
+import numpy as np
 from jax.sharding import PartitionSpec as P
 
 HEADS = 8
@@ -483,7 +484,8 @@
             self.ring.next[way],
         )
 
-    def reduce(self, first, landed, partial, group_work, finish):
+    def reduce(self, first, landed, partial, group_work, finish, extra=()):
+        extra = list(extra)
         ring = self.ring
         hops = ring.half
         f32 = jnp.float32
@@ -511,12 +513,16 @@
                     self.go(self.reduce_copy(first, landed, way, step, unit))
                 if queue:
                     queue.pop(0)()
+                elif extra:
+                    extra.pop(0)()
             for piece in queue:
                 piece()
             ahead = hops - step - 2
             queue = []
             if step < hops - 1:
                 queue = list(group_work(2 * ahead - 1, 2, step % 2) if ahead > 0 else group_work(0, 1, step % 2))
+        for piece in extra:
+            piece()
         for unit in range(UNITS):
             span = pl.ds(unit * self.unit_rows, self.unit_rows)
             total = partial[hops % 2, span, :]
@@ -549,9 +555,10 @@
 
 
 def ffn_kernel(
-    count, attn_ref, tokens_ref, cot_ref, gains_ref, gate_ref, up_ref, dn_ref,
-    layer_ref, dmid_ref, dattn_ref, gg_ref, h3_ref, hid_ref, dffn_ref, dgu_ref,
-    lin, partial, first, landed, middle, total_ref, s1, r1, s2, r2, s3, r3, s4, r4,
+    count, attn_ref, tokens_ref, cot_ref, gains_ref, gate_hbm, up_hbm, dn_hbm,
+    layer_ref, dmid_ref, dattn_ref, gg_ref, h3_hbm, dgu_hbm, part_hbm,
+    gate_ref, up_ref, dn_ref, h3_ref, hid_ref, dffn_ref, dgu_ref,
+    lin, partial, first, landed, middle, total_ref, s1, r1, s2, r2, s3, r3, s4, r4, loads, stores,
 ):
     f32, bf16 = jnp.float32, jnp.bfloat16
     ring = Ring(count)
@@ -559,6 +566,19 @@
     part = hid_ref.shape[1]
     tile = part // 3
     wide = width // 3
+    fetched = [
+        pltpu.make_async_copy(src, dst, loads.at[index])
+        for index, (src, dst) in enumerate(((gate_hbm, gate_ref), (up_hbm, up_ref), (dn_hbm, dn_ref)))
+    ]
+    for copy in fetched:
+        copy.start()
+    kept = []
+
+    def keep_out(src, dst):
+        copy = pltpu.make_async_copy(src, dst, stores.at[len(kept)])
+        copy.start()
+        kept.append(copy)
+
     meet(ring.next)
 
     def gain(index):
@@ -630,7 +650,13 @@
     def keep(unit, total):
         total_ref[pl.ds(unit * (rows // UNITS), rows // UNITS), :] = total
 
-    Flow(ring, rows, s1, r1).gather(h3_ref, lin_work)
+    def lin_first(slot, blocks):
+        work = lin_work(slot, blocks)
+        return [lambda: (fetched[0].wait(), fetched[1].wait())] + work if slot == 0 else work
+
+    Flow(ring, rows, s1, r1).gather(h3_ref, lin_first)
+    keep_out(h3_ref, h3_hbm)
+    fetched[2].wait()
     Flow(ring, rows, s2, r2).reduce(first, landed, partial, down_work, keep)
 
     def back_norm(value, index, grad):
@@ -651,7 +677,22 @@
     gg_ref[3:4, :] = gg
 
     Flow(ring, rows, s3, r3).gather(dffn_ref, back_work)
-    Flow(ring, rows, s4, r4).reduce(first, landed, partial, input_work, keep)
+    keep_out(dgu_ref, dgu_hbm)
+
+    def make_down(j):
+        span = pl.ds(j * tile, tile)
+
+        def body(n, carry):
+            cols = pl.ds(pl.multiple_of(n * wide, 128), wide)
+            lin[span, cols] = tn(hid_ref[:, span], dffn_ref[:, cols]).astype(bf16)
+            return carry
+
+        lax.fori_loop(0, 3, body, 0)
+        keep_out(lin.at[span, pl.ds(0, width)], part_hbm.at[span])
+
+    Flow(ring, rows, s4, r4).reduce(
+        first, landed, partial, input_work, keep, [functools.partial(make_down, j) for j in range(3)]
+    )
 
     gg1 = jnp.zeros((1, width), f32)
     gg2 = jnp.zeros((1, width), f32)
@@ -667,6 +708,8 @@
     gg_ref[2:3, :] = gg2
     gg_ref[0:1, :] = jnp.zeros((1, width), f32)
     gg_ref[4:8, :] = jnp.zeros((4, width), f32)
+    for copy in kept:
+        copy.wait()
 
 
 def feed_forward(attn_proj, tokens, cotangent, gain_rows, w_gate, w_up, w_down, count, collective_id):
@@ -684,21 +727,28 @@
             shape((rows, width), bf16),
             shape((8, width), f32),
             shape((every, width), bf16),
-            shape((every, part), bf16),
-            shape((every, width), bf16),
             shape((every, 2 * part), bf16),
+            shape((part, width), bf16),
         ],
-        in_specs=[pl.BlockSpec(memory_space=VM)] * 7,
-        out_specs=[pl.BlockSpec(memory_space=VM)] * 8,
+        in_specs=[pl.BlockSpec(memory_space=VM)] * 4 + [pl.BlockSpec(memory_space=HB)] * 3,
+        out_specs=[pl.BlockSpec(memory_space=VM)] * 4 + [pl.BlockSpec(memory_space=HB)] * 3,
         scratch_shapes=[
+            pltpu.VMEM(w_gate.shape, bf16),
+            pltpu.VMEM(w_up.shape, bf16),
+            pltpu.VMEM(w_down.shape, bf16),
+            pltpu.VMEM((every, width), bf16),
+            pltpu.VMEM((every, part), bf16),
+            pltpu.VMEM((every, width), bf16),
             pltpu.VMEM((every, 2 * part), bf16),
+            pltpu.VMEM((max(every, part), max(2 * part, width)), bf16),
             pltpu.VMEM((2, 2 * rows, width), f32),
             pltpu.VMEM((rows, width), bf16),
             pltpu.VMEM((2, count // 2, rows, width), bf16),
             pltpu.VMEM((rows, width), f32),
             pltpu.VMEM((rows, width), f32),
         ]
-        + [dma((2, count // 2, UNITS))] * 8,
+        + [dma((2, count // 2, UNITS))] * 8
+        + [dma((3,)), dma((5,))],
         compiler_params=pltpu.CompilerParams(
             collective_id=collective_id, has_side_effects=True, vmem_limit_bytes=VMEM_LIMIT
         ),
@@ -707,8 +757,8 @@
 
 
 def attention_kernel(
-    reps, count, h1_ref, in_ref, wo_ref, cos_ref, sin_ref, tagq_ref, tagk_ref, cut_ref,
-    proj_ref, q_ref, k_ref, v_ref, att_ref, probs_ref, damp_ref, up_ref,
+    reps, count, h1_ref, in_ref, got_ref, cos_ref, sin_ref, tagq_ref, tagk_ref, cut_ref,
+    proj_ref, q_ref, k_ref, v_ref, att_ref, probs_ref, damp_ref, wo_ref, up_ref,
     part, first, landed, r_send, r_recv, w_sems, loc
 ):
     f32, bf16 = jnp.float32, jnp.bfloat16
@@ -722,6 +772,11 @@
     weights.begin()
     own = pltpu.make_async_copy(cut_ref.at[ring.me], up_ref.at[ring.rep, ring.me], loc)
     own.start()
+    piece = got_ref.shape[2]
+    for block in range(got_ref.shape[1]):
+        for j in range(reps):
+            start = (block * reps + j) * piece
+            wo_ref[start : start + piece, :] = got_ref[j, block]
 
     def project(i, carry):
         at = pl.ds(pl.multiple_of(i * tall, 16), tall)
@@ -793,11 +848,11 @@
     return pl.pallas_call(
         functools.partial(attention_kernel, reps, count),
         out_shape=[
-            shape((rows, width), f32), head, head, head, head, square, square,
+            shape((rows, width), f32), head, head, head, head, square, square, shape((HEAD_DIM, width), low),
             shape((reps,) + cut_up.shape, low),
         ],
         in_specs=[pl.BlockSpec(memory_space=VM)] * 7 + [pl.BlockSpec(memory_space=HB)],
-        out_specs=[pl.BlockSpec(memory_space=VM)] * 7 + [pl.BlockSpec(memory_space=HB)],
+        out_specs=[pl.BlockSpec(memory_space=VM)] * 8 + [pl.BlockSpec(memory_space=HB)],
         scratch_shapes=[
             pltpu.VMEM((seq_len, width), f32),
             pltpu.VMEM((rows, width), low),
@@ -1097,9 +1152,8 @@
 
 
 class RepSum:
-    def __init__(self, part, from_core, to_across, from_across, sems, rep, me):
-        self.part, self.from_core = part, from_core
-        self.to_across, self.from_across = to_across, from_across
+    def __init__(self, part, from_core, from_across, sems, rep, me):
+        self.part, self.from_core, self.from_across = part, from_core, from_across
         self.c_send, self.c_recv, self.x_send, self.x_recv = sems
         self.across, self.beside = rep_partners(rep)
         self.rep, self.me = rep, me
@@ -1118,7 +1172,7 @@
 
     def cross_copy(self, piece):
         return remote(
-            self.to_across.at[piece],
+            self.from_core.at[0, piece],
             self.from_across.at[piece],
             self.x_send.at[piece],
             self.x_recv.at[piece],
@@ -1134,7 +1188,7 @@
         f32 = jnp.float32
         self.core_copy(0, piece).wait_recv()
         mine = self.part((1 - self.chip) * 2 + self.core, piece)[...].astype(f32)
-        self.to_across[piece] = (mine + self.from_core[0, piece].astype(f32)).astype(jnp.bfloat16)
+        self.from_core[0, piece] = (mine + self.from_core[0, piece].astype(f32)).astype(jnp.bfloat16)
         self.cross_copy(piece).start()
 
     def total(self, piece):
@@ -1239,18 +1293,37 @@
 
 
 def ffn_grads_kernel(
-    reps, count, dattn_ref, h3_ref, hid_ref, dffn_ref, dgu_ref, all_ref, sum_ref, down_ref,
-    g_part, g_core, g_to, g_from, d_part, d_core, d_to, d_from,
-    t_send, t_recv, gc_s, gc_r, gx_s, gx_r, dc_s, dc_r, dx_s, dx_r, s_send, s_recv, loc
+    reps, count, dattn_ref, wo_ref, q_ref, k_ref, v_ref, cos_ref, sin_ref, h3_hbm, dgu_hbm, part_hbm, probs_hbm, damp_hbm,
+    all_ref, sum_ref, down_ref, dproj,
+    h3_ref, dgu_ref, g_part, g_core, g_from, d_part, d_core, d_from, probs_ref, damp_ref, d_key, d_value,
+    t_send, t_recv, gc_s, gc_r, gx_s, gx_r, dc_s, dc_r, dx_s, dx_r, s_send, s_recv, loc, loads, square
 ):
-    bf16 = jnp.bfloat16
+    f32, bf16 = jnp.float32, jnp.bfloat16
     ring = Ring(count)
     rep, me = ring.rep, ring.me
     d_rows, columns = sum_ref.shape[1:]
     part, width = d_part.shape
     block = part // reps
-    wide = width // 3
-    tall = part // 3
+    seq_len = q_ref.shape[0]
+    blocks = 4
+    tall = seq_len // blocks
+    half = HEAD_DIM // 2
+    fetched = [
+        pltpu.make_async_copy(src, dst, loads.at[index])
+        for index, (src, dst) in enumerate(((part_hbm, d_part), (h3_hbm, h3_ref), (dgu_hbm, dgu_ref)))
+    ]
+    for copy in fetched:
+        copy.start()
+
+    def squares(i):
+        span = pl.ds(i * tall, tall)
+        return [
+            pltpu.make_async_copy(probs_hbm.at[span], probs_ref, square.at[0]),
+            pltpu.make_async_copy(damp_hbm.at[span], damp_ref, square.at[1]),
+        ]
+
+    for copy in squares(0):
+        copy.start()
     meet(near_devices(ring))
     gather = Gather(ring, dattn_ref, all_ref, t_send, t_recv)
     gather.begin()
@@ -1261,23 +1334,13 @@
         rows = block // DN_PIECES
         return d_part.at[pl.ds(owner * block + piece * rows, rows)]
 
-    down = RepSum(d_at, d_core, d_to, d_from, (dc_s, dc_r, dx_s, dx_r), rep, me)
+    down = RepSum(d_at, d_core, d_from, (dc_s, dc_r, dx_s, dx_r), rep, me)
     gate_up = RepSum(
-        lambda owner, piece: g_part.at[owner, piece], g_core, g_to, g_from, (gc_s, gc_r, gx_s, gx_r), rep, me
+        lambda owner, piece: g_part.at[owner, piece], g_core, g_from, (gc_s, gc_r, gx_s, gx_r), rep, me
     )
     spread = Spread(g_from, sum_ref, s_send, s_recv, rep, me, count)
     d_pieces = list(range(DN_PIECES))
     g_pieces = [(me + k) % count for k in range(1, count)] + [me]
-
-    def make_down(j):
-        def body(n, carry):
-            cols = pl.ds(pl.multiple_of(n * wide, 128), wide)
-            d_part[j * tall : (j + 1) * tall, cols] = tn(
-                hid_ref[:, j * tall : (j + 1) * tall], dffn_ref[:, cols]
-            ).astype(bf16)
-            return carry
-
-        lax.fori_loop(0, 3, body, 0)
 
     def make_gate_up(owner):
         rows = count * d_rows
@@ -1291,67 +1354,126 @@
 
         lax.fori_loop(0, 3, body, 0)
 
-    work = [functools.partial(make_down, j) for j in range(3)]
-    work.append(lambda: down.begin(d_pieces))
-    work.append(functools.partial(make_gate_up, 0))
-    work.append(lambda: [down.cross(piece) for piece in d_pieces])
-    work += [functools.partial(make_gate_up, owner) for owner in range(1, reps)]
-    work.append(lambda: gate_up.begin(g_pieces))
-    steps = gather.steps()
-    for step in steps:
-        step()
-        if work:
-            work.pop(0)()
-    for piece in work:
-        piece()
-    for piece in g_pieces:
-        gate_up.cross(piece)
-    for piece in d_pieces:
-        rows = block // DN_PIECES
-        down_ref[pl.ds(piece * rows, rows), :] = down.total(piece)
-    for k, piece in enumerate(g_pieces):
+    def nt(left, right):
+        return lax.dot_general(left, right, (((1,), (1,)), ((), ())), preferred_element_type=f32)
+
+    def unturned(flat, at):
+        cosine, sine = cos_ref[at, :], sin_ref[at, :]
+        low, high = flat[:, :half], flat[:, half:]
+        return jnp.concatenate([low * cosine + high * sine, high * cosine - low * sine], axis=1)
+
+    d_key[...] = jnp.zeros_like(d_key)
+    d_value[...] = jnp.zeros_like(d_value)
+
+    def attend(i):
+        at = pl.ds(i * tall, tall)
+        per = count // blocks
+        d_out = all_ref[i * per : (i + 1) * per].reshape(tall, width)
+        d_att = nt(d_out, wo_ref[...]).astype(bf16)
+        d_probs = nt(d_att, v_ref[...])
+        for copy in squares(i):
+            copy.wait()
+        probs = probs_ref[...]
+        inner = jnp.sum(probs.astype(f32) * d_probs, axis=-1, keepdims=True)
+        d_scores = (damp_ref[...].astype(f32) * (d_probs - inner)).astype(bf16)
+        d_query = jnp.dot(d_scores, k_ref[...], preferred_element_type=f32)
+        dproj[at, :HEAD_DIM] = (unturned(d_query, at) * HEAD_DIM ** (-0.5)).astype(bf16)
+        d_key[...] += tn(d_scores, q_ref[at, :])
+        d_value[...] += tn(probs, d_att)
+        if i < blocks - 1:
+            for copy in squares(i + 1):
+                copy.start()
+
+    def project():
+        for i in range(blocks):
+            at = pl.ds(i * tall, tall)
+            dproj[at, HEAD_DIM : 2 * HEAD_DIM] = unturned(d_key[at, :], at).astype(bf16)
+            dproj[at, 2 * HEAD_DIM :] = d_value[at, :].astype(bf16)
+
+    def finish_gate_up(k):
+        piece = g_pieces[k]
         total = gate_up.total(piece).astype(bf16)
         if k < count - 1:
             g_from[piece] = total
             spread.copy(k + 1).start()
         else:
             sum_ref[me] = total
+
+    def finish_down(piece):
+        rows = block // DN_PIECES
+        down_ref[pl.ds(piece * rows, rows), :] = down.total(piece)
+
+    fetched[0].wait()
+    down.begin(d_pieces)
+    for copy in fetched[1:]:
+        copy.wait()
+    work = [functools.partial(make_gate_up, 0)]
+    work += [functools.partial(down.cross, piece) for piece in d_pieces]
+    work += [functools.partial(make_gate_up, owner) for owner in range(1, reps)]
+    work += [lambda: gate_up.begin(g_pieces)]
+    work += [functools.partial(gate_up.cross, piece) for piece in g_pieces]
+    for step in gather.steps():
+        step()
+        if work:
+            work.pop(0)()
+    for piece in work:
+        piece()
+    own.wait()
+    after = [functools.partial(finish_gate_up, k) for k in range(count)]
+    per = max(1, count // blocks)
+    for i in range(blocks):
+        attend(i)
+        for _ in range(min(per, len(after) - 2)):
+            after.pop(0)()
+    project()
+    for piece in d_pieces:
+        finish_down(piece)
+    for piece in after:
+        piece()
     spread.finish()
     down.finish(d_pieces)
     gate_up.finish(g_pieces)
     gather.finish()
-    own.wait()
-
-
-def ffn_grads(reps, count, d_attn, h3, hidden, d_ffn, d_gu, d_rows, collective_id):
+
+
+def ffn_grads(
+    reps, count, d_attn, w_out, queries, keys, values, cosine, sine, h3, d_gu, part_down, probs, damp, d_rows, collective_id
+):
     dma = pltpu.SemaphoreType.DMA
-    low = jnp.bfloat16
+    low, f32 = jnp.bfloat16, jnp.float32
     shape = jax.ShapeDtypeStruct
     width = d_attn.shape[1]
     columns = d_gu.shape[1]
-    part = hidden.shape[1]
+    part = part_down.shape[0]
+    seq_len = h3.shape[0]
     block = part // reps
     blocks = (count, d_rows, columns)
     lots = (DN_PIECES, block // DN_PIECES, width)
     hops = dma((2, count // 2, UNITS))
+    vm, hb = pl.BlockSpec(memory_space=VM), pl.BlockSpec(memory_space=HB)
     return pl.pallas_call(
         functools.partial(ffn_grads_kernel, reps, count),
         out_shape=[
             shape((count,) + d_attn.shape, low),
             shape(blocks, low),
-            shape((block, width), jnp.float32),
+            shape((block, width), f32),
+            shape((seq_len, 3 * HEAD_DIM), low),
         ],
-        in_specs=[pl.BlockSpec(memory_space=VM)] * 5,
-        out_specs=[pl.BlockSpec(memory_space=HB)] + [pl.BlockSpec(memory_space=VM)] * 2,
+        in_specs=[vm] * 7 + [hb] * 5,
+        out_specs=[vm] * 4,
         scratch_shapes=[
+            pltpu.VMEM(h3.shape, low),
+            pltpu.VMEM(d_gu.shape, low),
             pltpu.VMEM((reps,) + blocks, low),
             pltpu.VMEM((2,) + blocks, low),
-            pltpu.VMEM(blocks, low),
             pltpu.VMEM(blocks, low),
             pltpu.VMEM((part, width), low),
             pltpu.VMEM((2,) + lots, low),
             pltpu.VMEM(lots, low),
-            pltpu.VMEM(lots, low),
+            pltpu.VMEM((seq_len // 4, seq_len), low),
+            pltpu.VMEM((seq_len // 4, seq_len), low),
+            pltpu.VMEM((seq_len, HEAD_DIM), f32),
+            pltpu.VMEM((seq_len, HEAD_DIM), f32),
             hops,
             hops,
             dma((2, count)),
@@ -1365,21 +1487,22 @@
             dma((count,)),
             dma((count,)),
             dma,
+            dma((3,)),
+            dma((2,)),
         ],
         compiler_params=pltpu.CompilerParams(
             collective_id=collective_id, has_side_effects=True, vmem_limit_bytes=VMEM_LIMIT
         ),
         name="ffn_grads",
-    )(d_attn, h3, hidden, d_ffn, d_gu)
+    )(d_attn, w_out, queries, keys, values, cosine, sine, h3, d_gu, part_down, probs, damp)
 
 
 def closing_kernel(
-    reps, count, dattn_ref, h1_ref, in_ref, wo_ref, q_ref, k_ref, v_ref, att_ref, probs_ref, damp_ref, cos_ref, sin_ref,
-    tokens_ref, dmid_ref, gains_ref, gg_ref, grad_ref, sum_ref, out_ref, gain_ref,
-    x_part, dproj, d_key, d_value, i_part, o_part, first, landed, total_ref, tiles, i_core, i_to, i_from,
-    o_core, o_to, o_from,
+    reps, count, dproj, in_ref, att_ref, h1_hbm, dattn_hbm, tokens_ref, dmid_ref, gains_ref, gg_ref,
+    grad_ref, sum_ref, out_ref, gain_ref,
+    h1_ref, dattn_ref, x_part, i_part, o_part, first, landed, total_ref, tiles, i_core, i_from, o_core, o_from,
     r_send, r_recv, ic_s, ic_r, ix_s, ix_r, oc_s, oc_r, ox_s, ox_r, s_send, s_recv, p_send, p_recv,
-    g_send, g_recv
+    g_send, g_recv, loads
 ):
     f32, bf16 = jnp.float32, jnp.bfloat16
     ring = Ring(count)
@@ -1390,46 +1513,26 @@
     d_rows = sum_ref.shape[1]
     seq_len, width = dattn_ref.shape
     rows = grad_ref.shape[0]
-    half = HEAD_DIM // 2
+    fetched = [
+        pltpu.make_async_copy(h1_hbm, h1_ref, loads.at[0]),
+        pltpu.make_async_copy(dattn_hbm, dattn_ref, loads.at[1]),
+    ]
+    for copy in fetched:
+        copy.start()
     meet(others)
-
-    def nt(left, right):
-        return lax.dot_general(left, right, (((1,), (1,)), ((), ())), preferred_element_type=f32)
-
-    def unturned(flat, at):
-        cosine, sine = cos_ref[at, :], sin_ref[at, :]
-        low, high = flat[:, :half], flat[:, half:]
-        return jnp.concatenate([low * cosine + high * sine, high * cosine - low * sine], axis=1)
-
     tall = seq_len // 4
-    d_key[...] = jnp.zeros_like(d_key)
-    d_value[...] = jnp.zeros_like(d_value)
-
-    def attend(i, carry):
-        at = pl.ds(pl.multiple_of(i * tall, 16), tall)
-        d_att = nt(dattn_ref[at, :], wo_ref[...]).astype(bf16)
-        d_probs = nt(d_att, v_ref[...])
-        probs = probs_ref[at, :]
-        inner = jnp.sum(probs.astype(f32) * d_probs, axis=-1, keepdims=True)
-        d_scores = (damp_ref[at, :].astype(f32) * (d_probs - inner)).astype(bf16)
-        d_query = jnp.dot(d_scores, k_ref[...], preferred_element_type=f32)
-        dproj[at, :HEAD_DIM] = (unturned(d_query, at) * HEAD_DIM ** (-0.5)).astype(bf16)
-        d_key[...] += tn(d_scores, q_ref[at, :])
-        d_value[...] += tn(probs, d_att)
-        return carry
-
-    lax.fori_loop(0, 4, attend, 0)
 
     def project(i, carry):
         at = pl.ds(pl.multiple_of(i * tall, 16), tall)
-        dproj[at, HEAD_DIM : 2 * HEAD_DIM] = unturned(d_key[at, :], at).astype(bf16)
-        dproj[at, 2 * HEAD_DIM :] = d_value[at, :].astype(bf16)
-        x_part[at, :] = nt(dproj[at, :], in_ref[...]).astype(bf16)
+        x_part[at, :] = lax.dot_general(
+            dproj[at, :], in_ref[...], (((1,), (1,)), ((), ())), preferred_element_type=f32
+        ).astype(bf16)
         return carry
 
     lax.fori_loop(0, 4, project, 0)
 
     def make_out():
+        fetched[1].wait()
         per = width // 3
 
         def body(n, carry):
@@ -1442,14 +1545,16 @@
         lax.fori_loop(0, 3, body, 0)
 
     def make_in(owner):
+        if owner == 0:
+            fetched[0].wait()
         deep = count * d_rows
         made = tn(h1_ref[:, owner * deep : (owner + 1) * deep], dproj[...])
         i_part[owner] = made.reshape(count, d_rows, 3 * HEAD_DIM).astype(bf16)
 
     o_pieces = list(range(full))
     i_pieces = [(me + k) % count for k in range(1, count)] + [me]
-    ins = RepSum(lambda owner, piece: i_part.at[owner, piece], i_core, i_to, i_from, (ic_s, ic_r, ix_s, ix_r), rep, me)
-    outs = RepSum(lambda owner, piece: o_part.at[owner, piece], o_core, o_to, o_from, (oc_s, oc_r, ox_s, ox_r), rep, me)
+    ins = RepSum(lambda owner, piece: i_part.at[owner, piece], i_core, i_from, (ic_s, ic_r, ix_s, ix_r), rep, me)
+    outs = RepSum(lambda owner, piece: o_part.at[owner, piece], o_core, o_from, (oc_s, oc_r, ox_s, ox_r), rep, me)
     spread = Spread(i_from, sum_ref, s_send, s_recv, rep, me, count)
 
     def o_owner(piece):
@@ -1544,8 +1649,7 @@
 
 
 def closing(
-    reps, count, d_attn, normed, w_in, w_out, queries, keys, values, attended, probs, damp, cosine, sine,
-    tokens, d_middle, gain_rows, gain_terms, piece, collective_id
+    reps, count, d_projected, w_in, attended, normed, d_attn, tokens, d_middle, gain_rows, gain_terms, piece, collective_id
 ):
     dma = pltpu.SemaphoreType.DMA
     low, f32 = jnp.bfloat16, jnp.float32
@@ -1559,6 +1663,7 @@
     i_block = (count, d_rows, 3 * HEAD_DIM)
     o_block = (full, piece, width)
     hops = dma((2, half, UNITS))
+    vm, hb = pl.BlockSpec(memory_space=VM), pl.BlockSpec(memory_space=HB)
     return pl.pallas_call(
         functools.partial(closing_kernel, reps, count),
         out_shape=[
@@ -1567,13 +1672,12 @@
             shape((reps, piece, width), low),
             shape((total, 8, 128), f32),
         ],
-        in_specs=[pl.BlockSpec(memory_space=VM)] * 16,
-        out_specs=[pl.BlockSpec(memory_space=VM)] * 4,
+        in_specs=[vm] * 3 + [hb] * 2 + [vm] * 4,
+        out_specs=[vm] * 4,
         scratch_shapes=[
             pltpu.VMEM((seq_len, width), low),
-            pltpu.VMEM((seq_len, 3 * HEAD_DIM), low),
-            pltpu.VMEM((seq_len, HEAD_DIM), f32),
-            pltpu.VMEM((seq_len, HEAD_DIM), f32),
+            pltpu.VMEM((seq_len, width), low),
+            pltpu.VMEM((seq_len, width), low),
             pltpu.VMEM((reps,) + i_block, low),
             pltpu.VMEM((reps,) + o_block, low),
             pltpu.VMEM((rows, width), low),
@@ -1582,9 +1686,7 @@
             pltpu.VMEM((total, 8, 128), f32),
             pltpu.VMEM((2,) + i_block, low),
             pltpu.VMEM(i_block, low),
-            pltpu.VMEM(i_block, low),
             pltpu.VMEM((2,) + o_block, low),
-            pltpu.VMEM(o_block, low),
             pltpu.VMEM(o_block, low),
             hops,
             hops,
@@ -1602,15 +1704,13 @@
             dma((reps,)),
             dma((total - 1,)),
             dma((total - 1,)),
+            dma((2,)),
         ],
         compiler_params=pltpu.CompilerParams(
             collective_id=collective_id, has_side_effects=True, vmem_limit_bytes=VMEM_LIMIT
         ),
         name="closing",
-    )(
-        d_attn, normed, w_in, w_out, queries, keys, values, attended, probs, damp, cosine, sine,
-        tokens, d_middle, gain_rows, gain_terms,
-    )
+    )(d_projected, w_in, attended, normed, d_attn, tokens, d_middle, gain_rows, gain_terms)
 
 
 def tiles_of(ref):
@@ -1863,6 +1963,13 @@
     return table[:2, :6], rest[0], rest[1], rest[2], list(fresh[1:]) + [fresh[0]]
 
 
+def rope_tables(seq_len):
+    exponent = -np.arange(HEAD_DIM // 2, dtype=np.float32) * np.float32(2.0) / np.float32(HEAD_DIM)
+    freq = np.float32(10000.0) ** exponent
+    angle = (np.arange(seq_len, dtype=np.float32)[:, None] * freq[None, :]).astype(np.float64)
+    return jnp.asarray(np.cos(angle).astype(np.float32)), jnp.asarray(np.sin(angle).astype(np.float32))
+
+
 def split_device(
     tokens, cotangent, piece_starts, inproj, outproj, ffn_gate, ffn_up, ffn_down, norm_gains,
     mean_inproj, mean_outproj, mean_gate, mean_up, mean_down, mean_gains,
@@ -1895,31 +2002,26 @@
     w_in = got_in.reshape(width, -1)
     w_gate = got_gate.reshape(width, ff_part)
     w_down = got_down.reshape(ff_part, width)
-    w_out = got_out.transpose(1, 0, 2, 3).reshape(HEAD_DIM, width)
-
-    half = HEAD_DIM // 2
+
     position = jnp.arange(seq_len, dtype=jnp.int32)
-    freq = 10000.0 ** (-(jnp.arange(half, dtype=f32) * 2.0 / HEAD_DIM))
-    angle = position.astype(f32)[:, None] * freq[None, :]
-    cosine, sine = jnp.cos(angle), jnp.sin(angle)
+    cosine, sine = rope_tables(seq_len)
     starts = lax.dynamic_slice_in_dim(piece_starts, rep, 1, 0)[0]
     inside = (position[:, None] >= starts[None, :]) & (position[:, None] < starts[None, :] + PIC)
     tag = jnp.sum(inside.astype(jnp.int32) * (jnp.arange(starts.shape[0], dtype=jnp.int32)[None, :] + 1), axis=1)
-    attn_proj, queries, keys, values, attended, probs, damp, got_up = attention(
-        reps, count, normed_in, w_in, w_out, cosine, sine, tag, cut_up, 4
+    attn_proj, queries, keys, values, attended, probs, damp, w_out, got_up = attention(
+        reps, count, normed_in, w_in, got_out, cosine, sine, tag, cut_up, 4
     )
     w_up = got_up.reshape(width, ff_part)
 
-    layer_out, d_middle, d_attn, gain_terms, normed_mid, hidden, d_ffn, d_gu = feed_forward(
+    layer_out, d_middle, d_attn, gain_terms, normed_mid, d_gu, part_down = feed_forward(
         attn_proj, tokens, cotangent, gain_rows, w_gate, w_up, w_down, count, 5
     )
-    d_attn, sum_gu, grad_down = ffn_grads(
-        reps, count, d_attn, normed_mid, hidden, d_ffn, d_gu, d_rows, 9
-    )
-    d_attn = d_attn.reshape(seq_len, width)
+    d_attn, sum_gu, grad_down, d_projected = ffn_grads(
+        reps, count, d_attn, w_out, queries, keys, values, cosine, sine, normed_mid, d_gu, part_down, probs, damp, d_rows, 9
+    )
     input_grad, sum_in, sum_out, gain_tiles = closing(
-        reps, count, d_attn, normed_in, w_in, w_out, queries, keys, values, attended, probs, damp, cosine, sine,
-        tokens, d_middle, gain_rows, gain_terms, piece, 12,
+        reps, count, d_projected, w_in, attended, normed_in, d_attn.reshape(seq_len, width), tokens, d_middle,
+        gain_rows, gain_terms, piece, 12,
     )
     norm_table, gradients, new_means, new_squares, fresh = lamb_step(
         reps,

time: 756 us -> 724 us (0.958)
  Pallas kernels: 731 us -> 696 us
    pallas_call x1, Pallas kernels: 126 us -> 112 us  [ffn_grads(): pl.pallas_call(functools.partial(ffn_grads_kernel, reps, count), out_shap...]
    pallas_call x1, Pallas kernels: 113 us -> 99.6 us  [closing(): pl.pallas_call(functools.partial(closing_kernel, reps, count), out_shape=...]
    pallas_call x1, Pallas kernels: 211 us -> 202 us  [feed_forward(): pl.pallas_call(functools.partial(ffn_kernel, count), out_shape=[shape((ro...]
where the time goes in v5:
time: 724 us; the launch traced here: 719 us
  Pallas kernels  696 us (96%)
  local copies, waits for them, and re-layouts  13.9 us (2%)
    pallas_call x1, Pallas kernels, feed_forward(): pl.pallas_call(functools.partial(ffn_kernel, count), out_shape=[shape((ro...  202 us
    pallas_call x1, Pallas kernels, opening(): pl.pallas_call(functools.partial(opening_kernel, reps, count), out_shape=...  122 us
    pallas_call x1, Pallas kernels, ffn_grads(): pl.pallas_call(functools.partial(ffn_grads_kernel, reps, count), out_shap...  112 us
    pallas_call x1, Pallas kernels, closing(): pl.pallas_call(functools.partial(closing_kernel, reps, count), out_shape=...  99.6 us
    pallas_call x1, Pallas kernels, attention(): pl.pallas_call(functools.partial(attention_kernel, reps, count), out_shap...  98 us
    pallas_call x1, Pallas kernels, lamb_step(): pl.pallas_call(functools.partial(lamb_kernel, reps, count), out_shape=[ti...  28.1 us
    pallas_call x1, Pallas kernels, lamb_step(): pl.pallas_call(fresh_kernel, out_shape=[like_gains] + [shape(item, f32) f...  14.6 us

profile of v5, /device:TPU:0, one launch (start us, length us, event | category | flops | bytes accessed | tf_op | source)
XLA Modules:
  0.0 718.5 jit_solution(2133212974967193851)
XLA Ops:
  0.7 0.9 dynamic-slice_reduce_fusion
  1.6 0.7 convert_bitcast_fusion
  2.3 0.1 fusion
  2.4 0.0 copy-start.2
  2.4 0.6 pad_convert_fusion.gain_ref
  3.0 1.4 copy.68.g_master
  4.3 1.4 copy.69.g_mean
  5.7 1.4 copy.70.g_square
  7.1 1.8 convert_element_type.15
  8.9 1.0 copy.67.tagq_ref
  9.9 2.9 convert_element_type.14.dn_ref
  12.9 0.0 copy-done.2
  12.9 5.4 cut_weights.1
  18.3 122.1 %opening.1 = (bf16[8,128,2304]{2,1,0:T(8,128)(2,1)}, f32[8,2304]{1,0:T(8,128)}, bf16[4,8,72,768]{3,2,1,0:T(8,128)(2,1)}, bf16[4,8,72,1152]{3,2,1,0:T(8,128)(2,1)...) custom-call(bf16[128,2304]{1,0:T(8,128)(2,1)} %tokens_ref.3, f32[8,128]{1,0:T(8,128)} %pad_convert_fusion.gain_ref, ...), custom_call_target="tpu_custom_call" | custom-call | tf_op jit(solution)/shard_map/opening/pallas_call | solution.py:1088
  140.4 98.0 %attention.1 = (f32[128,2304]{1,0:T(8,128)}, bf16[1024,256]{1,0:T(8,128)(2,1)}, bf16[1024,256]{1,0:T(8,128)(2,1)}, bf16[1024,256]{1,0:T(8,128)(2,1)}, bf16[1024,...) custom-call(bf16[1024,2304]{1,0:T(8,128)(2,1)} %bitcast.11, ...), custom_call_target="tpu_custom_call" | custom-call | tf_op jit(solution)/shard_map/attention/pallas_call | solution.py:848
  238.4 202.4 %feed_forward.1 = (bf16[128,2304]{1,0:T(8,128)(2,1)}, f32[128,2304]{1,0:T(8,128)}, bf16[128,2304]{1,0:T(8,128)(2,1)}, f32[8,2304]{1,0:T(8,128)}, bf16[1024,2304]...) custom-call(f32[128,2304]{1,0:T(8,128)} %get-tuple-element.97.attn_ref, ...), custom_call_target="tpu_custom_call" | custom-call | tf_op jit(solution)/shard_map/feed_forward/pallas_call | solution.py:722
  440.8 112.5 %ffn_grads.1 = (bf16[8,128,2304]{2,1,0:T(8,128)(2,1)}, bf16[8,72,2304]{2,1,0:T(8,128)(2,1)}, f32[288,2304]{1,0:T(8,128)}, bf16[1024,768]{1,0:T(8,128)(2,1)}) custom-call(bf16[128,2304]{1,0:T(8,128)(2,1)} %get-tuple-element.103.dattn_ref, bf16[256,2304]{1,0:T(8,128)(2,1)} %get-tuple-element.104.wo_ref, bf16[1024,256]{1,0:T(8,128)(2,1)} %get-tuple-element.105.q_ref, ...), custom_call_target="tpu_custom_call" | custom-call | tf_op jit(solution)/shard_map/ffn_grads/pallas_call | solution.py:1454
  553.3 99.6 %closing.1 = (f32[128,2304]{1,0:T(8,128)}, bf16[8,72,768]{2,1,0:T(8,128)(2,1)}, bf16[4,16,2304]{2,1,0:T(8,128)(2,1)}, f32[32,8,128]{2,1,0:T(8,128)}) custom-call(bf16[1024,768]{1,0:T(8,128)(2,1)} %get-tuple-element.113.dproj, bf16[2304,768]{1,0:T(8,128)(2,1)} %bitcast.14, bf16[1024,256]{1,0:T(8,128)(2,1)} %get-tuple-element.114.att_ref, ...), custom_call_target="tpu_custom_call" | custom-call | tf_op jit(solution)/shard_map/closing/pallas_call | solution.py:1667
  652.8 28.1 %lamb_moments.1 = (f32[8,128]{1,0:T(8,128)}, f32[72,4]{1,0:T(8,128)}, f32[72,4]{1,0:T(8,128)}, f32[72,4]{1,0:T(8,128)}, f32[72,4]{1,0:T(8,128)}, /*index=5*/f32[...) custom-call(bf16[8,72,768]{2,1,0:T(8,128)(2,1)} %get-tuple-element.1, ...), custom_call_target="tpu_custom_call" | custom-call | tf_op jit(solution)/shard_map/lamb_moments/pallas_call | solution.py:1925
  681.0 1.4 copy.72
  682.4 1.4 copy.73
  683.8 1.4 copy.74
  685.2 13.7 %norm_table.1.table_ref = f32[8,128]{1,0:T(8,128)} custom-call(f32[8,128]{1,0:T(8,128)} %get-tuple-element.142.x_ref), custom_call_target="tpu_custom_call" | custom-call | tf_op jit(solution)/shard_map/norm_table/pallas_call | solution.py:1936
  699.0 0.0 copy-start.1
  699.0 0.0 copy-start
  699.0 14.6 %lamb_masters.1 = (f32[72,4]{1,0:T(8,128)}, f32[72,4096]{1,0:T(8,128)}, f32[64,2304]{1,0:T(8,128)}, f32[72,9216]{1,0:T(8,128)}, f32[72,9216]{1,0:T(8,128)}, /*index=5*/f32[288,2304]{1,0:T(8,128)}) custom-call(f32[8,128]{1,0:T(8,128)} %norm_table.1.table_ref, f32[72,4]{1,0:T(8,128)} %copy.68.g_master, f32[72,4]{1,0:T(8,128)} %get-tuple-element.143.g_step, ...), custom_call_target="tpu_custom_call" | custom-call | tf_op jit(solution)/shard_map/lamb_masters/pallas_call | solution.py:1953
  713.6 1.2 slice.3
  714.8 1.4 copy.75
  716.3 0.0 copy-done.1
  716.3 0.8 copy.78
  717.1 0.0 copy-done
  717.1 1.0 copy.79
  (1 shorter events, 0.0 us)
Async XLA Ops:
  2.4 10.5 %copy-start.2 = (s32[1024]{0:T(1024)}, s32[1024]{0:T(1024)S(1)}, u32[]{:S(2)}) copy-start(s32[1024]{0:T(1024)S(1)} %fusion) | copy-start | bytes 12292
  699.0 17.3 %copy-start.1 = (bf16[128,2304]{1,0:T(8,128)(2,1)S(1)}, bf16[128,2304]{1,0:T(8,128)(2,1)}, u32[]{:S(2)}) copy-start(bf16[128,2304]{1,0:T(8,128)(2,1)} %get-tuple-element.265) | copy-start | bytes 1769476
  699.0 18.1 %copy-start = (f32[128,2304]{1,0:T(8,128)S(1)}, f32[128,2304]{1,0:T(8,128)}, u32[]{:S(2)}) copy-start(f32[128,2304]{1,0:T(8,128)} %get-tuple-element.266) | copy-start | bytes 3538948

commit v6 on v5

--- a/solution.py
+++ b/solution.py
@@ -794,12 +794,12 @@
 
     lax.fori_loop(0, 4, project, 0)
 
-    def attend(i, carry):
-        at = pl.ds(pl.multiple_of(i * tall, 16), tall)
+    def attend(shard):
+        at = pl.ds(pl.multiple_of(shard * rows, 16), rows)
         raw = lax.dot_general(q_ref[at, :], k_ref[...], (((1,), (1,)), ((), ())), preferred_element_type=f32)
         bent = jnp.tanh(raw * (1.0 / 50.0))
-        query_at = i * tall + lax.broadcasted_iota(jnp.int32, (tall, seq_len), 0)
-        key_at = lax.broadcasted_iota(jnp.int32, (tall, seq_len), 1)
+        query_at = shard * rows + lax.broadcasted_iota(jnp.int32, (rows, seq_len), 0)
+        key_at = lax.broadcasted_iota(jnp.int32, (rows, seq_len), 1)
         tag = tagq_ref[at, :]
         visible = (key_at <= query_at) | ((tag == tagk_ref[...]) & (tag > 0))
         masked = jnp.where(visible, 50.0 * bent, -1e30)
@@ -811,14 +811,25 @@
         attended = jnp.dot(low, v_ref[...], preferred_element_type=f32).astype(bf16)
         att_ref[at, :] = attended
         part[at, :] = jnp.dot(attended, wo_ref[...], preferred_element_type=f32)
-        return carry
-
-    lax.fori_loop(0, 4, attend, 0)
+
+    def attend_both(hop):
+        def body(way, carry):
+            attend(ring.at(hop + way * (count - 2 * hop)))
+            return carry
+
+        lax.fori_loop(0, 2 if hop else 1, body, 0)
 
     work = weights.steps()
+    first_of_step = [0] + [1 + UNITS * step for step in range(ring.half - 1)]
+    calls = []
 
     def pause():
-        for _ in range(min(2, len(work))):
+        call = len(calls)
+        calls.append(call)
+        if call in first_of_step:
+            attend_both(ring.half - 1 - first_of_step.index(call))
+            return
+        for _ in range(min(3, len(work))):
             work.pop(0)()
 
     def finish(span, total):
@@ -827,6 +838,7 @@
     def take(shard, span):
         return part[pl.ds(pl.multiple_of(shard * rows + span.start, 16), span.size), :]
 
+    attend(ring.at(ring.half))
     started = reduce_on_ring(ring, rows, take, first, landed, r_send, r_recv, finish, pause)
     for piece in work:
         piece()
@@ -946,8 +958,10 @@
 
 
 def opening_kernel(
-    reps, count, tok_ref, gain_ref, in_ref, gate_ref, dn_ref, ou_ref, h1_ref, gains_ref, w_in, w_gate, w_dn, w_ou,
-    tok_all, gain_all, t_send, t_recv, g_send, g_recv, i_sems, u_sems, o_send, o_recv, n_send, n_recv, loc
+    reps, count, tok_ref, gain_ref, in_hbm, dn_hbm, ou_hbm, gate_hbm, up_hbm,
+    h1_ref, gains_ref, w_in, w_gate, w_dn, w_ou, cut_up,
+    in_f, dn_f, ou_f, gate_f, up_f, in_ref, dn_ref, ou_ref, gate_ref, tok_all, gain_all,
+    t_send, t_recv, g_send, g_recv, i_sems, u_sems, o_send, o_recv, n_send, n_recv, loc, loads
 ):
     f32 = jnp.float32
     ring = Ring(count)
@@ -957,6 +971,14 @@
     mine = rep * count + me
     d_rows = in_ref.shape[1]
     rows = tok_ref.shape[0]
+    fetched = [
+        pltpu.make_async_copy(src, dst, loads.at[index])
+        for index, (src, dst) in enumerate(
+            ((in_hbm, in_f), (dn_hbm, dn_f), (ou_hbm, ou_f), (gate_hbm, gate_f), (up_hbm, up_f))
+        )
+    ]
+    for copy in fetched:
+        copy.start()
     meet(others)
     started = []
 
@@ -970,33 +992,42 @@
     ins = Fetch(ring, in_ref, w_in, i_sems)
     gates = Fetch(ring, gate_ref, w_gate, u_sems)
     gather = Gather(ring, tok_ref, tok_all, t_send, t_recv)
+    gather.begin()
+    fetched[0].wait()
+    cut_heads(count, in_f, in_ref)
     ins.begin()
-    gather.begin()
-
-    per_head = count * reps // HEADS
-    target = mine // per_head
-    slot = mine % per_head
-
-    def ou_copy(j):
-        return remote(ou_ref.at[j], w_ou.at[j, slot], o_send.at[j], o_recv.at[slot], (j, target))
-
-    def is_self(j):
-        return (rep == j) & (me == target)
-
-    for j in range(reps):
-        @pl.when(jnp.logical_not(is_self(j)))
-        def _():
-            ou_copy(j).start()
-
-        @pl.when(is_self(j))
-        def _():
-            pltpu.make_async_copy(ou_ref.at[j], w_ou.at[j, slot], o_recv.at[slot]).start()
-
+    fetched[1].wait()
+    dn_ref[...] = dn_f[...].astype(dn_ref.dtype)
     dn_x = remote(dn_ref, w_dn.at[rep], n_send.at[0], n_recv.at[0], (across, me))
     dn_c = remote(dn_ref, w_dn.at[rep], n_send.at[1], n_recv.at[1], (beside, me))
     dn_d = remote(w_dn.at[across], w_dn.at[across], n_send.at[2], n_recv.at[2], (beside, me))
     go(dn_x)
     go(dn_c)
+    fetched[2].wait()
+    for j in range(reps):
+        ou_ref[j] = ou_f[j * ou_ref.shape[1] : (j + 1) * ou_ref.shape[1], :].astype(ou_ref.dtype)
+
+    per_head = count * reps // HEADS
+    target = mine // per_head
+    slot = mine % per_head
+
+    def ou_copy(j):
+        return remote(ou_ref.at[j], w_ou.at[j, slot], o_send.at[j], o_recv.at[slot], (j, target))
+
+    def is_self(j):
+        return (rep == j) & (me == target)
+
+    for j in range(reps):
+        @pl.when(jnp.logical_not(is_self(j)))
+        def _():
+            ou_copy(j).start()
+
+        @pl.when(is_self(j))
+        def _():
+            pltpu.make_async_copy(ou_ref.at[j], w_ou.at[j, slot], o_recv.at[slot]).start()
+
+    fetched[3].wait()
+    cut_units(reps, count, gate_f, gate_ref)
     gates.begin()
     locals_ = []
     for index, (src, dst) in enumerate(
@@ -1036,6 +1067,8 @@
     for k in range(1, count):
         ins.pass_on(k)
     take_hop(1)
+    fetched[4].wait()
+    cut_units(reps, count, up_f, cut_up)
     for k in range(count):
         ins.pass_beside(k)
     take_hop(2)
@@ -1076,30 +1109,45 @@
         copy.wait()
 
 
-def opening(reps, count, tokens, gain_tile, w_in, w_gate, w_dn, w_ou, collective_id):
+def opening(reps, count, tokens, gain_tile, inproj, outproj, ffn_gate, ffn_up, ffn_down, collective_id):
     dma = pltpu.SemaphoreType.DMA
     per_head = count * reps // HEADS
     total = reps * count
-    low = jnp.bfloat16
+    low, f32 = jnp.bfloat16, jnp.float32
     shape = jax.ShapeDtypeStruct
     hops = dma((2, count // 2, UNITS))
     width = tokens.shape[1]
     gathered = (count,) + tokens.shape
+    d_rows = inproj.shape[0]
+    heads = (count, d_rows, 3 * HEAD_DIM)
+    units = (count, d_rows, ffn_gate.shape[1] // count)
+    outs = (reps, outproj.shape[0] // reps, width)
+    vm, hb = pl.BlockSpec(memory_space=VM), pl.BlockSpec(memory_space=HB)
     return pl.pallas_call(
         functools.partial(opening_kernel, reps, count),
         out_shape=[
             shape(gathered, low),
-            shape((8, width), jnp.float32),
-            shape((reps,) + w_in.shape, low),
-            shape((reps,) + w_gate.shape, low),
-            shape((reps,) + w_dn.shape, low),
-            shape((reps, per_head) + w_ou.shape[1:], low),
+            shape((8, width), f32),
+            shape((reps,) + heads, low),
+            shape((reps,) + units, low),
+            shape((reps,) + ffn_down.shape, low),
+            shape((reps, per_head) + outs[1:], low),
+            shape(units, low),
         ],
-        in_specs=[pl.BlockSpec(memory_space=VM)] * 2 + [pl.BlockSpec(memory_space=HB)] * 4,
-        out_specs=[pl.BlockSpec(memory_space=VM)] * 2 + [pl.BlockSpec(memory_space=HB)] * 4,
+        in_specs=[vm] * 2 + [hb] * 5,
+        out_specs=[vm] * 2 + [hb] * 4 + [vm],
         scratch_shapes=[
+            pltpu.VMEM(inproj.shape, f32),
+            pltpu.VMEM(ffn_down.shape, f32),
+            pltpu.VMEM(outproj.shape, f32),
+            pltpu.VMEM(ffn_gate.shape, f32),
+            pltpu.VMEM(ffn_up.shape, f32),
+            pltpu.VMEM(heads, low),
+            pltpu.VMEM(ffn_down.shape, low),
+            pltpu.VMEM(outs, low),
+            pltpu.VMEM(units, low),
             pltpu.VMEM(gathered, low),
-            pltpu.VMEM((total,) + gain_tile.shape, jnp.float32),
+            pltpu.VMEM((total,) + gain_tile.shape, f32),
             hops,
             hops,
             dma((total - 1,)),
@@ -1111,44 +1159,30 @@
             dma((6,)),
             dma((6,)),
             dma((3,)),
+            dma((5,)),
         ],
         compiler_params=pltpu.CompilerParams(
             collective_id=collective_id, has_side_effects=True, vmem_limit_bytes=VMEM_LIMIT
         ),
         name="opening",
-    )(tokens, gain_tile, w_in, w_gate, w_dn, w_ou)
-
-
-def cut_kernel(reps, count, in_ref, gate_ref, up_ref, cut_in, cut_gate, cut_up):
-    low = jnp.bfloat16
+    )(tokens, gain_tile, inproj, ffn_down, outproj, ffn_gate, ffn_up)
+
+
+def cut_units(reps, count, ref, cut):
+    block = ref.shape[1] // (reps * count)
+    for shard in range(count):
+        pieces = [ref[:, (r * count + shard) * block : (r * count + shard + 1) * block] for r in range(reps)]
+        cut[shard] = jnp.concatenate(pieces, axis=1).astype(cut.dtype)
+
+
+def cut_heads(count, ref, cut):
     group = HEADS // KV_HEADS
-    block = gate_ref.shape[1] // (reps * count)
     for shard in range(count):
-        for ref, cut in ((gate_ref, cut_gate), (up_ref, cut_up)):
-            pieces = [ref[:, (r * count + shard) * block : (r * count + shard + 1) * block] for r in range(reps)]
-            cut[shard] = jnp.concatenate(pieces, axis=1).astype(low)
         heads = shard, HEADS + shard // group, HEADS + KV_HEADS + shard // group
         for index, head in enumerate(heads):
-            cut_in[shard, :, index * HEAD_DIM : (index + 1) * HEAD_DIM] = in_ref[
+            cut[shard, :, index * HEAD_DIM : (index + 1) * HEAD_DIM] = ref[
                 :, head * HEAD_DIM : (head + 1) * HEAD_DIM
-            ].astype(low)
-
-
-def cut_weights(reps, count, inproj, ffn_gate, ffn_up):
-    rows = inproj.shape[0]
-    shape = jax.ShapeDtypeStruct
-    return pl.pallas_call(
-        functools.partial(cut_kernel, reps, count),
-        out_shape=[
-            shape((count, rows, 3 * HEAD_DIM), jnp.bfloat16),
-            shape((count, rows, ffn_gate.shape[1] // count), jnp.bfloat16),
-            shape((count, rows, ffn_up.shape[1] // count), jnp.bfloat16),
-        ],
-        in_specs=[pl.BlockSpec(memory_space=VM)] * 3,
-        out_specs=[pl.BlockSpec(memory_space=VM)] * 3,
-        compiler_params=pltpu.CompilerParams(vmem_limit_bytes=VMEM_LIMIT),
-        name="cut_weights",
-    )(inproj, ffn_gate, ffn_up)
+            ].astype(cut.dtype)
 
 
 class RepSum:
@@ -1826,8 +1860,8 @@
             store(i, j).start()
         sums = note(sums, i, pair)
     gain_total = functools.reduce(jnp.add, [gain_tiles[device] for device in range(total)])
-    d_rows, kinds = g_master.shape
-    gain_grad = gain_total.T[:d_rows, :kinds]
+    kinds, d_rows = g_master.shape
+    gain_grad = gain_total[:kinds, :d_rows]
     gain_master = g_master[...]
     new_mean, new_square, gain_step = lamb(gain_master, gain_grad, g_mean[...], g_square[...])
     gg_out[...] = gain_grad
@@ -1880,7 +1914,7 @@
 def fresh_kernel(table_ref, g_master, g_step, *refs):
     names = 5
     hbm_in, refs = [refs[2 * i : 2 * i + 2] for i in range(names)], refs[2 * names :]
-    gp_out, refs = refs[0], refs[1:]
+    (gp_out, table_out), refs = refs[:2], refs[2:]
     hbm_out, refs = refs[:names], refs[names:]
     masters, steps, refs = refs[:names], refs[names : 2 * names], refs[2 * names :]
     in_sem, out_sem = refs
@@ -1894,6 +1928,7 @@
     for i in LAMB_ORDER:
         for j in (0, 1):
             fetch(i, j).start()
+    table_out[...] = table_ref[0:2, 0 : names + 1]
     rate = 0.3 * table_ref[0:1, :] / table_ref[1:2, :]
     gp_out[...] = g_master[...] - rate[:, 5:6] * g_step[...]
     for i in LAMB_ORDER:
@@ -1952,15 +1987,15 @@
     )(sums)
     fresh = pl.pallas_call(
         fresh_kernel,
-        out_shape=[like_gains] + [shape(item, f32) for item in shapes],
+        out_shape=[like_gains, shape((2, 6), f32)] + [shape(item, f32) for item in shapes],
         in_specs=[vm] * 3 + [hb] * 10,
-        out_specs=[vm] + [hb] * 5,
+        out_specs=[vm] * 2 + [hb] * 5,
         scratch_shapes=[pltpu.VMEM(item, f32) for _ in range(2) for item in shapes] + [dma((5, 2)), dma((5,))],
         compiler_params=local,
         name="lamb_masters",
     )(table, gains[0], gain_parts[3], *[item for i in range(5) for item in (states[i][0], parts[i][3])])
-    rest = [[parts[i][j] for i in range(5)] + [gain_parts[j]] for j in range(3)]
-    return table[:2, :6], rest[0], rest[1], rest[2], list(fresh[1:]) + [fresh[0]]
+    rest = [[parts[i][j] for i in range(5)] + [gain_parts[j].T] for j in range(3)]
+    return fresh[1], rest[0], rest[1], rest[2], list(fresh[2:]) + [fresh[0].T]
 
 
 def rope_tables(seq_len):
@@ -1992,11 +2027,9 @@
     per_head = HEAD_DIM // o_rows
     piece = o_rows // reps
 
-    cut_in, cut_gate, cut_up = cut_weights(reps, count, inproj, ffn_gate, ffn_up)
-    cut_out = outproj.astype(bf16).reshape(reps, piece, width)
-    gain_tile = jnp.pad(norm_gains.astype(bf16).astype(f32).T, ((0, 4), (0, 128 - d_rows)))
-    normed_in, gain_rows, got_in, got_gate, got_down, got_out = opening(
-        reps, count, tokens, gain_tile, cut_in, cut_gate, ffn_down.astype(bf16), cut_out, 1
+    gain_tile = jnp.pad(norm_gains.T.astype(bf16).astype(f32), ((0, 4), (0, 128 - d_rows)))
+    normed_in, gain_rows, got_in, got_gate, got_down, got_out, cut_up = opening(
+        reps, count, tokens, gain_tile, inproj, outproj, ffn_gate, ffn_up, ffn_down, 1
     )
     normed_in = normed_in.reshape(seq_len, width)
     w_in = got_in.reshape(width, -1)
@@ -2028,7 +2061,7 @@
         count,
         (sum_in, sum_out, sum_gu, gain_tiles),
         grad_down,
-        (norm_gains, mean_gains, square_gains),
+        (norm_gains.T, mean_gains.T, square_gains.T),
         (
             (inproj, mean_inproj, square_inproj),
             (outproj, mean_outproj, square_outproj),

time: 724 us -> 704 us (0.972)
  local copies, waits for them, and re-layouts: 13.9 us -> 2.87 us
    unnamed x15 -> x8, local copies, waits for them, and re-layouts: 11.7 us -> 1.85 us
    pallas_call x2 -> x1, Pallas kernels: 20 us -> 14.5 us  [lamb_step(): pl.pallas_call(fresh_kernel, out_shape=[like_gains, shape((2, 6), f32)] +...]
where the time goes in v6:
time: 704 us; the launch traced here: 699 us
  Pallas kernels  693 us (98%)
    pallas_call x1, Pallas kernels, feed_forward(): pl.pallas_call(functools.partial(ffn_kernel, count), out_shape=[shape((ro...  196 us
    pallas_call x1, Pallas kernels, opening(): pl.pallas_call(functools.partial(opening_kernel, reps, count), out_shape=...  124 us
    pallas_call x1, Pallas kernels, ffn_grads(): pl.pallas_call(functools.partial(ffn_grads_kernel, reps, count), out_shap...  113 us
    pallas_call x1, Pallas kernels, attention(): pl.pallas_call(functools.partial(attention_kernel, reps, count), out_shap...  105 us
    pallas_call x1, Pallas kernels, closing(): pl.pallas_call(functools.partial(closing_kernel, reps, count), out_shape=...  99.7 us
    pallas_call x1, Pallas kernels, lamb_step(): pl.pallas_call(functools.partial(lamb_kernel, reps, count), out_shape=[ti...  28.1 us
    pallas_call x1, Pallas kernels, lamb_step(): pl.pallas_call(fresh_kernel, out_shape=[like_gains, shape((2, 6), f32)] +...  14.5 us

profile of v6, /device:TPU:0, one launch (start us, length us, event | category | flops | bytes accessed | tf_op | source)
XLA Modules:
  0.0 699.1 jit_solution(1621033978923952228)
XLA Ops:
  0.7 0.9 dynamic-slice_reduce_fusion
  1.6 0.7 bitcast_convert_fusion
  2.3 0.1 fusion
  2.4 0.0 copy-start.2
  2.4 0.6 pad_convert_fusion.gain_ref
  3.0 1.0 copy.51.tagq_ref
  4.0 123.9 %opening.1 = (bf16[8,128,2304]{2,1,0:T(8,128)(2,1)}, f32[8,2304]{1,0:T(8,128)}, bf16[4,8,72,768]{3,2,1,0:T(8,128)(2,1)}, bf16[4,8,72,1152]{3,2,1,0:T(8,128)(2,1)...) custom-call(bf16[128,2304]{1,0:T(8,128)(2,1)} %tokens_ref.3, ...), custom_call_target="tpu_custom_call" | custom-call | tf_op jit(solution)/shard_map/opening/pallas_call | solution.py:1126
  127.9 0.0 copy-done.2
  127.9 104.5 %attention.1 = (f32[128,2304]{1,0:T(8,128)}, bf16[1024,256]{1,0:T(8,128)(2,1)}, bf16[1024,256]{1,0:T(8,128)(2,1)}, bf16[1024,256]{1,0:T(8,128)(2,1)}, bf16[1024,...) custom-call(bf16[1024,2304]{1,0:T(8,128)(2,1)} %bitcast.16, ...), custom_call_target="tpu_custom_call" | custom-call | tf_op jit(solution)/shard_map/attention/pallas_call | solution.py:860
  232.4 195.6 %feed_forward.1 = (bf16[128,2304]{1,0:T(8,128)(2,1)}, f32[128,2304]{1,0:T(8,128)}, bf16[128,2304]{1,0:T(8,128)(2,1)}, f32[8,2304]{1,0:T(8,128)}, bf16[1024,2304]...) custom-call(f32[128,2304]{1,0:T(8,128)} %get-tuple-element.94.attn_ref, ...), custom_call_target="tpu_custom_call" | custom-call | tf_op jit(solution)/shard_map/feed_forward/pallas_call | solution.py:722
  428.0 112.7 %ffn_grads.1 = (bf16[8,128,2304]{2,1,0:T(8,128)(2,1)}, bf16[8,72,2304]{2,1,0:T(8,128)(2,1)}, f32[288,2304]{1,0:T(8,128)}, bf16[1024,768]{1,0:T(8,128)(2,1)}) custom-call(bf16[128,2304]{1,0:T(8,128)(2,1)} %get-tuple-element.100.dattn_ref, bf16[256,2304]{1,0:T(8,128)(2,1)} %get-tuple-element.101.wo_ref, bf16[1024,256]{1,0:T(8,128)(2,1)} %get-tuple-element.102.q_ref, ...), custom_call_target="tpu_custom_call" | custom-call | tf_op jit(solution)/shard_map/ffn_grads/pallas_call | solution.py:1488
  540.8 99.7 %closing.1 = (f32[128,2304]{1,0:T(8,128)}, bf16[8,72,768]{2,1,0:T(8,128)(2,1)}, bf16[4,16,2304]{2,1,0:T(8,128)(2,1)}, f32[32,8,128]{2,1,0:T(8,128)}) custom-call(bf16[1024,768]{1,0:T(8,128)(2,1)} %get-tuple-element.110.dproj, bf16[2304,768]{1,0:T(8,128)(2,1)} %bitcast.19, bf16[1024,256]{1,0:T(8,128)(2,1)} %get-tuple-element.111.att_ref, ...), custom_call_target="tpu_custom_call" | custom-call | tf_op jit(solution)/shard_map/closing/pallas_call | solution.py:1701
  640.5 28.1 %lamb_moments.1 = (f32[8,128]{1,0:T(8,128)}, f32[4,72]{1,0:T(4,128)}, f32[4,72]{1,0:T(4,128)}, f32[4,72]{1,0:T(4,128)}, f32[4,72]{1,0:T(4,128)}, /*index=5*/f32[...) custom-call(bf16[8,72,768]{2,1,0:T(8,128)(2,1)} %get-tuple-element.1, ...), custom_call_target="tpu_custom_call" | custom-call | tf_op jit(solution)/shard_map/lamb_moments/pallas_call | solution.py:1960
  668.7 13.6 %norm_table.1.table_ref = f32[8,128]{1,0:T(8,128)} custom-call(f32[8,128]{1,0:T(8,128)} %get-tuple-element.139.x_ref), custom_call_target="tpu_custom_call" | custom-call | tf_op jit(solution)/shard_map/norm_table/pallas_call | solution.py:1971
  682.3 0.0 copy-start.1
  682.3 0.0 copy-start
  682.3 14.5 %lamb_masters.1 = (f32[4,72]{1,0:T(4,128)}, f32[2,6]{1,0:T(2,128)}, f32[72,4096]{1,0:T(8,128)}, f32[64,2304]{1,0:T(8,128)}, f32[72,9216]{1,0:T(8,128)}, /*index=5*/f32[72,9216]{1,0:T(8,128)}, f32[288,2304]{1,0:T(8,128)}) custom-call(f32[8,128]{1,0:T(8,128)} %norm_table.1.table_ref, f32[4,72]{1,0:T(4,128)} %bitcast.27, f32[4,72]{1,0:T(4,128)} %get-tuple-element.140.g_step, ...), custom_call_target="tpu_custom_call" | custom-call | tf_op jit(solution)/shard_map/lamb_masters/pallas_call | solution.py:1988
  696.8 0.0 copy-done.1
  696.8 0.8 copy.54
  697.6 0.0 copy-done
  697.6 1.0 copy.55
  (1 shorter events, 0.0 us)
Async XLA Ops:
  2.4 125.5 %copy-start.2 = (s32[1024]{0:T(1024)}, s32[1024]{0:T(1024)S(1)}, u32[]{:S(2)}) copy-start(s32[1024]{0:T(1024)S(1)} %fusion) | copy-start | bytes 12292
  682.3 14.5 %copy-start.1 = (bf16[128,2304]{1,0:T(8,128)(2,1)S(1)}, bf16[128,2304]{1,0:T(8,128)(2,1)}, u32[]{:S(2)}) copy-start(bf16[128,2304]{1,0:T(8,128)(2,1)} %get-tuple-element.182) | copy-start | bytes 1769476
  682.3 15.3 %copy-start = (f32[128,2304]{1,0:T(8,128)S(1)}, f32[128,2304]{1,0:T(8,128)}, u32[]{:S(2)}) copy-start(f32[128,2304]{1,0:T(8,128)} %get-tuple-element.183) | copy-start | bytes 3538948

commit v7 on v6

--- a/solution.py
+++ b/solution.py
@@ -992,7 +992,6 @@
     ins = Fetch(ring, in_ref, w_in, i_sems)
     gates = Fetch(ring, gate_ref, w_gate, u_sems)
     gather = Gather(ring, tok_ref, tok_all, t_send, t_recv)
-    gather.begin()
     fetched[0].wait()
     cut_heads(count, in_f, in_ref)
     ins.begin()
@@ -1066,12 +1065,11 @@
 
     for k in range(1, count):
         ins.pass_on(k)
-    take_hop(1)
     fetched[4].wait()
     cut_units(reps, count, up_f, cut_up)
-    for k in range(count):
-        ins.pass_beside(k)
-    take_hop(2)
+    gather.begin()
+    for k in range(1, count):
+        gates.pass_on(k)
     for i in range(per_head):
         remote(
             ou_ref.at[0], w_ou.at[rep, i], o_send.at[0], o_recv.at[i], (across, me)
@@ -1081,14 +1079,13 @@
     ou_d = remote(w_ou.at[across], w_ou.at[across], n_send.at[5], n_recv.at[5], (beside, me))
     go(ou_x)
     go(ou_c)
+    take_hop(1)
     dn_x.wait_recv()
     go(dn_d)
-    for k in range(1, count // 2):
-        gates.pass_on(k)
-    take_hop(3)
-    for k in range(count // 2, count):
-        gates.pass_on(k)
-    for hop in range(4, ring.half + 1):
+    take_hop(2)
+    for k in range(count):
+        ins.pass_beside(k)
+    for hop in range(3, ring.half + 1):
         take_hop(hop)
     ou_x.wait_recv()
     go(ou_d)
@@ -1780,9 +1777,13 @@
 
     fetch_dn = pltpu.make_async_copy(grad_dn, grads[4], dn_sem)
     fetch_dn.start()
-    for i in LAMB_ORDER:
-        for j in range(3):
-            fetch(i, j).start()
+
+    def fetch_all(order):
+        for i in order:
+            for j in range(3):
+                fetch(i, j).start()
+
+    fetch_all(LAMB_ORDER[:2])
 
     def store(i, j):
         return pltpu.make_async_copy((grads, means, squares, masters)[j][i], hbm_out[i][j], out_sem.at[i, j])
@@ -1819,9 +1820,10 @@
             fetch_dn.wait()
 
     def lamb(master, grad, mean, square):
-        new_mean = 0.5 * mean + 0.5 * grad
-        new_square = 0.5 * square + 0.5 * grad * grad
-        return new_mean, new_square, new_mean / (jnp.sqrt(new_square) + 1e-06) + 0.01 * master
+        new_mean = 0.5 * (mean + grad)
+        new_square = 0.5 * (square + grad * grad)
+        root = new_square * lax.rsqrt(new_square)
+        return new_mean, new_square, new_mean / (root + 1e-06) + 0.01 * master
 
     def sweep(i):
         down, across, tall, wide = tiles_of(masters[i])
@@ -1851,10 +1853,11 @@
         return sums
 
     sums = jnp.zeros((8, 128), f32)
-    for i in LAMB_ORDER:
+    for place, i in enumerate(LAMB_ORDER):
         make_grad(i)
         for j in range(3):
             fetch(i, j).wait()
+        fetch_all(LAMB_ORDER[place + 2 : place + 3])
         pair = sweep(i)
         for j in range(4):
             store(i, j).start()
@@ -1925,17 +1928,21 @@
     def store(i):
         return pltpu.make_async_copy(masters[i], hbm_out[i], out_sem.at[i])
 
-    for i in LAMB_ORDER:
-        for j in (0, 1):
-            fetch(i, j).start()
+    def fetch_all(order):
+        for i in order:
+            for j in (0, 1):
+                fetch(i, j).start()
+
+    fetch_all(LAMB_ORDER[:2])
     table_out[...] = table_ref[0:2, 0 : names + 1]
     rate = 0.3 * table_ref[0:1, :] / table_ref[1:2, :]
     gp_out[...] = g_master[...] - rate[:, 5:6] * g_step[...]
-    for i in LAMB_ORDER:
+    for place, i in enumerate(LAMB_ORDER):
         down, across, _, _ = tiles_of(masters[i])
         scale = rate[:, i : i + 1]
         for j in (0, 1):
             fetch(i, j).wait()
+        fetch_all(LAMB_ORDER[place + 2 : place + 3])
 
         def body(n, carry):
             at = tile_at(masters[i], n)

time: 704 us -> 689 us (0.979)
  Pallas kernels: 693 us -> 677 us
    pallas_call x1, Pallas kernels: 105 us -> 97.4 us  [attention(): pl.pallas_call(functools.partial(attention_kernel, reps, count), out_shap...]
where the time goes in v7:
time: 689 us; the launch traced here: 684 us
  Pallas kernels  677 us (98%)
    pallas_call x1, Pallas kernels, feed_forward(): pl.pallas_call(functools.partial(ffn_kernel, count), out_shape=[shape((ro...  197 us
    pallas_call x1, Pallas kernels, opening(): pl.pallas_call(functools.partial(opening_kernel, reps, count), out_shape=...  118 us
    pallas_call x1, Pallas kernels, ffn_grads(): pl.pallas_call(functools.partial(ffn_grads_kernel, reps, count), out_shap...  110 us
    pallas_call x1, Pallas kernels, closing(): pl.pallas_call(functools.partial(closing_kernel, reps, count), out_shape=...  102 us
    pallas_call x1, Pallas kernels, attention(): pl.pallas_call(functools.partial(attention_kernel, reps, count), out_shap...  97.4 us
    pallas_call x1, Pallas kernels, lamb_step(): pl.pallas_call(functools.partial(lamb_kernel, reps, count), out_shape=[ti...  25 us
    pallas_call x1, Pallas kernels, lamb_step(): pl.pallas_call(fresh_kernel, out_shape=[like_gains, shape((2, 6), f32)] +...  14.5 us

profile of v7, /device:TPU:0, one launch (start us, length us, event | category | flops | bytes accessed | tf_op | source)
XLA Modules:
  0.0 683.6 jit_solution(64271593019505769)
XLA Ops:
  0.7 0.9 dynamic-slice_reduce_fusion
  1.6 0.7 bitcast_convert_fusion
  2.3 0.1 fusion
  2.4 0.0 copy-start.2
  2.4 0.6 pad_convert_fusion.gain_ref
  3.0 1.0 copy.51.tagq_ref
  4.0 117.8 %opening.1 = (bf16[8,128,2304]{2,1,0:T(8,128)(2,1)}, f32[8,2304]{1,0:T(8,128)}, bf16[4,8,72,768]{3,2,1,0:T(8,128)(2,1)}, bf16[4,8,72,1152]{3,2,1,0:T(8,128)(2,1)...) custom-call(bf16[128,2304]{1,0:T(8,128)(2,1)} %tokens_ref.3, ...), custom_call_target="tpu_custom_call" | custom-call | tf_op jit(solution)/shard_map/opening/pallas_call | solution.py:1123
  121.8 0.0 copy-done.2
  121.8 97.4 %attention.1 = (f32[128,2304]{1,0:T(8,128)}, bf16[1024,256]{1,0:T(8,128)(2,1)}, bf16[1024,256]{1,0:T(8,128)(2,1)}, bf16[1024,256]{1,0:T(8,128)(2,1)}, bf16[1024,...) custom-call(bf16[1024,2304]{1,0:T(8,128)(2,1)} %bitcast.16, ...), custom_call_target="tpu_custom_call" | custom-call | tf_op jit(solution)/shard_map/attention/pallas_call | solution.py:860
  219.2 197.1 %feed_forward.1 = (bf16[128,2304]{1,0:T(8,128)(2,1)}, f32[128,2304]{1,0:T(8,128)}, bf16[128,2304]{1,0:T(8,128)(2,1)}, f32[8,2304]{1,0:T(8,128)}, bf16[1024,2304]...) custom-call(f32[128,2304]{1,0:T(8,128)} %get-tuple-element.94.attn_ref, ...), custom_call_target="tpu_custom_call" | custom-call | tf_op jit(solution)/shard_map/feed_forward/pallas_call | solution.py:722
  416.3 110.4 %ffn_grads.1 = (bf16[8,128,2304]{2,1,0:T(8,128)(2,1)}, bf16[8,72,2304]{2,1,0:T(8,128)(2,1)}, f32[288,2304]{1,0:T(8,128)}, bf16[1024,768]{1,0:T(8,128)(2,1)}) custom-call(bf16[128,2304]{1,0:T(8,128)(2,1)} %get-tuple-element.100.dattn_ref, bf16[256,2304]{1,0:T(8,128)(2,1)} %get-tuple-element.101.wo_ref, bf16[1024,256]{1,0:T(8,128)(2,1)} %get-tuple-element.102.q_ref, ...), custom_call_target="tpu_custom_call" | custom-call | tf_op jit(solution)/shard_map/ffn_grads/pallas_call | solution.py:1485
  526.8 101.5 %closing.1 = (f32[128,2304]{1,0:T(8,128)}, bf16[8,72,768]{2,1,0:T(8,128)(2,1)}, bf16[4,16,2304]{2,1,0:T(8,128)(2,1)}, f32[32,8,128]{2,1,0:T(8,128)}) custom-call(bf16[1024,768]{1,0:T(8,128)(2,1)} %get-tuple-element.110.dproj, bf16[2304,768]{1,0:T(8,128)(2,1)} %bitcast.19, bf16[1024,256]{1,0:T(8,128)(2,1)} %get-tuple-element.111.att_ref, ...), custom_call_target="tpu_custom_call" | custom-call | tf_op jit(solution)/shard_map/closing/pallas_call | solution.py:1698
  628.3 25.0 %lamb_moments.1 = (f32[8,128]{1,0:T(8,128)}, f32[4,72]{1,0:T(4,128)}, f32[4,72]{1,0:T(4,128)}, f32[4,72]{1,0:T(4,128)}, f32[4,72]{1,0:T(4,128)}, /*index=5*/f32[...) custom-call(bf16[8,72,768]{2,1,0:T(8,128)(2,1)} %get-tuple-element.1, ...), custom_call_target="tpu_custom_call" | custom-call | tf_op jit(solution)/shard_map/lamb_moments/pallas_call | solution.py:1967
  653.3 13.5 %norm_table.1.table_ref = f32[8,128]{1,0:T(8,128)} custom-call(f32[8,128]{1,0:T(8,128)} %get-tuple-element.139.x_ref), custom_call_target="tpu_custom_call" | custom-call | tf_op jit(solution)/shard_map/norm_table/pallas_call | solution.py:1978
  666.8 0.0 copy-start.1
  666.8 0.0 copy-start
  666.8 14.5 %lamb_masters.1 = (f32[4,72]{1,0:T(4,128)}, f32[2,6]{1,0:T(2,128)}, f32[72,4096]{1,0:T(8,128)}, f32[64,2304]{1,0:T(8,128)}, f32[72,9216]{1,0:T(8,128)}, /*index=5*/f32[72,9216]{1,0:T(8,128)}, f32[288,2304]{1,0:T(8,128)}) custom-call(f32[8,128]{1,0:T(8,128)} %norm_table.1.table_ref, f32[4,72]{1,0:T(4,128)} %bitcast.27, f32[4,72]{1,0:T(4,128)} %get-tuple-element.140.g_step, ...), custom_call_target="tpu_custom_call" | custom-call | tf_op jit(solution)/shard_map/lamb_masters/pallas_call | solution.py:1995
  681.3 0.0 copy-done.1
  681.3 0.8 copy.54
  682.1 0.0 copy-done
  682.1 1.0 copy.55
  (1 shorter events, 0.0 us)
Async XLA Ops:
  2.4 119.4 %copy-start.2 = (s32[1024]{0:T(1024)}, s32[1024]{0:T(1024)S(1)}, u32[]{:S(2)}) copy-start(s32[1024]{0:T(1024)S(1)} %fusion) | copy-start | bytes 12292
  666.8 14.5 %copy-start.1 = (bf16[128,2304]{1,0:T(8,128)(2,1)S(1)}, bf16[128,2304]{1,0:T(8,128)(2,1)}, u32[]{:S(2)}) copy-start(bf16[128,2304]{1,0:T(8,128)(2,1)} %get-tuple-element.182) | copy-start | bytes 1769476
  666.8 15.3 %copy-start = (f32[128,2304]{1,0:T(8,128)S(1)}, f32[128,2304]{1,0:T(8,128)}, u32[]{:S(2)}) copy-start(f32[128,2304]{1,0:T(8,128)} %get-tuple-element.183) | copy-start | bytes 3538948

commit v8 on v7

--- a/solution.py
+++ b/solution.py
@@ -1438,11 +1438,15 @@
     down.begin(d_pieces)
     for copy in fetched[1:]:
         copy.wait()
-    work = [functools.partial(make_gate_up, 0)]
-    work += [functools.partial(down.cross, piece) for piece in d_pieces]
-    work += [functools.partial(make_gate_up, owner) for owner in range(1, reps)]
+    work = [lambda: [down.cross(piece) for piece in d_pieces]]
+    work += [functools.partial(make_gate_up, owner) for owner in range(reps)]
     work += [lambda: gate_up.begin(g_pieces)]
-    work += [functools.partial(gate_up.cross, piece) for piece in g_pieces]
+
+    def cross_two(k):
+        for piece in g_pieces[k : k + 2]:
+            gate_up.cross(piece)
+
+    work += [functools.partial(cross_two, k) for k in range(0, count, 2)]
     for step in gather.steps():
         step()
         if work:
@@ -1757,7 +1761,7 @@
     return pl.ds(pl.multiple_of(down * tall, 8), tall), pl.ds(pl.multiple_of(right * wide, 128), wide)
 
 
-LAMB_ORDER = (4, 2, 3, 0, 1)
+LAMB_ORDER = (1, 4, 2, 3, 0)
 
 
 def lamb_kernel(reps, count, sum_in, sum_out, sum_gu, gain_tiles, g_master, g_mean, g_square, *refs):

time: 689 us -> 686 us (level)
  no operation moved by 1% of the time
where the time goes in v8:
time: 686 us; the launch traced here: 681 us
  Pallas kernels  675 us (98%)
    pallas_call x1, Pallas kernels, feed_forward(): pl.pallas_call(functools.partial(ffn_kernel, count), out_shape=[shape((ro...  197 us
    pallas_call x1, Pallas kernels, opening(): pl.pallas_call(functools.partial(opening_kernel, reps, count), out_shape=...  118 us
    pallas_call x1, Pallas kernels, ffn_grads(): pl.pallas_call(functools.partial(ffn_grads_kernel, reps, count), out_shap...  109 us
    pallas_call x1, Pallas kernels, closing(): pl.pallas_call(functools.partial(closing_kernel, reps, count), out_shape=...  101 us
    pallas_call x1, Pallas kernels, attention(): pl.pallas_call(functools.partial(attention_kernel, reps, count), out_shap...  97.4 us
    pallas_call x1, Pallas kernels, lamb_step(): pl.pallas_call(functools.partial(lamb_kernel, reps, count), out_shape=[ti...  25 us
    pallas_call x1, Pallas kernels, lamb_step(): pl.pallas_call(fresh_kernel, out_shape=[like_gains, shape((2, 6), f32)] +...  14.6 us

profile of v8, /device:TPU:0, one launch (start us, length us, event | category | flops | bytes accessed | tf_op | source)
XLA Modules:
  0.0 681.0 jit_solution(10075741121640477253)
XLA Ops:
  0.7 0.9 dynamic-slice_reduce_fusion
  1.6 0.7 bitcast_convert_fusion
  2.3 0.1 fusion
  2.4 0.0 copy-start.2
  2.4 0.6 pad_convert_fusion.gain_ref
  3.0 1.0 copy.51.tagq_ref
  4.0 117.8 %opening.1 = (bf16[8,128,2304]{2,1,0:T(8,128)(2,1)}, f32[8,2304]{1,0:T(8,128)}, bf16[4,8,72,768]{3,2,1,0:T(8,128)(2,1)}, bf16[4,8,72,1152]{3,2,1,0:T(8,128)(2,1)...) custom-call(bf16[128,2304]{1,0:T(8,128)(2,1)} %tokens_ref.3, ...), custom_call_target="tpu_custom_call" | custom-call | tf_op jit(solution)/shard_map/opening/pallas_call | solution.py:1123
  121.8 0.0 copy-done.2
  121.8 97.4 %attention.1 = (f32[128,2304]{1,0:T(8,128)}, bf16[1024,256]{1,0:T(8,128)(2,1)}, bf16[1024,256]{1,0:T(8,128)(2,1)}, bf16[1024,256]{1,0:T(8,128)(2,1)}, bf16[1024,...) custom-call(bf16[1024,2304]{1,0:T(8,128)(2,1)} %bitcast.16, ...), custom_call_target="tpu_custom_call" | custom-call | tf_op jit(solution)/shard_map/attention/pallas_call | solution.py:860
  219.2 197.1 %feed_forward.1 = (bf16[128,2304]{1,0:T(8,128)(2,1)}, f32[128,2304]{1,0:T(8,128)}, bf16[128,2304]{1,0:T(8,128)(2,1)}, f32[8,2304]{1,0:T(8,128)}, bf16[1024,2304]...) custom-call(f32[128,2304]{1,0:T(8,128)} %get-tuple-element.94.attn_ref, ...), custom_call_target="tpu_custom_call" | custom-call | tf_op jit(solution)/shard_map/feed_forward/pallas_call | solution.py:722
  416.3 108.8 %ffn_grads.1 = (bf16[8,128,2304]{2,1,0:T(8,128)(2,1)}, bf16[8,72,2304]{2,1,0:T(8,128)(2,1)}, f32[288,2304]{1,0:T(8,128)}, bf16[1024,768]{1,0:T(8,128)(2,1)}) custom-call(bf16[128,2304]{1,0:T(8,128)(2,1)} %get-tuple-element.100.dattn_ref, bf16[256,2304]{1,0:T(8,128)(2,1)} %get-tuple-element.101.wo_ref, bf16[1024,256]{1,0:T(8,128)(2,1)} %get-tuple-element.102.q_ref, ...), custom_call_target="tpu_custom_call" | custom-call | tf_op jit(solution)/shard_map/ffn_grads/pallas_call | solution.py:1489
  525.1 100.6 %closing.1 = (f32[128,2304]{1,0:T(8,128)}, bf16[8,72,768]{2,1,0:T(8,128)(2,1)}, bf16[4,16,2304]{2,1,0:T(8,128)(2,1)}, f32[32,8,128]{2,1,0:T(8,128)}) custom-call(bf16[1024,768]{1,0:T(8,128)(2,1)} %get-tuple-element.110.dproj, bf16[2304,768]{1,0:T(8,128)(2,1)} %bitcast.19, bf16[1024,256]{1,0:T(8,128)(2,1)} %get-tuple-element.111.att_ref, ...), custom_call_target="tpu_custom_call" | custom-call | tf_op jit(solution)/shard_map/closing/pallas_call | solution.py:1702
  625.7 25.0 %lamb_moments.1 = (f32[8,128]{1,0:T(8,128)}, f32[4,72]{1,0:T(4,128)}, f32[4,72]{1,0:T(4,128)}, f32[4,72]{1,0:T(4,128)}, f32[4,72]{1,0:T(4,128)}, /*index=5*/f32[...) custom-call(bf16[8,72,768]{2,1,0:T(8,128)(2,1)} %get-tuple-element.1, ...), custom_call_target="tpu_custom_call" | custom-call | tf_op jit(solution)/shard_map/lamb_moments/pallas_call | solution.py:1971
  650.7 13.5 %norm_table.1.table_ref = f32[8,128]{1,0:T(8,128)} custom-call(f32[8,128]{1,0:T(8,128)} %get-tuple-element.139.x_ref), custom_call_target="tpu_custom_call" | custom-call | tf_op jit(solution)/shard_map/norm_table/pallas_call | solution.py:1982
  664.1 0.0 copy-start.1
  664.1 0.0 copy-start
  664.2 14.6 %lamb_masters.1 = (f32[4,72]{1,0:T(4,128)}, f32[2,6]{1,0:T(2,128)}, f32[72,4096]{1,0:T(8,128)}, f32[64,2304]{1,0:T(8,128)}, f32[72,9216]{1,0:T(8,128)}, /*index=5*/f32[72,9216]{1,0:T(8,128)}, f32[288,2304]{1,0:T(8,128)}) custom-call(f32[8,128]{1,0:T(8,128)} %norm_table.1.table_ref, f32[4,72]{1,0:T(4,128)} %bitcast.27, f32[4,72]{1,0:T(4,128)} %get-tuple-element.140.g_step, ...), custom_call_target="tpu_custom_call" | custom-call | tf_op jit(solution)/shard_map/lamb_masters/pallas_call | solution.py:1999
  678.7 0.0 copy-done.1
  678.7 0.8 copy.54
  679.6 0.0 copy-done
  679.6 1.0 copy.55
  (1 shorter events, 0.0 us)
Async XLA Ops:
  2.4 119.4 %copy-start.2 = (s32[1024]{0:T(1024)}, s32[1024]{0:T(1024)S(1)}, u32[]{:S(2)}) copy-start(s32[1024]{0:T(1024)S(1)} %fusion) | copy-start | bytes 12292
  664.1 14.6 %copy-start.1 = (bf16[128,2304]{1,0:T(8,128)(2,1)S(1)}, bf16[128,2304]{1,0:T(8,128)(2,1)}, u32[]{:S(2)}) copy-start(bf16[128,2304]{1,0:T(8,128)(2,1)} %get-tuple-element.182) | copy-start | bytes 1769476
  664.1 15.4 %copy-start = (f32[128,2304]{1,0:T(8,128)S(1)}, f32[128,2304]{1,0:T(8,128)}, u32[]{:S(2)}) copy-start(f32[128,2304]{1,0:T(8,128)} %get-tuple-element.183) | copy-start | bytes 3538948

commit v9 on v8

--- a/solution.py
+++ b/solution.py
@@ -1436,9 +1436,8 @@
 
     fetched[0].wait()
     down.begin(d_pieces)
-    for copy in fetched[1:]:
-        copy.wait()
     work = [lambda: [down.cross(piece) for piece in d_pieces]]
+    work += [lambda: [copy.wait() for copy in fetched[1:]]]
     work += [functools.partial(make_gate_up, owner) for owner in range(reps)]
     work += [lambda: gate_up.begin(g_pieces)]
 

time: 686 us -> 686 us (level)
  no operation moved by 1% of the time
where the time goes in v9:
time: 686 us; the launch traced here: 681 us
  Pallas kernels  675 us (98%)
    pallas_call x1, Pallas kernels, feed_forward(): pl.pallas_call(functools.partial(ffn_kernel, count), out_shape=[shape((ro...  197 us
    pallas_call x1, Pallas kernels, opening(): pl.pallas_call(functools.partial(opening_kernel, reps, count), out_shape=...  118 us
    pallas_call x1, Pallas kernels, ffn_grads(): pl.pallas_call(functools.partial(ffn_grads_kernel, reps, count), out_shap...  109 us
    pallas_call x1, Pallas kernels, closing(): pl.pallas_call(functools.partial(closing_kernel, reps, count), out_shape=...  99.6 us
    pallas_call x1, Pallas kernels, attention(): pl.pallas_call(functools.partial(attention_kernel, reps, count), out_shap...  97.4 us
    pallas_call x1, Pallas kernels, lamb_step(): pl.pallas_call(functools.partial(lamb_kernel, reps, count), out_shape=[ti...  25 us
    pallas_call x1, Pallas kernels, lamb_step(): pl.pallas_call(fresh_kernel, out_shape=[like_gains, shape((2, 6), f32)] +...  14.6 us
    pallas_call x1, Pallas kernels, lamb_step(): pl.pallas_call(functools.partial(table_kernel, reps, count, sizes), out_s...  13.9 us

profile of v9, /device:TPU:0, one launch (start us, length us, event | category | flops | bytes accessed | tf_op | source)
XLA Modules:
  0.0 681.1 jit_solution(9268694532722367146)
XLA Ops:
  0.7 0.9 dynamic-slice_reduce_fusion
  1.6 0.7 bitcast_convert_fusion
  2.3 0.1 fusion
  2.4 0.0 copy-start.2
  2.4 0.6 pad_convert_fusion.gain_ref
  3.0 1.0 copy.51.tagq_ref
  4.0 117.8 %opening.1 = (bf16[8,128,2304]{2,1,0:T(8,128)(2,1)}, f32[8,2304]{1,0:T(8,128)}, bf16[4,8,72,768]{3,2,1,0:T(8,128)(2,1)}, bf16[4,8,72,1152]{3,2,1,0:T(8,128)(2,1)...) custom-call(bf16[128,2304]{1,0:T(8,128)(2,1)} %tokens_ref.3, ...), custom_call_target="tpu_custom_call" | custom-call | tf_op jit(solution)/shard_map/opening/pallas_call | solution.py:1123
  121.8 0.0 copy-done.2
  121.8 97.4 %attention.1 = (f32[128,2304]{1,0:T(8,128)}, bf16[1024,256]{1,0:T(8,128)(2,1)}, bf16[1024,256]{1,0:T(8,128)(2,1)}, bf16[1024,256]{1,0:T(8,128)(2,1)}, bf16[1024,...) custom-call(bf16[1024,2304]{1,0:T(8,128)(2,1)} %bitcast.16, ...), custom_call_target="tpu_custom_call" | custom-call | tf_op jit(solution)/shard_map/attention/pallas_call | solution.py:860
  219.2 197.1 %feed_forward.1 = (bf16[128,2304]{1,0:T(8,128)(2,1)}, f32[128,2304]{1,0:T(8,128)}, bf16[128,2304]{1,0:T(8,128)(2,1)}, f32[8,2304]{1,0:T(8,128)}, bf16[1024,2304]...) custom-call(f32[128,2304]{1,0:T(8,128)} %get-tuple-element.94.attn_ref, ...), custom_call_target="tpu_custom_call" | custom-call | tf_op jit(solution)/shard_map/feed_forward/pallas_call | solution.py:722
  416.3 109.4 %ffn_grads.1 = (bf16[8,128,2304]{2,1,0:T(8,128)(2,1)}, bf16[8,72,2304]{2,1,0:T(8,128)(2,1)}, f32[288,2304]{1,0:T(8,128)}, bf16[1024,768]{1,0:T(8,128)(2,1)}) custom-call(bf16[128,2304]{1,0:T(8,128)(2,1)} %get-tuple-element.100.dattn_ref, bf16[256,2304]{1,0:T(8,128)(2,1)} %get-tuple-element.101.wo_ref, bf16[1024,256]{1,0:T(8,128)(2,1)} %get-tuple-element.102.q_ref, ...), custom_call_target="tpu_custom_call" | custom-call | tf_op jit(solution)/shard_map/ffn_grads/pallas_call | solution.py:1488
  525.8 99.6 %closing.1 = (f32[128,2304]{1,0:T(8,128)}, bf16[8,72,768]{2,1,0:T(8,128)(2,1)}, bf16[4,16,2304]{2,1,0:T(8,128)(2,1)}, f32[32,8,128]{2,1,0:T(8,128)}) custom-call(bf16[1024,768]{1,0:T(8,128)(2,1)} %get-tuple-element.110.dproj, bf16[2304,768]{1,0:T(8,128)(2,1)} %bitcast.19, bf16[1024,256]{1,0:T(8,128)(2,1)} %get-tuple-element.111.att_ref, ...), custom_call_target="tpu_custom_call" | custom-call | tf_op jit(solution)/shard_map/closing/pallas_call | solution.py:1701
  625.3 25.0 %lamb_moments.1 = (f32[8,128]{1,0:T(8,128)}, f32[4,72]{1,0:T(4,128)}, f32[4,72]{1,0:T(4,128)}, f32[4,72]{1,0:T(4,128)}, f32[4,72]{1,0:T(4,128)}, /*index=5*/f32[...) custom-call(bf16[8,72,768]{2,1,0:T(8,128)(2,1)} %get-tuple-element.1, ...), custom_call_target="tpu_custom_call" | custom-call | tf_op jit(solution)/shard_map/lamb_moments/pallas_call | solution.py:1970
  650.3 13.9 %norm_table.1.table_ref = f32[8,128]{1,0:T(8,128)} custom-call(f32[8,128]{1,0:T(8,128)} %get-tuple-element.139.x_ref), custom_call_target="tpu_custom_call" | custom-call | tf_op jit(solution)/shard_map/norm_table/pallas_call | solution.py:1981
  664.2 0.0 copy-start.1
  664.2 0.0 copy-start
  664.2 14.6 %lamb_masters.1 = (f32[4,72]{1,0:T(4,128)}, f32[2,6]{1,0:T(2,128)}, f32[72,4096]{1,0:T(8,128)}, f32[64,2304]{1,0:T(8,128)}, f32[72,9216]{1,0:T(8,128)}, /*index=5*/f32[72,9216]{1,0:T(8,128)}, f32[288,2304]{1,0:T(8,128)}) custom-call(f32[8,128]{1,0:T(8,128)} %norm_table.1.table_ref, f32[4,72]{1,0:T(4,128)} %bitcast.27, f32[4,72]{1,0:T(4,128)} %get-tuple-element.140.g_step, ...), custom_call_target="tpu_custom_call" | custom-call | tf_op jit(solution)/shard_map/lamb_masters/pallas_call | solution.py:1998
  678.8 0.0 copy-done.1
  678.8 0.8 copy.54
  679.6 0.0 copy-done
  679.6 1.0 copy.55
  (1 shorter events, 0.0 us)
Async XLA Ops:
  2.4 119.4 %copy-start.2 = (s32[1024]{0:T(1024)}, s32[1024]{0:T(1024)S(1)}, u32[]{:S(2)}) copy-start(s32[1024]{0:T(1024)S(1)} %fusion) | copy-start | bytes 12292
  664.2 14.6 %copy-start.1 = (bf16[128,2304]{1,0:T(8,128)(2,1)S(1)}, bf16[128,2304]{1,0:T(8,128)(2,1)}, u32[]{:S(2)}) copy-start(bf16[128,2304]{1,0:T(8,128)(2,1)} %get-tuple-element.182) | copy-start | bytes 1769476
  664.2 15.4 %copy-start = (f32[128,2304]{1,0:T(8,128)S(1)}, f32[128,2304]{1,0:T(8,128)}, u32[]{:S(2)}) copy-start(f32[128,2304]{1,0:T(8,128)} %get-tuple-element.183) | copy-start | bytes 3538948
